TPU v7x, 256 devices: a whole 4x4x8 slice. The times are simulated.
256 devices in a mesh: gx: 16 (over y_hi, x, core), gy: 16 (over z, y_lo).
Axes of the slice: x: 4, y: 4 (y_hi: 2, y_lo: 2; y = y_hi * 2 + y_lo), z: 8, core: 2. Of those that a mesh axis runs over, the one named last changes fastest.
Arguments:
- block_ids: int32 [2, 1024, 4096], P(None, 'gx', 'gy'), may hold values from 0 to 31
- block_power: float32 [32], replicated, may hold values from 0.2 to 5
- layer_class: int32 [2, 4], replicated, may hold values from 0 to 3
- power_share: float32 [4], replicated, may hold values from 0.1 to 1
- lateral_k: float32 [4], replicated, may hold values from 0.3 to 3
- vertical_k: float32 [4], replicated, may hold values from 0.3 to 3
- sink_conductance: float32 [2], replicated, may hold values from 0.5 to 3
- bond_conductance: float32 [1024, 4096], P('gx', 'gy'), may hold values from 0.5 to 4
- peak_heat_factors_flipped: float32 [2, 4, 1024, 4096], P(None, None, 'gx', 'gy'), may hold values from 0.1 to 2
- sensor_weight: float32 [2, 4, 1024, 4096], P(None, None, 'gx', 'gy'), may hold values from -6 to 6
Outputs:
- thermal_excess: float32 [2, 4, 1024, 4096], P(None, None, 'gx', 'gy')
- peak_heat_sensitivity: float32 [2, 4, 1024, 4096], P(None, None, 'gx', 'gy')
- sensor_heat_sensitivity: float32 [2, 4, 1024, 4096], P(None, None, 'gx', 'gy')
All inputs are finite; a program needn't handle non-finite values.
Results may differ from a plain program's by a relative error of at most 0.00002.
Values sent between devices are 32-bit elements; how exact they have to be, the bound alone decides.
No kernel may reach another device: no remote copies, remote signals or barrier semaphores. Data moves between devices by JAX's collectives and lax.ppermute only.
A program may use at most 64 MiB of HBM per device.

v0:
```python
import jax
import jax.numpy as jnp
from jax import lax
from jax.sharding import PartitionSpec as P

SWEEPS = 4


def with_halo(block, sides, width):
    for axis, dim in sides:
        count = lax.axis_size(axis)
        forward = [(i, i + 1) for i in range(count - 1)]
        backward = [(target, source) for source, target in forward]
        low = lax.ppermute(
            lax.slice_in_dim(block, block.shape[dim] - width, None, axis=dim), axis, forward
        )
        high = lax.ppermute(lax.slice_in_dim(block, 0, width, axis=dim), axis, backward)
        block = jnp.concatenate([low, block, high], axis=dim)
    return block


def partner(shard, axis, bit):
    return lax.ppermute(shard, axis, [(i, i ^ 1 << bit) for i in range(lax.axis_size(axis))])


def pick_class(lookup, classes):
    hits = classes[:, :, None] == jnp.arange(lookup.shape[0], dtype=jnp.int32)[None, None, :]
    return jnp.sum(jnp.where(hits, lookup[None, None, :], 0.0), axis=2)


def die_power(cell_blocks, lookup):

    def one_die(blocks):
        hits = blocks[None] == jnp.arange(lookup.shape[0], dtype=jnp.int32)[:, None, None]
        return jnp.sum(jnp.where(hits, lookup[:, None, None], 0.0), axis=0)

    return lax.map(one_die, cell_blocks)


def reverse_die_rows(array):
    return jnp.flip(array, axis=-2)


def neighbours(values, conductance_tuple, joined_counterpart):
    lateral_g, upper_g, lower_g, face_mask = conductance_tuple
    padded = with_halo(values, (("gx", 3), ("gy", 4)), 1)
    lateral = (
        padded[:, :, :, 2:, 1:-1]
        + padded[:, :, :, :-2, 1:-1]
        + padded[:, :, :, 1:-1, 2:]
        + padded[:, :, :, 1:-1, :-2]
    )
    zero_layer = jnp.zeros_like(values[:, :, :1])
    upper = jnp.concatenate([values[:, :, 1:], zero_layer], axis=2)
    lower = jnp.concatenate([zero_layer, values[:, :, :-1]], axis=2)
    faces = values[:, :, -1]
    other_die = faces[:, ::-1][:, :, None]
    return (
        lateral_g * lateral
        + upper_g * upper
        + lower_g * lower
        + face_mask * joined_counterpart * other_die
    )


def pointwise_iterative_update(source, conductance_tuple, joined_counterpart, matrix_main_line):
    values = jnp.zeros_like(source)
    for sweep_index in range(SWEEPS):
        values = (
            source + neighbours(values, conductance_tuple, joined_counterpart)
        ) / matrix_main_line
    return values


def local(
    block_ids,
    block_power,
    layer_class,
    power_share,
    lateral_k,
    vertical_k,
    sink_conductance,
    bond_conductance,
    peak_heat_factors_flipped,
    sensor_weight,
):
    layers = peak_heat_factors_flipped.shape[1]
    level = jnp.arange(layers)
    share = pick_class(power_share, layer_class)
    lateral_g = pick_class(lateral_k, layer_class)
    vertical_g = pick_class(vertical_k, layer_class)
    upper_g = jnp.where(level[None, :] < layers - 1, vertical_g, 0.0)
    lower_g = jnp.concatenate([jnp.zeros_like(upper_g[:, :1]), upper_g[:, :-1]], axis=1)
    heating_rate_field = die_power(block_ids, block_power)[:, None] * share[:, :, None, None]
    moved = jnp.stack([heating_rate_field[1], peak_heat_factors_flipped[1], sensor_weight[1]])
    for bit_index in range(lax.axis_size("gx").bit_length() - 1):
        moved = partner(moved, "gx", bit_index)
    moved = reverse_die_rows(moved)
    heating_rate_field = jnp.stack([heating_rate_field[0], moved[0]])
    peak_heat_derivative = jnp.stack([peak_heat_factors_flipped[0], moved[1]])
    sensor_local = jnp.stack([sensor_weight[0], moved[2]])
    joined_counterpart = jnp.stack([bond_conductance, bond_conductance])
    joined_counterpart = joined_counterpart[None, :, None]
    face_mask = (level == layers - 1).astype(jnp.float32)[None, None, :, None, None]
    sink_mask = (level == 0).astype(jnp.float32)[None, None, :, None, None]
    lateral_g = lateral_g[None, :, :, None, None]
    upper_g = upper_g[None, :, :, None, None]
    lower_g = lower_g[None, :, :, None, None]
    matrix_main_line = (
        4.0 * lateral_g
        + upper_g
        + lower_g
        + face_mask * joined_counterpart
        + sink_mask * sink_conductance[None, :, None, None, None]
    )
    conductance_tuple = (lateral_g, upper_g, lower_g, face_mask)
    thermal_excess = pointwise_iterative_update(
        heating_rate_field[None], conductance_tuple, joined_counterpart, matrix_main_line
    )[0]
    peak_heat_sensitivity = pointwise_iterative_update(
        (peak_heat_derivative * thermal_excess)[None],
        conductance_tuple,
        joined_counterpart,
        matrix_main_line,
    )[0]
    sensor_heat_sensitivity = pointwise_iterative_update(
        sensor_local[None], conductance_tuple, joined_counterpart, matrix_main_line
    )[0]
    iteration_result = reverse_die_rows(
        jnp.stack([thermal_excess[1], peak_heat_sensitivity[1], sensor_heat_sensitivity[1]])
    )
    for bit_index in range(lax.axis_size("gx").bit_length() - 1):
        iteration_result = partner(iteration_result, "gx", bit_index)
    thermal_excess = jnp.stack([thermal_excess[0], iteration_result[0]])
    peak_heat_sensitivity = jnp.stack([peak_heat_sensitivity[0], iteration_result[1]])
    sensor_heat_sensitivity = jnp.stack([sensor_heat_sensitivity[0], iteration_result[2]])
    return (thermal_excess, peak_heat_sensitivity, sensor_heat_sensitivity)


def solution(mesh):
    return jax.shard_map(
        local,
        mesh=mesh,
        in_specs=(
            P(None, "gx", "gy"),
            P(),
            P(),
            P(),
            P(),
            P(),
            P(),
            P("gx", "gy"),
            P(None, None, "gx", "gy"),
            P(None, None, "gx", "gy"),
        ),
        out_specs=(P(None, None, "gx", "gy"), P(None, None, "gx", "gy"), P(None, None, "gx", "gy")),
        check_vma=False,
    )
```

profile of v0, /device:TPU:111, one launch (start us, length us, event | category | flops | bytes accessed | tf_op | source)
XLA Modules:
  0.0 370.1 jit_solution(14943378059295373451)
XLA Ops:
  0.7 3.6 while.10
  9.8 18.2 %collective-permute-done.1 = f32[3,4,64,256]{3,2,1,0:T(8,128)S(1)} collective-permute-done((f32[3,4,64,256]{3,2,1,0:T(8,128)S(1)}, f32[3,4,64,256]{3,2,1,0:T(8,128)S(1)}, u32[]{:S(2)}, u32[]{:S(2)}) %collective-permute-start.1) | collective-permute-done | bytes 786464 | tf_op jit(solution)/shard_map/ppermute | solution.py:23
  29.2 3.4 collective-permute-start.4
  32.5 5.8 %collective-permute-start.5 = (f32[1,2,4,1,256]{4,3,2,1,0:T(1,128)S(1)}, f32[1,2,4,1,256]{4,3,2,1,0:T(1,128)S(1)}, u32[]{:S(2)}, u32[]{:S(2)}) collective-permute-start(f32[1,2,4,1,256]{4,3,2,1,0:T(1,128)S(1)} %broadcast.361), channel_id=1, source_target_pairs={{0,16},{16,32},{32,48},{48,64},{64,80},{80,96},{96,112},{112,128},... | collective-permute-start | bytes 24584 | tf_op jit(solution)/shard_map/ppermute | solution.py:14
  38.4 8.9 %collective-permute-done.2 = f32[3,4,64,256]{3,2,1,0:T(8,128)S(1)} collective-permute-done((f32[3,4,64,256]{3,2,1,0:T(8,128)S(1)}, f32[3,4,64,256]{3,2,1,0:T(8,128)S(1)}, u32[]{:S(2)}, u32[]{:S(2)}) %collective-permute-start.2) | collective-permute-done | bytes 786464 | tf_op jit(solution)/shard_map/ppermute | solution.py:23
  47.4 2.0 collective-permute-start.3
  51.2 5.5 %collective-permute-start.7 = (f32[1,2,4,66,1]{4,3,2,1,0:T(8,128)}, f32[1,2,4,66,1]{4,3,2,1,0:T(8,128)S(1)}, u32[]{:S(2)}, u32[]{:S(2)}) collective-permute-start(f32[1,2,4,66,1]{4,3,2,1,0:T(8,128)} %get-tuple-element.67), channel_id=1, source_target_pairs={{0,1},{1,2},{2,3},{3,4},{4,5},{5,6},{6,7},{7,8},{8,9},{9,10},{10,1... | collective-permute-start | bytes 6344 | tf_op jit(solution)/shard_map/ppermute | solution.py:14
  58.6 13.5 %collective-permute-done.3 = f32[3,4,64,256]{3,2,1,0:T(8,128)S(1)} collective-permute-done((f32[3,4,64,256]{3,2,1,0:T(8,128)S(1)}, f32[3,4,64,256]{3,2,1,0:T(8,128)S(1)}, u32[]{:S(2)}, u32[]{:S(2)}) %collective-permute-start.3) | collective-permute-done | bytes 786464 | tf_op jit(solution)/shard_map/ppermute | solution.py:23
  73.1 5.4 %collective-permute-done.7 = f32[1,2,4,66,1]{4,3,2,1,0:T(8,128)S(1)} collective-permute-done((f32[1,2,4,66,1]{4,3,2,1,0:T(8,128)}, f32[1,2,4,66,1]{4,3,2,1,0:T(8,128)S(1)}, u32[]{:S(2)}, u32[]{:S(2)}) %collective-permute-start.7) | collective-permute-done | bytes 2144 | tf_op jit(solution)/shard_map/ppermute | solution.py:14
  82.3 5.0 %collective-permute-start.32 = (f32[1,2,4,1,256]{4,3,2,1,0:T(1,128)}, f32[1,2,4,1,256]{4,3,2,1,0:T(1,128)}, u32[]{:S(2)}, u32[]{:S(2)}) collective-permute-start(f32[1,2,4,1,256]{4,3,2,1,0:T(1,128)} %get-tuple-element.111), channel_id=1, source_target_pairs={{16,0},{32,16},{48,32},{64,48},{80,64},{96,80},{112,96},{128,112},... | collective-permute-start | bytes 24584 | tf_op jit(solution)/shard_map/ppermute | solution.py:17
  87.3 4.2 %collective-permute-start.33 = (f32[1,2,4,1,256]{4,3,2,1,0:T(1,128)}, f32[1,2,4,1,256]{4,3,2,1,0:T(1,128)}, u32[]{:S(2)}, u32[]{:S(2)}) collective-permute-start(f32[1,2,4,1,256]{4,3,2,1,0:T(1,128)} %get-tuple-element.110), channel_id=1, source_target_pairs={{0,16},{16,32},{32,48},{48,64},{64,80},{80,96},{96,112},{112,128},... | collective-permute-start | bytes 24584 | tf_op jit(solution)/shard_map/ppermute | solution.py:14
  96.4 7.3 %collective-permute-start.9 = (f32[1,2,4,1,256]{4,3,2,1,0:T(1,128)}, f32[1,2,4,1,256]{4,3,2,1,0:T(1,128)S(1)}, u32[]{:S(2)}, u32[]{:S(2)}) collective-permute-start(f32[1,2,4,1,256]{4,3,2,1,0:T(1,128)} %get-tuple-element.96), channel_id=1, source_target_pairs={{0,16},{16,32},{32,48},{48,64},{64,80},{80,96},{96,112},{112,128},... | collective-permute-start | bytes 24584 | tf_op jit(solution)/shard_map/ppermute | solution.py:14
  104.6 4.9 %collective-permute-start.35 = (f32[1,2,4,66,1]{4,3,2,1,0:T(8,128)S(1)}, f32[1,2,4,66,1]{4,3,2,1,0:T(8,128)S(1)}, u32[]{:S(2)}, u32[]{:S(2)}) collective-permute-start(f32[1,2,4,66,1]{4,3,2,1,0:T(8,128)S(1)} %get-tuple-element.65), channel_id=1, source_target_pairs={{0,1},{1,2},{2,3},{3,4},{4,5},{5,6},{6,7},{7,8},{8,9},{9,10},{10,1... | collective-permute-start | bytes 6344 | tf_op jit(solution)/shard_map/ppermute | solution.py:14
  111.7 5.6 %collective-permute-start.11 = (f32[1,2,4,66,1]{4,3,2,1,0:T(8,128)S(1)}, f32[1,2,4,66,1]{4,3,2,1,0:T(8,128)S(1)}, u32[]{:S(2)}, u32[]{:S(2)}) collective-permute-start(f32[1,2,4,66,1]{4,3,2,1,0:T(8,128)S(1)} %get-tuple-element.59), channel_id=1, source_target_pairs={{0,1},{1,2},{2,3},{3,4},{4,5},{5,6},{6,7},{7,8},{8,9},{9,10},{10,1... | collective-permute-start | bytes 6344 | tf_op jit(solution)/shard_map/ppermute | solution.py:14
  119.2 5.0 %collective-permute-done.34 = f32[1,2,4,66,1]{4,3,2,1,0:T(8,128)S(1)} collective-permute-done((f32[1,2,4,66,1]{4,3,2,1,0:T(8,128)S(1)}, f32[1,2,4,66,1]{4,3,2,1,0:T(8,128)S(1)}, u32[]{:S(2)}, u32[]{:S(2)}) %collective-permute-start.34) | collective-permute-done | bytes 2144 | tf_op jit(solution)/shard_map/ppermute | solution.py:17
  125.9 5.1 %collective-permute-done.11 = f32[1,2,4,66,1]{4,3,2,1,0:T(8,128)S(1)} collective-permute-done((f32[1,2,4,66,1]{4,3,2,1,0:T(8,128)S(1)}, f32[1,2,4,66,1]{4,3,2,1,0:T(8,128)S(1)}, u32[]{:S(2)}, u32[]{:S(2)}) %collective-permute-start.11) | collective-permute-done | bytes 2144 | tf_op jit(solution)/shard_map/ppermute | solution.py:14
  133.8 7.3 %collective-permute-start.37 = (f32[1,2,4,1,256]{4,3,2,1,0:T(1,128)S(1)}, f32[1,2,4,1,256]{4,3,2,1,0:T(1,128)S(1)}, u32[]{:S(2)}, u32[]{:S(2)}) collective-permute-start(f32[1,2,4,1,256]{4,3,2,1,0:T(1,128)S(1)} %get-tuple-element.106), channel_id=1, source_target_pairs={{0,16},{16,32},{32,48},{48,64},{64,80},{80,96},{96,112},{112,128},... | collective-permute-start | bytes 24584 | tf_op jit(solution)/shard_map/ppermute | solution.py:14
  141.0 1.9 collective-permute-start.12
  143.0 7.3 %collective-permute-start.13 = (f32[1,2,4,1,256]{4,3,2,1,0:T(1,128)S(1)}, f32[1,2,4,1,256]{4,3,2,1,0:T(1,128)S(1)}, u32[]{:S(2)}, u32[]{:S(2)}) collective-permute-start(f32[1,2,4,1,256]{4,3,2,1,0:T(1,128)S(1)} %get-tuple-element.92), channel_id=1, source_target_pairs={{0,16},{16,32},{32,48},{48,64},{64,80},{80,96},{96,112},{112,128},... | collective-permute-start | bytes 24584 | tf_op jit(solution)/shard_map/ppermute | solution.py:14
  150.5 5.8 %collective-permute-start.39 = (f32[1,2,4,66,1]{4,3,2,1,0:T(8,128)S(1)}, f32[1,2,4,66,1]{4,3,2,1,0:T(8,128)S(1)}, u32[]{:S(2)}, u32[]{:S(2)}) collective-permute-start(f32[1,2,4,66,1]{4,3,2,1,0:T(8,128)S(1)} %get-tuple-element.63), channel_id=1, source_target_pairs={{0,1},{1,2},{2,3},{3,4},{4,5},{5,6},{6,7},{7,8},{8,9},{9,10},{10,1... | collective-permute-start | bytes 6344 | tf_op jit(solution)/shard_map/ppermute | solution.py:14
  158.4 5.5 %collective-permute-start.15 = (f32[1,2,4,66,1]{4,3,2,1,0:T(8,128)S(1)}, f32[1,2,4,66,1]{4,3,2,1,0:T(8,128)S(1)}, u32[]{:S(2)}, u32[]{:S(2)}) collective-permute-start(f32[1,2,4,66,1]{4,3,2,1,0:T(8,128)S(1)} %get-tuple-element.57), channel_id=1, source_target_pairs={{0,1},{1,2},{2,3},{3,4},{4,5},{5,6},{6,7},{7,8},{8,9},{9,10},{10,1... | collective-permute-start | bytes 6344 | tf_op jit(solution)/shard_map/ppermute | solution.py:14
  165.8 4.4 %collective-permute-done.38 = f32[1,2,4,66,1]{4,3,2,1,0:T(8,128)S(1)} collective-permute-done((f32[1,2,4,66,1]{4,3,2,1,0:T(8,128)S(1)}, f32[1,2,4,66,1]{4,3,2,1,0:T(8,128)S(1)}, u32[]{:S(2)}, u32[]{:S(2)}) %collective-permute-start.38) | collective-permute-done | bytes 2144 | tf_op jit(solution)/shard_map/ppermute | solution.py:17
  171.0 6.5 %collective-permute-done.15 = f32[1,2,4,66,1]{4,3,2,1,0:T(8,128)S(1)} collective-permute-done((f32[1,2,4,66,1]{4,3,2,1,0:T(8,128)S(1)}, f32[1,2,4,66,1]{4,3,2,1,0:T(8,128)S(1)}, u32[]{:S(2)}, u32[]{:S(2)}) %collective-permute-start.15) | collective-permute-done | bytes 2144 | tf_op jit(solution)/shard_map/ppermute | solution.py:14
  180.3 7.3 %collective-permute-start.41 = (f32[1,2,4,1,256]{4,3,2,1,0:T(1,128)S(1)}, f32[1,2,4,1,256]{4,3,2,1,0:T(1,128)S(1)}, u32[]{:S(2)}, u32[]{:S(2)}) collective-permute-start(f32[1,2,4,1,256]{4,3,2,1,0:T(1,128)S(1)} %get-tuple-element.102), channel_id=1, source_target_pairs={{0,16},{16,32},{32,48},{48,64},{64,80},{80,96},{96,112},{112,128},... | collective-permute-start | bytes 24584 | tf_op jit(solution)/shard_map/ppermute | solution.py:14
  187.6 1.9 collective-permute-start.16
  189.5 7.3 %collective-permute-start.17 = (f32[1,2,4,1,256]{4,3,2,1,0:T(1,128)S(1)}, f32[1,2,4,1,256]{4,3,2,1,0:T(1,128)S(1)}, u32[]{:S(2)}, u32[]{:S(2)}) collective-permute-start(f32[1,2,4,1,256]{4,3,2,1,0:T(1,128)S(1)} %get-tuple-element.86), channel_id=1, source_target_pairs={{0,16},{16,32},{32,48},{48,64},{64,80},{80,96},{96,112},{112,128},... | collective-permute-start | bytes 24584 | tf_op jit(solution)/shard_map/ppermute | solution.py:14
  197.8 5.9 %collective-permute-start.19 = (f32[1,2,4,66,1]{4,3,2,1,0:T(8,128)S(1)}, f32[1,2,4,66,1]{4,3,2,1,0:T(8,128)S(1)}, u32[]{:S(2)}, u32[]{:S(2)}) collective-permute-start(f32[1,2,4,66,1]{4,3,2,1,0:T(8,128)S(1)} %get-tuple-element.55), channel_id=1, source_target_pairs={{0,1},{1,2},{2,3},{3,4},{4,5},{5,6},{6,7},{7,8},{8,9},{9,10},{10,1... | collective-permute-start | bytes 6344 | tf_op jit(solution)/shard_map/ppermute | solution.py:14
  203.6 1.9 collective-permute-start.18
  205.8 5.5 %collective-permute-start.43 = (f32[1,2,4,66,1]{4,3,2,1,0:T(8,128)S(1)}, f32[1,2,4,66,1]{4,3,2,1,0:T(8,128)S(1)}, u32[]{:S(2)}, u32[]{:S(2)}) collective-permute-start(f32[1,2,4,66,1]{4,3,2,1,0:T(8,128)S(1)} %get-tuple-element.61), channel_id=1, source_target_pairs={{0,1},{1,2},{2,3},{3,4},{4,5},{5,6},{6,7},{7,8},{8,9},{9,10},{10,1... | collective-permute-start | bytes 6344 | tf_op jit(solution)/shard_map/ppermute | solution.py:14
  211.3 2.1 collective-permute-start.42
  213.4 4.6 %collective-permute-done.18 = f32[1,2,4,66,1]{4,3,2,1,0:T(8,128)S(1)} collective-permute-done((f32[1,2,4,66,1]{4,3,2,1,0:T(8,128)S(1)}, f32[1,2,4,66,1]{4,3,2,1,0:T(8,128)S(1)}, u32[]{:S(2)}, u32[]{:S(2)}) %collective-permute-start.18) | collective-permute-done | bytes 2144 | tf_op jit(solution)/shard_map/ppermute | solution.py:17
  218.8 6.2 %collective-permute-done.43 = f32[1,2,4,66,1]{4,3,2,1,0:T(8,128)S(1)} collective-permute-done((f32[1,2,4,66,1]{4,3,2,1,0:T(8,128)S(1)}, f32[1,2,4,66,1]{4,3,2,1,0:T(8,128)S(1)}, u32[]{:S(2)}, u32[]{:S(2)}) %collective-permute-start.43) | collective-permute-done | bytes 2144 | tf_op jit(solution)/shard_map/ppermute | solution.py:14
  227.6 8.3 %collective-permute-start.21 = (f32[1,2,4,1,256]{4,3,2,1,0:T(1,128)S(1)}, f32[1,2,4,1,256]{4,3,2,1,0:T(1,128)S(1)}, u32[]{:S(2)}, u32[]{:S(2)}) collective-permute-start(f32[1,2,4,1,256]{4,3,2,1,0:T(1,128)S(1)} %get-tuple-element.84), channel_id=1, source_target_pairs={{0,16},{16,32},{32,48},{48,64},{64,80},{80,96},{96,112},{112,128},... | collective-permute-start | bytes 24584 | tf_op jit(solution)/shard_map/ppermute | solution.py:14
  236.9 4.8 %collective-permute-start.23 = (f32[1,2,4,66,1]{4,3,2,1,0:T(8,128)S(1)}, f32[1,2,4,66,1]{4,3,2,1,0:T(8,128)S(1)}, u32[]{:S(2)}, u32[]{:S(2)}) collective-permute-start(f32[1,2,4,66,1]{4,3,2,1,0:T(8,128)S(1)} %get-tuple-element.53), channel_id=1, source_target_pairs={{0,1},{1,2},{2,3},{3,4},{4,5},{5,6},{6,7},{7,8},{8,9},{9,10},{10,1... | collective-permute-start | bytes 6344 | tf_op jit(solution)/shard_map/ppermute | solution.py:14
  245.4 6.2 %collective-permute-done.22 = f32[1,2,4,66,1]{4,3,2,1,0:T(8,128)S(1)} collective-permute-done((f32[1,2,4,66,1]{4,3,2,1,0:T(8,128)S(1)}, f32[1,2,4,66,1]{4,3,2,1,0:T(8,128)S(1)}, u32[]{:S(2)}, u32[]{:S(2)}) %collective-permute-start.22) | collective-permute-done | bytes 2144 | tf_op jit(solution)/shard_map/ppermute | solution.py:17
  254.3 8.5 %collective-permute-start.25 = (f32[1,2,4,1,256]{4,3,2,1,0:T(1,128)S(1)}, f32[1,2,4,1,256]{4,3,2,1,0:T(1,128)S(1)}, u32[]{:S(2)}, u32[]{:S(2)}) collective-permute-start(f32[1,2,4,1,256]{4,3,2,1,0:T(1,128)S(1)} %get-tuple-element.80), channel_id=1, source_target_pairs={{0,16},{16,32},{32,48},{48,64},{64,80},{80,96},{96,112},{112,128},... | collective-permute-start | bytes 24584 | tf_op jit(solution)/shard_map/ppermute | solution.py:14
  263.8 4.6 %collective-permute-start.27 = (f32[1,2,4,66,1]{4,3,2,1,0:T(8,128)S(1)}, f32[1,2,4,66,1]{4,3,2,1,0:T(8,128)S(1)}, u32[]{:S(2)}, u32[]{:S(2)}) collective-permute-start(f32[1,2,4,66,1]{4,3,2,1,0:T(8,128)S(1)} %get-tuple-element.51), channel_id=1, source_target_pairs={{0,1},{1,2},{2,3},{3,4},{4,5},{5,6},{6,7},{7,8},{8,9},{9,10},{10,1... | collective-permute-start | bytes 6344 | tf_op jit(solution)/shard_map/ppermute | solution.py:14
  270.3 2.7 collective-permute-done.27
  273.0 6.2 %collective-permute-done.26 = f32[1,2,4,66,1]{4,3,2,1,0:T(8,128)S(1)} collective-permute-done((f32[1,2,4,66,1]{4,3,2,1,0:T(8,128)S(1)}, f32[1,2,4,66,1]{4,3,2,1,0:T(8,128)S(1)}, u32[]{:S(2)}, u32[]{:S(2)}) %collective-permute-start.26) | collective-permute-done | bytes 2144 | tf_op jit(solution)/shard_map/ppermute | solution.py:17
  281.9 7.5 %collective-permute-start.29 = (f32[1,2,4,1,256]{4,3,2,1,0:T(1,128)S(1)}, f32[1,2,4,1,256]{4,3,2,1,0:T(1,128)S(1)}, u32[]{:S(2)}, u32[]{:S(2)}) collective-permute-start(f32[1,2,4,1,256]{4,3,2,1,0:T(1,128)S(1)} %get-tuple-element.76), channel_id=1, source_target_pairs={{0,16},{16,32},{32,48},{48,64},{64,80},{80,96},{96,112},{112,128},... | collective-permute-start | bytes 24584 | tf_op jit(solution)/shard_map/ppermute | solution.py:14
  290.4 5.6 %collective-permute-start.31 = (f32[1,2,4,66,1]{4,3,2,1,0:T(8,128)S(1)}, f32[1,2,4,66,1]{4,3,2,1,0:T(8,128)S(1)}, u32[]{:S(2)}, u32[]{:S(2)}) collective-permute-start(f32[1,2,4,66,1]{4,3,2,1,0:T(8,128)S(1)} %get-tuple-element.49), channel_id=1, source_target_pairs={{0,1},{1,2},{2,3},{3,4},{4,5},{5,6},{6,7},{7,8},{8,9},{9,10},{10,1... | collective-permute-start | bytes 6344 | tf_op jit(solution)/shard_map/ppermute | solution.py:14
  298.0 2.7 collective-permute-done.31
  300.7 6.2 %collective-permute-done.30 = f32[1,2,4,66,1]{4,3,2,1,0:T(8,128)S(1)} collective-permute-done((f32[1,2,4,66,1]{4,3,2,1,0:T(8,128)S(1)}, f32[1,2,4,66,1]{4,3,2,1,0:T(8,128)S(1)}, u32[]{:S(2)}, u32[]{:S(2)}) %collective-permute-start.30) | collective-permute-done | bytes 2144 | tf_op jit(solution)/shard_map/ppermute | solution.py:17
  308.0 2.3 collective-permute-done.44
  310.3 19.0 %collective-permute-done.45 = f32[3,4,64,256]{3,2,1,0:T(8,128)S(1)} collective-permute-done((f32[3,4,64,256]{3,2,1,0:T(8,128)S(1)}, f32[3,4,64,256]{3,2,1,0:T(8,128)S(1)}, u32[]{:S(2)}, u32[]{:S(2)}) %collective-permute-start.45) | collective-permute-done | bytes 786464 | tf_op jit(solution)/shard_map/ppermute | solution.py:23
  329.3 19.6 %collective-permute-done.46 = f32[3,4,64,256]{3,2,1,0:T(8,128)S(1)} collective-permute-done((f32[3,4,64,256]{3,2,1,0:T(8,128)S(1)}, f32[3,4,64,256]{3,2,1,0:T(8,128)S(1)}, u32[]{:S(2)}, u32[]{:S(2)}) %collective-permute-start.46) | collective-permute-done | bytes 786464 | tf_op jit(solution)/shard_map/ppermute | solution.py:23
  348.8 2.7 collective-permute-start.47
  351.6 15.9 %collective-permute-done.47 = f32[3,4,64,256]{3,2,1,0:T(8,128)S(1)} collective-permute-done((f32[3,4,64,256]{3,2,1,0:T(8,128)S(1)}, f32[3,4,64,256]{3,2,1,0:T(8,128)S(1)}, u32[]{:S(2)}, u32[]{:S(2)}) %collective-permute-start.47) | collective-permute-done | bytes 786464 | tf_op jit(solution)/shard_map/ppermute | solution.py:23
  (185 shorter events, 64.6 us)
Async XLA Ops:
  6.6 2.7 collective-permute-start
  9.3 18.8 %collective-permute-start.1 = (f32[3,4,64,256]{3,2,1,0:T(8,128)S(1)}, f32[3,4,64,256]{3,2,1,0:T(8,128)S(1)}, u32[]{:S(2)}, u32[]{:S(2)}) collective-permute-start(f32[3,4,64,256]{3,2,1,0:T(8,128)S(1)} %collective-permute-done), channel_id=1, source_target_pairs={{0,32},{16,48},{32,0},{48,16},{64,96},{80,112},{96,64},{112,80},{1... | collective-permute-start | bytes 2359304 | tf_op jit(solution)/shard_map/ppermute | solution.py:23
  28.0 19.3 %collective-permute-start.2 = (f32[3,4,64,256]{3,2,1,0:T(8,128)S(1)}, f32[3,4,64,256]{3,2,1,0:T(8,128)S(1)}, u32[]{:S(2)}, u32[]{:S(2)}) collective-permute-start(f32[3,4,64,256]{3,2,1,0:T(8,128)S(1)} %collective-permute-done.1), channel_id=1, source_target_pairs={{0,64},{16,80},{32,96},{48,112},{64,0},{80,16},{96,32},{112,48},{1... | collective-permute-start | bytes 2359304 | tf_op jit(solution)/shard_map/ppermute | solution.py:23
  29.2 20.9 %collective-permute-start.4 = (f32[1,2,4,1,256]{4,3,2,1,0:T(1,128)S(1)}, f32[1,2,4,1,256]{4,3,2,1,0:T(1,128)S(1)}, u32[]{:S(2)}, u32[]{:S(2)}) collective-permute-start(f32[1,2,4,1,256]{4,3,2,1,0:T(1,128)S(1)} %broadcast.361), channel_id=1, source_target_pairs={{16,0},{32,16},{48,32},{64,48},{80,64},{96,80},{112,96},{128,112},... | collective-permute-start | bytes 24584 | tf_op jit(solution)/shard_map/ppermute | solution.py:17
  32.5 17.6 %collective-permute-start.5 = (f32[1,2,4,1,256]{4,3,2,1,0:T(1,128)S(1)}, f32[1,2,4,1,256]{4,3,2,1,0:T(1,128)S(1)}, u32[]{:S(2)}, u32[]{:S(2)}) collective-permute-start(f32[1,2,4,1,256]{4,3,2,1,0:T(1,128)S(1)} %broadcast.361), channel_id=1, source_target_pairs={{0,16},{16,32},{32,48},{48,64},{64,80},{80,96},{96,112},{112,128},... | collective-permute-start | bytes 24584 | tf_op jit(solution)/shard_map/ppermute | solution.py:14
  47.4 24.7 %collective-permute-start.3 = (f32[3,4,64,256]{3,2,1,0:T(8,128)S(1)}, f32[3,4,64,256]{3,2,1,0:T(8,128)S(1)}, u32[]{:S(2)}, u32[]{:S(2)}) collective-permute-start(f32[3,4,64,256]{3,2,1,0:T(8,128)S(1)} %collective-permute-done.2), channel_id=1, source_target_pairs={{0,128},{16,144},{32,160},{48,176},{64,192},{80,208},{96,224},{112... | collective-permute-start | bytes 2359304 | tf_op jit(solution)/shard_map/ppermute | solution.py:23
  51.2 27.3 %collective-permute-start.7 = (f32[1,2,4,66,1]{4,3,2,1,0:T(8,128)}, f32[1,2,4,66,1]{4,3,2,1,0:T(8,128)S(1)}, u32[]{:S(2)}, u32[]{:S(2)}) collective-permute-start(f32[1,2,4,66,1]{4,3,2,1,0:T(8,128)} %get-tuple-element.67), channel_id=1, source_target_pairs={{0,1},{1,2},{2,3},{3,4},{4,5},{5,6},{6,7},{7,8},{8,9},{9,10},{10,1... | collective-permute-start | bytes 6344 | tf_op jit(solution)/shard_map/ppermute | solution.py:14
  56.7 21.8 %collective-permute-start.6 = (f32[1,2,4,66,1]{4,3,2,1,0:T(8,128)}, f32[1,2,4,66,1]{4,3,2,1,0:T(8,128)S(1)}, u32[]{:S(2)}, u32[]{:S(2)}) collective-permute-start(f32[1,2,4,66,1]{4,3,2,1,0:T(8,128)} %get-tuple-element.66), channel_id=1, source_target_pairs={{1,0},{2,1},{3,2},{4,3},{5,4},{6,5},{7,6},{8,7},{9,8},{10,9},{11,1... | collective-permute-start | bytes 6344 | tf_op jit(solution)/shard_map/ppermute | solution.py:17
  82.3 21.3 %collective-permute-start.32 = (f32[1,2,4,1,256]{4,3,2,1,0:T(1,128)}, f32[1,2,4,1,256]{4,3,2,1,0:T(1,128)}, u32[]{:S(2)}, u32[]{:S(2)}) collective-permute-start(f32[1,2,4,1,256]{4,3,2,1,0:T(1,128)} %get-tuple-element.111), channel_id=1, source_target_pairs={{16,0},{32,16},{48,32},{64,48},{80,64},{96,80},{112,96},{128,112},... | collective-permute-start | bytes 24584 | tf_op jit(solution)/shard_map/ppermute | solution.py:17
  87.3 16.3 %collective-permute-start.33 = (f32[1,2,4,1,256]{4,3,2,1,0:T(1,128)}, f32[1,2,4,1,256]{4,3,2,1,0:T(1,128)}, u32[]{:S(2)}, u32[]{:S(2)}) collective-permute-start(f32[1,2,4,1,256]{4,3,2,1,0:T(1,128)} %get-tuple-element.110), channel_id=1, source_target_pairs={{0,16},{16,32},{32,48},{48,64},{64,80},{80,96},{96,112},{112,128},... | collective-permute-start | bytes 24584 | tf_op jit(solution)/shard_map/ppermute | solution.py:14
  94.4 16.9 %collective-permute-start.8 = (f32[1,2,4,1,256]{4,3,2,1,0:T(1,128)}, f32[1,2,4,1,256]{4,3,2,1,0:T(1,128)S(1)}, u32[]{:S(2)}, u32[]{:S(2)}) collective-permute-start(f32[1,2,4,1,256]{4,3,2,1,0:T(1,128)} %get-tuple-element.97), channel_id=1, source_target_pairs={{16,0},{32,16},{48,32},{64,48},{80,64},{96,80},{112,96},{128,112},... | collective-permute-start | bytes 24584 | tf_op jit(solution)/shard_map/ppermute | solution.py:17
  96.4 15.0 %collective-permute-start.9 = (f32[1,2,4,1,256]{4,3,2,1,0:T(1,128)}, f32[1,2,4,1,256]{4,3,2,1,0:T(1,128)S(1)}, u32[]{:S(2)}, u32[]{:S(2)}) collective-permute-start(f32[1,2,4,1,256]{4,3,2,1,0:T(1,128)} %get-tuple-element.96), channel_id=1, source_target_pairs={{0,16},{16,32},{32,48},{48,64},{64,80},{80,96},{96,112},{112,128},... | collective-permute-start | bytes 24584 | tf_op jit(solution)/shard_map/ppermute | solution.py:14
  104.6 14.6 %collective-permute-start.35 = (f32[1,2,4,66,1]{4,3,2,1,0:T(8,128)S(1)}, f32[1,2,4,66,1]{4,3,2,1,0:T(8,128)S(1)}, u32[]{:S(2)}, u32[]{:S(2)}) collective-permute-start(f32[1,2,4,66,1]{4,3,2,1,0:T(8,128)S(1)} %get-tuple-element.65), channel_id=1, source_target_pairs={{0,1},{1,2},{2,3},{3,4},{4,5},{5,6},{6,7},{7,8},{8,9},{9,10},{10,1... | collective-permute-start | bytes 6344 | tf_op jit(solution)/shard_map/ppermute | solution.py:14
  109.4 14.8 %collective-permute-start.34 = (f32[1,2,4,66,1]{4,3,2,1,0:T(8,128)S(1)}, f32[1,2,4,66,1]{4,3,2,1,0:T(8,128)S(1)}, u32[]{:S(2)}, u32[]{:S(2)}) collective-permute-start(f32[1,2,4,66,1]{4,3,2,1,0:T(8,128)S(1)} %get-tuple-element.64), channel_id=1, source_target_pairs={{1,0},{2,1},{3,2},{4,3},{5,4},{6,5},{7,6},{8,7},{9,8},{10,9},{11,1... | collective-permute-start | bytes 6344 | tf_op jit(solution)/shard_map/ppermute | solution.py:17
  111.7 19.3 %collective-permute-start.11 = (f32[1,2,4,66,1]{4,3,2,1,0:T(8,128)S(1)}, f32[1,2,4,66,1]{4,3,2,1,0:T(8,128)S(1)}, u32[]{:S(2)}, u32[]{:S(2)}) collective-permute-start(f32[1,2,4,66,1]{4,3,2,1,0:T(8,128)S(1)} %get-tuple-element.59), channel_id=1, source_target_pairs={{0,1},{1,2},{2,3},{3,4},{4,5},{5,6},{6,7},{7,8},{8,9},{9,10},{10,1... | collective-permute-start | bytes 6344 | tf_op jit(solution)/shard_map/ppermute | solution.py:14
  117.3 13.7 %collective-permute-start.10 = (f32[1,2,4,66,1]{4,3,2,1,0:T(8,128)S(1)}, f32[1,2,4,66,1]{4,3,2,1,0:T(8,128)S(1)}, u32[]{:S(2)}, u32[]{:S(2)}) collective-permute-start(f32[1,2,4,66,1]{4,3,2,1,0:T(8,128)S(1)} %get-tuple-element.58), channel_id=1, source_target_pairs={{1,0},{2,1},{3,2},{4,3},{5,4},{6,5},{7,6},{8,7},{9,8},{10,9},{11,1... | collective-permute-start | bytes 6344 | tf_op jit(solution)/shard_map/ppermute | solution.py:17
  131.8 18.4 %collective-permute-start.36 = (f32[1,2,4,1,256]{4,3,2,1,0:T(1,128)S(1)}, f32[1,2,4,1,256]{4,3,2,1,0:T(1,128)S(1)}, u32[]{:S(2)}, u32[]{:S(2)}) collective-permute-start(f32[1,2,4,1,256]{4,3,2,1,0:T(1,128)S(1)} %get-tuple-element.107), channel_id=1, source_target_pairs={{16,0},{32,16},{48,32},{64,48},{80,64},{96,80},{112,96},{128,112},... | collective-permute-start | bytes 24584 | tf_op jit(solution)/shard_map/ppermute | solution.py:17
  133.8 16.5 %collective-permute-start.37 = (f32[1,2,4,1,256]{4,3,2,1,0:T(1,128)S(1)}, f32[1,2,4,1,256]{4,3,2,1,0:T(1,128)S(1)}, u32[]{:S(2)}, u32[]{:S(2)}) collective-permute-start(f32[1,2,4,1,256]{4,3,2,1,0:T(1,128)S(1)} %get-tuple-element.106), channel_id=1, source_target_pairs={{0,16},{16,32},{32,48},{48,64},{64,80},{80,96},{96,112},{112,128},... | collective-permute-start | bytes 24584 | tf_op jit(solution)/shard_map/ppermute | solution.py:14
  141.0 17.1 %collective-permute-start.12 = (f32[1,2,4,1,256]{4,3,2,1,0:T(1,128)S(1)}, f32[1,2,4,1,256]{4,3,2,1,0:T(1,128)S(1)}, u32[]{:S(2)}, u32[]{:S(2)}) collective-permute-start(f32[1,2,4,1,256]{4,3,2,1,0:T(1,128)S(1)} %get-tuple-element.93), channel_id=1, source_target_pairs={{16,0},{32,16},{48,32},{64,48},{80,64},{96,80},{112,96},{128,112},... | collective-permute-start | bytes 24584 | tf_op jit(solution)/shard_map/ppermute | solution.py:17
  143.0 15.2 %collective-permute-start.13 = (f32[1,2,4,1,256]{4,3,2,1,0:T(1,128)S(1)}, f32[1,2,4,1,256]{4,3,2,1,0:T(1,128)S(1)}, u32[]{:S(2)}, u32[]{:S(2)}) collective-permute-start(f32[1,2,4,1,256]{4,3,2,1,0:T(1,128)S(1)} %get-tuple-element.92), channel_id=1, source_target_pairs={{0,16},{16,32},{32,48},{48,64},{64,80},{80,96},{96,112},{112,128},... | collective-permute-start | bytes 24584 | tf_op jit(solution)/shard_map/ppermute | solution.py:14
  150.5 15.3 %collective-permute-start.39 = (f32[1,2,4,66,1]{4,3,2,1,0:T(8,128)S(1)}, f32[1,2,4,66,1]{4,3,2,1,0:T(8,128)S(1)}, u32[]{:S(2)}, u32[]{:S(2)}) collective-permute-start(f32[1,2,4,66,1]{4,3,2,1,0:T(8,128)S(1)} %get-tuple-element.63), channel_id=1, source_target_pairs={{0,1},{1,2},{2,3},{3,4},{4,5},{5,6},{6,7},{7,8},{8,9},{9,10},{10,1... | collective-permute-start | bytes 6344 | tf_op jit(solution)/shard_map/ppermute | solution.py:14
  156.2 13.9 %collective-permute-start.38 = (f32[1,2,4,66,1]{4,3,2,1,0:T(8,128)S(1)}, f32[1,2,4,66,1]{4,3,2,1,0:T(8,128)S(1)}, u32[]{:S(2)}, u32[]{:S(2)}) collective-permute-start(f32[1,2,4,66,1]{4,3,2,1,0:T(8,128)S(1)} %get-tuple-element.62), channel_id=1, source_target_pairs={{1,0},{2,1},{3,2},{4,3},{5,4},{6,5},{7,6},{8,7},{9,8},{10,9},{11,1... | collective-permute-start | bytes 6344 | tf_op jit(solution)/shard_map/ppermute | solution.py:17
  158.4 19.1 %collective-permute-start.15 = (f32[1,2,4,66,1]{4,3,2,1,0:T(8,128)S(1)}, f32[1,2,4,66,1]{4,3,2,1,0:T(8,128)S(1)}, u32[]{:S(2)}, u32[]{:S(2)}) collective-permute-start(f32[1,2,4,66,1]{4,3,2,1,0:T(8,128)S(1)} %get-tuple-element.57), channel_id=1, source_target_pairs={{0,1},{1,2},{2,3},{3,4},{4,5},{5,6},{6,7},{7,8},{8,9},{9,10},{10,1... | collective-permute-start | bytes 6344 | tf_op jit(solution)/shard_map/ppermute | solution.py:14
  163.9 13.6 %collective-permute-start.14 = (f32[1,2,4,66,1]{4,3,2,1,0:T(8,128)S(1)}, f32[1,2,4,66,1]{4,3,2,1,0:T(8,128)S(1)}, u32[]{:S(2)}, u32[]{:S(2)}) collective-permute-start(f32[1,2,4,66,1]{4,3,2,1,0:T(8,128)S(1)} %get-tuple-element.56), channel_id=1, source_target_pairs={{1,0},{2,1},{3,2},{4,3},{5,4},{6,5},{7,6},{8,7},{9,8},{10,9},{11,1... | collective-permute-start | bytes 6344 | tf_op jit(solution)/shard_map/ppermute | solution.py:17
  178.4 27.2 %collective-permute-start.40 = (f32[1,2,4,1,256]{4,3,2,1,0:T(1,128)S(1)}, f32[1,2,4,1,256]{4,3,2,1,0:T(1,128)S(1)}, u32[]{:S(2)}, u32[]{:S(2)}) collective-permute-start(f32[1,2,4,1,256]{4,3,2,1,0:T(1,128)S(1)} %get-tuple-element.103), channel_id=1, source_target_pairs={{16,0},{32,16},{48,32},{64,48},{80,64},{96,80},{112,96},{128,112},... | collective-permute-start | bytes 24584 | tf_op jit(solution)/shard_map/ppermute | solution.py:17
  180.3 25.3 %collective-permute-start.41 = (f32[1,2,4,1,256]{4,3,2,1,0:T(1,128)S(1)}, f32[1,2,4,1,256]{4,3,2,1,0:T(1,128)S(1)}, u32[]{:S(2)}, u32[]{:S(2)}) collective-permute-start(f32[1,2,4,1,256]{4,3,2,1,0:T(1,128)S(1)} %get-tuple-element.102), channel_id=1, source_target_pairs={{0,16},{16,32},{32,48},{48,64},{64,80},{80,96},{96,112},{112,128},... | collective-permute-start | bytes 24584 | tf_op jit(solution)/shard_map/ppermute | solution.py:14
  187.6 9.2 %collective-permute-start.16 = (f32[1,2,4,1,256]{4,3,2,1,0:T(1,128)S(1)}, f32[1,2,4,1,256]{4,3,2,1,0:T(1,128)S(1)}, u32[]{:S(2)}, u32[]{:S(2)}) collective-permute-start(f32[1,2,4,1,256]{4,3,2,1,0:T(1,128)S(1)} %get-tuple-element.87), channel_id=1, source_target_pairs={{16,0},{32,16},{48,32},{64,48},{80,64},{96,80},{112,96},{128,112},... | collective-permute-start | bytes 24584 | tf_op jit(solution)/shard_map/ppermute | solution.py:17
  189.5 8.0 %collective-permute-start.17 = (f32[1,2,4,1,256]{4,3,2,1,0:T(1,128)S(1)}, f32[1,2,4,1,256]{4,3,2,1,0:T(1,128)S(1)}, u32[]{:S(2)}, u32[]{:S(2)}) collective-permute-start(f32[1,2,4,1,256]{4,3,2,1,0:T(1,128)S(1)} %get-tuple-element.86), channel_id=1, source_target_pairs={{0,16},{16,32},{32,48},{48,64},{64,80},{80,96},{96,112},{112,128},... | collective-permute-start | bytes 24584 | tf_op jit(solution)/shard_map/ppermute | solution.py:14
  197.8 15.6 %collective-permute-start.19 = (f32[1,2,4,66,1]{4,3,2,1,0:T(8,128)S(1)}, f32[1,2,4,66,1]{4,3,2,1,0:T(8,128)S(1)}, u32[]{:S(2)}, u32[]{:S(2)}) collective-permute-start(f32[1,2,4,66,1]{4,3,2,1,0:T(8,128)S(1)} %get-tuple-element.55), channel_id=1, source_target_pairs={{0,1},{1,2},{2,3},{3,4},{4,5},{5,6},{6,7},{7,8},{8,9},{9,10},{10,1... | collective-permute-start | bytes 6344 | tf_op jit(solution)/shard_map/ppermute | solution.py:14
  203.6 14.4 %collective-permute-start.18 = (f32[1,2,4,66,1]{4,3,2,1,0:T(8,128)S(1)}, f32[1,2,4,66,1]{4,3,2,1,0:T(8,128)S(1)}, u32[]{:S(2)}, u32[]{:S(2)}) collective-permute-start(f32[1,2,4,66,1]{4,3,2,1,0:T(8,128)S(1)} %get-tuple-element.54), channel_id=1, source_target_pairs={{1,0},{2,1},{3,2},{4,3},{5,4},{6,5},{7,6},{8,7},{9,8},{10,9},{11,1... | collective-permute-start | bytes 6344 | tf_op jit(solution)/shard_map/ppermute | solution.py:17
  205.8 19.1 %collective-permute-start.43 = (f32[1,2,4,66,1]{4,3,2,1,0:T(8,128)S(1)}, f32[1,2,4,66,1]{4,3,2,1,0:T(8,128)S(1)}, u32[]{:S(2)}, u32[]{:S(2)}) collective-permute-start(f32[1,2,4,66,1]{4,3,2,1,0:T(8,128)S(1)} %get-tuple-element.61), channel_id=1, source_target_pairs={{0,1},{1,2},{2,3},{3,4},{4,5},{5,6},{6,7},{7,8},{8,9},{9,10},{10,1... | collective-permute-start | bytes 6344 | tf_op jit(solution)/shard_map/ppermute | solution.py:14
  211.3 13.7 %collective-permute-start.42 = (f32[1,2,4,66,1]{4,3,2,1,0:T(8,128)S(1)}, f32[1,2,4,66,1]{4,3,2,1,0:T(8,128)S(1)}, u32[]{:S(2)}, u32[]{:S(2)}) collective-permute-start(f32[1,2,4,66,1]{4,3,2,1,0:T(8,128)S(1)} %get-tuple-element.60), channel_id=1, source_target_pairs={{1,0},{2,1},{3,2},{4,3},{5,4},{6,5},{7,6},{8,7},{9,8},{10,9},{11,1... | collective-permute-start | bytes 6344 | tf_op jit(solution)/shard_map/ppermute | solution.py:17
  225.7 10.3 %collective-permute-start.20 = (f32[1,2,4,1,256]{4,3,2,1,0:T(1,128)S(1)}, f32[1,2,4,1,256]{4,3,2,1,0:T(1,128)S(1)}, u32[]{:S(2)}, u32[]{:S(2)}) collective-permute-start(f32[1,2,4,1,256]{4,3,2,1,0:T(1,128)S(1)} %get-tuple-element.85), channel_id=1, source_target_pairs={{16,0},{32,16},{48,32},{64,48},{80,64},{96,80},{112,96},{128,112},... | collective-permute-start | bytes 24584 | tf_op jit(solution)/shard_map/ppermute | solution.py:17
  227.6 9.1 %collective-permute-start.21 = (f32[1,2,4,1,256]{4,3,2,1,0:T(1,128)S(1)}, f32[1,2,4,1,256]{4,3,2,1,0:T(1,128)S(1)}, u32[]{:S(2)}, u32[]{:S(2)}) collective-permute-start(f32[1,2,4,1,256]{4,3,2,1,0:T(1,128)S(1)} %get-tuple-element.84), channel_id=1, source_target_pairs={{0,16},{16,32},{32,48},{48,64},{64,80},{80,96},{96,112},{112,128},... | collective-permute-start | bytes 24584 | tf_op jit(solution)/shard_map/ppermute | solution.py:14
  236.9 8.5 %collective-permute-start.23 = (f32[1,2,4,66,1]{4,3,2,1,0:T(8,128)S(1)}, f32[1,2,4,66,1]{4,3,2,1,0:T(8,128)S(1)}, u32[]{:S(2)}, u32[]{:S(2)}) collective-permute-start(f32[1,2,4,66,1]{4,3,2,1,0:T(8,128)S(1)} %get-tuple-element.53), channel_id=1, source_target_pairs={{0,1},{1,2},{2,3},{3,4},{4,5},{5,6},{6,7},{7,8},{8,9},{9,10},{10,1... | collective-permute-start | bytes 6344 | tf_op jit(solution)/shard_map/ppermute | solution.py:14
  241.7 9.8 %collective-permute-start.22 = (f32[1,2,4,66,1]{4,3,2,1,0:T(8,128)S(1)}, f32[1,2,4,66,1]{4,3,2,1,0:T(8,128)S(1)}, u32[]{:S(2)}, u32[]{:S(2)}) collective-permute-start(f32[1,2,4,66,1]{4,3,2,1,0:T(8,128)S(1)} %get-tuple-element.52), channel_id=1, source_target_pairs={{1,0},{2,1},{3,2},{4,3},{5,4},{6,5},{7,6},{8,7},{9,8},{10,9},{11,1... | collective-permute-start | bytes 6344 | tf_op jit(solution)/shard_map/ppermute | solution.py:17
  252.3 10.5 %collective-permute-start.24 = (f32[1,2,4,1,256]{4,3,2,1,0:T(1,128)S(1)}, f32[1,2,4,1,256]{4,3,2,1,0:T(1,128)S(1)}, u32[]{:S(2)}, u32[]{:S(2)}) collective-permute-start(f32[1,2,4,1,256]{4,3,2,1,0:T(1,128)S(1)} %get-tuple-element.81), channel_id=1, source_target_pairs={{16,0},{32,16},{48,32},{64,48},{80,64},{96,80},{112,96},{128,112},... | collective-permute-start | bytes 24584 | tf_op jit(solution)/shard_map/ppermute | solution.py:17
  254.3 9.3 %collective-permute-start.25 = (f32[1,2,4,1,256]{4,3,2,1,0:T(1,128)S(1)}, f32[1,2,4,1,256]{4,3,2,1,0:T(1,128)S(1)}, u32[]{:S(2)}, u32[]{:S(2)}) collective-permute-start(f32[1,2,4,1,256]{4,3,2,1,0:T(1,128)S(1)} %get-tuple-element.80), channel_id=1, source_target_pairs={{0,16},{16,32},{32,48},{48,64},{64,80},{80,96},{96,112},{112,128},... | collective-permute-start | bytes 24584 | tf_op jit(solution)/shard_map/ppermute | solution.py:14
  263.8 9.3 %collective-permute-start.27 = (f32[1,2,4,66,1]{4,3,2,1,0:T(8,128)S(1)}, f32[1,2,4,66,1]{4,3,2,1,0:T(8,128)S(1)}, u32[]{:S(2)}, u32[]{:S(2)}) collective-permute-start(f32[1,2,4,66,1]{4,3,2,1,0:T(8,128)S(1)} %get-tuple-element.51), channel_id=1, source_target_pairs={{0,1},{1,2},{2,3},{3,4},{4,5},{5,6},{6,7},{7,8},{8,9},{9,10},{10,1... | collective-permute-start | bytes 6344 | tf_op jit(solution)/shard_map/ppermute | solution.py:14
  268.4 10.8 %collective-permute-start.26 = (f32[1,2,4,66,1]{4,3,2,1,0:T(8,128)S(1)}, f32[1,2,4,66,1]{4,3,2,1,0:T(8,128)S(1)}, u32[]{:S(2)}, u32[]{:S(2)}) collective-permute-start(f32[1,2,4,66,1]{4,3,2,1,0:T(8,128)S(1)} %get-tuple-element.50), channel_id=1, source_target_pairs={{1,0},{2,1},{3,2},{4,3},{5,4},{6,5},{7,6},{8,7},{9,8},{10,9},{11,1... | collective-permute-start | bytes 6344 | tf_op jit(solution)/shard_map/ppermute | solution.py:17
  280.0 9.5 %collective-permute-start.28 = (f32[1,2,4,1,256]{4,3,2,1,0:T(1,128)S(1)}, f32[1,2,4,1,256]{4,3,2,1,0:T(1,128)S(1)}, u32[]{:S(2)}, u32[]{:S(2)}) collective-permute-start(f32[1,2,4,1,256]{4,3,2,1,0:T(1,128)S(1)} %get-tuple-element.77), channel_id=1, source_target_pairs={{16,0},{32,16},{48,32},{64,48},{80,64},{96,80},{112,96},{128,112},... | collective-permute-start | bytes 24584 | tf_op jit(solution)/shard_map/ppermute | solution.py:17
  281.9 8.3 %collective-permute-start.29 = (f32[1,2,4,1,256]{4,3,2,1,0:T(1,128)S(1)}, f32[1,2,4,1,256]{4,3,2,1,0:T(1,128)S(1)}, u32[]{:S(2)}, u32[]{:S(2)}) collective-permute-start(f32[1,2,4,1,256]{4,3,2,1,0:T(1,128)S(1)} %get-tuple-element.76), channel_id=1, source_target_pairs={{0,16},{16,32},{32,48},{48,64},{64,80},{80,96},{96,112},{112,128},... | collective-permute-start | bytes 24584 | tf_op jit(solution)/shard_map/ppermute | solution.py:14
  290.4 10.3 %collective-permute-start.31 = (f32[1,2,4,66,1]{4,3,2,1,0:T(8,128)S(1)}, f32[1,2,4,66,1]{4,3,2,1,0:T(8,128)S(1)}, u32[]{:S(2)}, u32[]{:S(2)}) collective-permute-start(f32[1,2,4,66,1]{4,3,2,1,0:T(8,128)S(1)} %get-tuple-element.49), channel_id=1, source_target_pairs={{0,1},{1,2},{2,3},{3,4},{4,5},{5,6},{6,7},{7,8},{8,9},{9,10},{10,1... | collective-permute-start | bytes 6344 | tf_op jit(solution)/shard_map/ppermute | solution.py:14
  296.1 10.8 %collective-permute-start.30 = (f32[1,2,4,66,1]{4,3,2,1,0:T(8,128)S(1)}, f32[1,2,4,66,1]{4,3,2,1,0:T(8,128)S(1)}, u32[]{:S(2)}, u32[]{:S(2)}) collective-permute-start(f32[1,2,4,66,1]{4,3,2,1,0:T(8,128)S(1)} %get-tuple-element.48), channel_id=1, source_target_pairs={{1,0},{2,1},{3,2},{4,3},{5,4},{6,5},{7,6},{8,7},{9,8},{10,9},{11,1... | collective-permute-start | bytes 6344 | tf_op jit(solution)/shard_map/ppermute | solution.py:17
  307.9 2.4 collective-permute-start.44
  310.2 19.0 %collective-permute-start.45 = (f32[3,4,64,256]{3,2,1,0:T(8,128)S(1)}, f32[3,4,64,256]{3,2,1,0:T(8,128)S(1)}, u32[]{:S(2)}, u32[]{:S(2)}) collective-permute-start(f32[3,4,64,256]{3,2,1,0:T(8,128)S(1)} %collective-permute-done.44), channel_id=1, source_target_pairs={{0,32},{16,48},{32,0},{48,16},{64,96},{80,112},{96,64},{112,80},{1... | collective-permute-start | bytes 2359304 | tf_op jit(solution)/shard_map/ppermute | solution.py:23
  329.3 19.6 %collective-permute-start.46 = (f32[3,4,64,256]{3,2,1,0:T(8,128)S(1)}, f32[3,4,64,256]{3,2,1,0:T(8,128)S(1)}, u32[]{:S(2)}, u32[]{:S(2)}) collective-permute-start(f32[3,4,64,256]{3,2,1,0:T(8,128)S(1)} %collective-permute-done.45), channel_id=1, source_target_pairs={{0,64},{16,80},{32,96},{48,112},{64,0},{80,16},{96,32},{112,48},{1... | collective-permute-start | bytes 2359304 | tf_op jit(solution)/shard_map/ppermute | solution.py:23
  348.8 18.7 %collective-permute-start.47 = (f32[3,4,64,256]{3,2,1,0:T(8,128)S(1)}, f32[3,4,64,256]{3,2,1,0:T(8,128)S(1)}, u32[]{:S(2)}, u32[]{:S(2)}) collective-permute-start(f32[3,4,64,256]{3,2,1,0:T(8,128)S(1)} %collective-permute-done.46), channel_id=1, source_target_pairs={{0,128},{16,144},{32,160},{48,176},{64,192},{80,208},{96,224},{112... | collective-permute-start | bytes 2359304 | tf_op jit(solution)/shard_map/ppermute | solution.py:23
  (17 other events, 213.8 us)
where the time goes:
time: 376 us; the launch traced here: 370 us
  starting transfers between devices  175 us (47%)
  waiting for transfers between devices  165 us (44%)
  other arithmetic  15.5 us (4%)
  local copies, waits for them, and re-layouts  13.1 us (3%)
    ppermute x20, starting transfers between devices, with_halo(): lax.ppermute(lax.slice_in_dim(block, block.shape[dim] - width, None, axis...  124 us
    ppermute x8, waiting for transfers between devices, partner(): lax.ppermute(shard, axis, [(i, i ^ 1 << bit) for i in range(lax.axis_size...  99.3 us
    ppermute x20, starting transfers between devices, with_halo(): lax.ppermute(lax.slice_in_dim(block, 0, width, axis=dim), axis, backward)  43.1 us
    ppermute x20, waiting for transfers between devices, with_halo(): lax.ppermute(lax.slice_in_dim(block, block.shape[dim] - width, None, axis...  33.2 us
    ppermute x20, waiting for transfers between devices, with_halo(): lax.ppermute(lax.slice_in_dim(block, 0, width, axis=dim), axis, backward)  32.5 us
    div x11, other arithmetic, pointwise_iterative_update(): (source + neighbours(values, conductance_tuple, joined_counterpart)) / ma...  8.63 us
  transfers between devices with their start and end apart: 48, of which 25 were waited for; matrix products, arithmetic and copies ran while one was open for 3% of the time, Pallas kernels for 0%

commit v1 on v0

v1 whole, which is shorter than its diff:
```python
import functools

import jax
import jax.numpy as jnp
from jax import lax
from jax.experimental import pallas as pl
from jax.experimental.pallas import tpu as pltpu
from jax.sharding import PartitionSpec as P


BLOCKS = 32
ROWS = 80
DEEP = 6
NEAR = 3
F32 = jnp.float32

VMEM = pl.BlockSpec(memory_space=pltpu.VMEM)
SMEM = pl.BlockSpec(memory_space=pltpu.SMEM)

STRIP_H = [DEEP] * 3 + [NEAR] * 16
STRIP_AT = [sum(STRIP_H[:n]) for n in range(19)]
PART_H = [DEEP] * 3 + [2, 1] * 4
PART_AT = [2 * sum(PART_H[:n]) for n in range(11)]


def lanes():
    return lax.broadcasted_iota(jnp.int32, (8, 128), 1)


def sublanes():
    return lax.broadcasted_iota(jnp.int32, (8, 128), 0)


def rolled(x, shift, axis):
    size = x.shape[axis]
    shift %= size
    return x if shift == 0 else pltpu.roll(x, shift, axis)


def mirrored(x):
    return jnp.take_along_axis(x, 7 - sublanes(), axis=0)


def field_tile(refs, n, rows, t):
    power, bond, sensor, peak = refs
    if n < 2:
        return power[n, t, rows, :]
    cut = slice(128 * t, 128 * t + 128)
    if n == 2:
        return bond[rows, cut]
    field = sensor if n < 11 else peak
    m = (n - 3) % 8
    return field[m // 4, m % 4, rows, cut]


def ring_tile(from_right, from_left, n):
    h, at = STRIP_H[n], STRIP_AT[n]
    lane = lanes()
    return jnp.where(
        lane < h,
        rolled(from_right, -at, 1),
        jnp.where(lane >= 128 - h, rolled(from_left, 128 - h - at, 1), 0.0),
    )


def flip_layers_kernel(field, out):
    for d in range(2):
        for l in range(3):
            for t in range(2):
                for k in range(8):
                    out[d, l, t, 8 * (7 - k) : 8 * (8 - k), :] = mirrored(
                        field[d, l + 1, 8 * k : 8 * k + 8, 128 * t : 128 * t + 128]
                    )


def column_kernel(place, block_power, ids, bond, sensor, peak, power, to_a, to_b):
    values = [block_power[n] for n in range(BLOCKS)]

    def look_up(k, _):
        rows = pl.ds(pl.multiple_of(8 * k, 8), 8)
        for d in range(2):
            for t in range(2):
                index = ids[d, rows, 128 * t : 128 * t + 128]
                level = values
                bit = 1
                while len(level) > 1:
                    odd = (index & bit) != 0
                    level = [
                        jnp.where(odd, level[2 * n + 1], level[2 * n])
                        for n in range(len(level) // 2)
                    ]
                    bit *= 2
                power[d, t, rows, :] = level[0]
        return 0

    lax.fori_loop(0, 8, look_up, 0)
    even = (place[1] & 1) == 0
    refs = (power, bond, sensor, peak)

    def pack(k, _):
        rows = pl.ds(pl.multiple_of(8 * k, 8), 8)
        lane = lanes()
        right_edge = jnp.zeros((8, 128), F32)
        left_edge = jnp.zeros((8, 128), F32)
        for n in range(19):
            h, at = STRIP_H[n], STRIP_AT[n]
            here = (lane >= at) & (lane < at + h)
            left_edge = jnp.where(here, rolled(field_tile(refs, n, rows, 0), at, 1), left_edge)
            right_edge = jnp.where(
                here, rolled(field_tile(refs, n, rows, 1), at - (128 - h), 1), right_edge
            )
        to_a[rows, :] = jnp.where(even, right_edge, left_edge)
        to_b[rows, :] = jnp.where(even, left_edge, right_edge)
        return 0

    lax.fori_loop(0, 8, pack, 0)


def sides(place, axis, from_a, from_b, rows):
    even = (place[axis] & 1) == 0
    a, b = from_a[rows, :], from_b[rows, :]
    return jnp.where(even, a, b), jnp.where(even, b, a)


def row_kernel(place, power, bond, sensor, peak, col_a, col_b, to_a, to_b):
    even = (place[0] & 1) == 0
    refs = (power, bond, sensor, peak)
    row = sublanes()
    strips = []
    for first in (0, 56):
        rows = slice(first, first + 8)
        right, left = sides(place, 1, col_a, col_b, rows)

        def tile(n, t):
            return field_tile(refs, n, rows, t) if t < 2 else ring_tile(right, left, n)

        strip = []
        for t in range(3):
            for n in range(3):
                strip.append(tile(n, t))
            for m in range(8):
                x, y = tile(3 + 2 * m, t), tile(4 + 2 * m, t)
                if first == 0:
                    strip.append(jnp.where(row < 4, x, rolled(y, 4, 0)))
                else:
                    strip.append(jnp.where(row >= 4, x, rolled(y, -4, 0)))
        strips.append(strip)
    top, bottom = strips
    for n in range(33):
        rows = slice(8 * n, 8 * n + 8)
        to_a[rows, :] = jnp.where(even, bottom[n], top[n])
        to_b[rows, :] = jnp.where(even, top[n], bottom[n])


def build_kernel(place, power, bond, sensor, peak, col_a, col_b, row_a, row_b, own, message):
    refs = (power, bond, sensor, peak)

    def core(k, _):
        rows = pl.ds(pl.multiple_of(8 * k, 8), 8)
        to = pl.ds(pl.multiple_of(8 * k + 8, 8), 8)
        right, left = sides(place, 1, col_a, col_b, rows)
        for n in range(19):
            own[n, 0, to, :] = field_tile(refs, n, rows, 0)
            own[n, 1, to, :] = field_tile(refs, n, rows, 1)
            own[n, 2, to, :] = ring_tile(right, left, n)
        return 0

    lax.fori_loop(0, 8, core, 0)
    for t in range(3):
        for n in range(11):
            at = 8 * (11 * t + n)
            below, above = sides(place, 0, row_a, row_b, slice(at, at + 8))
            if n < 3:
                own[n, t, 0:8, :] = above
                own[n, t, 72:80, :] = below
            else:
                m = 3 + 2 * (n - 3)
                own[m, t, 0:8, :] = above
                own[m, t, 72:80, :] = below
                own[m + 1, t, 0:8, :] = rolled(above, 4, 0)
                own[m + 1, t, 72:80, :] = rolled(below, -4, 0)

    def pack(k, _):
        rows = pl.ds(pl.multiple_of(8 * k, 8), 8)
        back = 8 * (9 - k)
        lane = lanes()
        for n in range(3):
            for t in range(2):
                to = pl.ds(pl.multiple_of(80 * (2 * n + t) + back, 8), 8)
                message[to, :] = mirrored(own[n, t, rows, :])
        column = jnp.zeros((8, 128), F32)
        planes = [0, 1, 2]
        for field in range(2):
            for d in range(2):
                planes += [3 + 8 * field + 4 * d + 3, 3 + 8 * field + 4 * d + 2]
        for slot, n in enumerate(planes):
            h, at = PART_H[slot], PART_AT[slot]
            here = (lane >= at) & (lane < at + 2 * h)
            column = jnp.where(here, rolled(own[n, 2, rows, :], at + h, 1), column)
        message[pl.ds(pl.multiple_of(480 + back, 8), 8), :] = mirrored(column)
        return 0

    lax.fori_loop(0, 10, pack, 0)
    row = sublanes()
    for field in range(2):
        for d in range(2):
            n = 3 + 8 * field + 4 * d
            for t in range(2):
                above = jnp.where(
                    row >= 4, own[n + 3, t, 0:8, :], rolled(own[n + 2, t, 0:8, :], 4, 0)
                )
                below = jnp.where(
                    row < 4, own[n + 3, t, 72:80, :], rolled(own[n + 2, t, 72:80, :], 4, 0)
                )
                at = 560 + 16 * (4 * field + 2 * d + t)
                message[at : at + 8, :] = mirrored(below)
                message[at + 8 : at + 16, :] = mirrored(above)


def partner_ring(message, slot, rows):
    h, at = PART_H[slot], PART_AT[slot]
    lane = lanes()
    return jnp.where(
        (lane < h) | (lane >= 128 - h), rolled(message[rows, :], -(at + h), 1), 0.0
    )


class Solver:
    def __init__(self, place, tables, d, v, cond, v_scalars=None):
        self.place, self.d, self.v, self.cond = place, d, v, cond
        layer_class, share, lateral, vertical, sink = tables
        self.coef = []
        for side in range(2):
            die = d if side == 0 else 1 - d
            classes = [layer_class[die, l] for l in range(4)]
            coefs = []
            for l in range(4):
                g = lateral[classes[l]]
                up = vertical[classes[l]] if l < 3 else jnp.float32(0)
                down = vertical[classes[l - 1]] if l > 0 else jnp.float32(0)
                diagonal = 4 * g + up + down
                if l == 0:
                    diagonal = diagonal + sink[die]
                part = share[classes[l]] if share is not None else None
                if l < 3:
                    inverse = 1.0 / jnp.full((8, 128), diagonal, F32)
                    coefs.append(
                        (
                            inverse if part is None else inverse * part,
                            g * inverse,
                            up * inverse,
                            down * inverse,
                        )
                    )
                else:
                    coefs.append((diagonal, g, down, part))
            self.coef.append(coefs)

    def prepare(self, bond_tile):
        def body(k, _):
            rows = pl.ds(pl.multiple_of(8 * k, 8), 8)
            for t in range(3):
                bond = bond_tile(k, rows, t)
                self.cond[0, t, rows, :] = bond
                for side in range(2):
                    self.cond[1 + side, t, rows, :] = 1.0 / (self.coef[side][3][0] + bond)
            return 0

        lax.fori_loop(0, 10, body, 0)

    def masks(self, k):
        gx, gy = self.place[0], self.place[1]
        outside = ((k == 0) & (gx == 0)) | ((k == 9) & (gx == 15))
        row = jnp.where(outside, 0.0, 1.0).astype(F32)
        lane = lanes()
        right = jnp.where(gy == 15, 0.0, 1.0).astype(F32)
        left = jnp.where(gy == 0, 0.0, 1.0).astype(F32)
        ring = jnp.where(lane < 64, right, left)
        return row, row * ring

    def first(self, side, layers, source):
        def body(k, _):
            rows = pl.ds(pl.multiple_of(8 * k, 8), 8)
            to = pl.ds(pl.multiple_of(8 * k + 8, 8), 8)
            row, ring = self.masks(k)
            for t in range(3):
                mask = ring if t == 2 else row
                shared = {}
                for l in layers:
                    s = source(l, t, rows, shared)
                    coef = self.coef[side][l]
                    if l < 3:
                        s = s * coef[0]
                    else:
                        if coef[3] is not None:
                            s = s * coef[3]
                        s = s * self.cond[1 + side, t, rows, :]
                    self.v[0, side, l, t, to, :] = s * mask
            return 0

        lax.fori_loop(0, 10, body, 0)

    def sweep(self, b, side, layers, source, emit=None, core_only=False):
        v = self.v

        def body(k, _):
            rows = pl.ds(pl.multiple_of(8 * k, 8), 8)
            to = pl.ds(pl.multiple_of(8 * k + 8, 8), 8)
            row, ring = self.masks(k)
            lane = lanes()
            shared = {}
            for l in layers:
                coef = self.coef[side][l]
                centre = [v[b, side, l, t, to, :] for t in range(3)]
                forward = [pltpu.roll(c, 1, 1) for c in centre]
                backward = [pltpu.roll(c, 127, 1) for c in centre]
                for t in range(2 if core_only else 3):
                    left = jnp.where(lane == 0, forward[t - 1], forward[t])
                    right = jnp.where(lane == 127, backward[(t + 1) % 3], backward[t])
                    lateral = (left + right) + (
                        v[b, side, l, t, pl.ds(8 * k + 7, 8), :]
                        + v[b, side, l, t, pl.ds(8 * k + 9, 8), :]
                    )
                    s = source(l, t, rows, shared)
                    if l < 3:
                        total = s * coef[0] + coef[1] * lateral
                        total = total + coef[2] * v[b, side, l + 1, t, to, :]
                        if l > 0:
                            total = total + coef[3] * v[b, side, l - 1, t, to, :]
                    else:
                        if coef[3] is not None:
                            s = s * coef[3]
                        total = s + coef[1] * lateral
                        total = total + coef[2] * v[b, side, 2, t, to, :]
                        total = total + self.cond[0, t, rows, :] * v[b, 1 - side, 3, t, to, :]
                        total = total * self.cond[1 + side, t, rows, :]
                    if not core_only:
                        total = total * (ring if t == 2 else row)
                    if emit is None:
                        v[1 - b, side, l, t, to, :] = total
                    else:
                        emit(l, t, k, rows, total)
            return 0

        if core_only:
            lax.fori_loop(1, 9, body, 0)
        else:
            lax.fori_loop(0, 10, body, 0)

    def partial_solve(self, own_source, other_source, emit):
        self.first(0, (0, 1, 2, 3), own_source)
        self.first(1, (1, 2, 3), other_source)
        self.sweep(0, 0, (0, 1, 2, 3), own_source)
        self.sweep(0, 1, (2, 3), other_source)
        self.sweep(1, 0, (0, 1, 2, 3), own_source)
        self.sweep(1, 1, (3,), other_source)
        self.sweep(0, 0, (0, 1, 2, 3), own_source, emit, core_only=True)


def clear_pads(v):
    zero = jnp.zeros((8, 128), F32)
    for b in range(2):
        for side in range(2):
            for l in range(4):
                for t in range(3):
                    v[b, side, l, t, 0:8, :] = zero
                    v[b, side, l, t, 88:96, :] = zero


def place_other(planes, layers_in, message, field, d):
    other = 1 - d
    zero = jnp.zeros((8, 128), F32)

    def body(k, _):
        rows = pl.ds(pl.multiple_of(8 * k, 8), 8)
        to = pl.ds(pl.multiple_of(8 * k + 8, 8), 8)
        for l in range(3):
            for t in range(2):
                planes[l, t, to, :] = layers_in[other, l, t, rows, :]
        return 0

    lax.fori_loop(0, 8, body, 0)

    def ring(k, _):
        rows = pl.ds(pl.multiple_of(8 * k, 8), 8)
        column = message[pl.ds(pl.multiple_of(480 + 8 * k, 8), 8), :]
        lane = lanes()
        planes[0, 2, rows, :] = zero
        for slot_in, l, h in ((0, 2, 2), (1, 1, 1)):
            ats = [PART_AT[3 + 4 * field + 2 * die + slot_in] + h for die in range(2)]
            picked = jnp.where(other == 0, rolled(column, -ats[0], 1), rolled(column, -ats[1], 1))
            planes[l, 2, rows, :] = jnp.where((lane < h) | (lane >= 128 - h), picked, 0.0)
        return 0

    lax.fori_loop(0, 10, ring, 0)
    for t in range(2):
        planes[0, t, 0:8, :] = zero
        planes[0, t, 72:80, :] = zero
        at = 560 + 64 * field + 32 * other + 16 * t
        above = message[pl.ds(pl.multiple_of(at, 8), 8), :]
        below = message[pl.ds(pl.multiple_of(at + 8, 8), 8), :]
        planes[2, t, 0:8, :] = above
        planes[2, t, 72:80, :] = below
        planes[1, t, 0:8, :] = rolled(above, 4, 0)
        planes[1, t, 72:80, :] = rolled(below, -4, 0)


def thermal_sensor_kernel(
    place, layer_class, share, lateral, vertical, sink, own, layers_in, message,
    thermal, sensed, heat, v, cond, power, planes,
):
    clear_pads(v)

    def frame(d, _):
        solver = Solver(place, (layer_class, share, lateral, vertical, sink), d, v, cond)

        def bond_tile(k, rows, t):
            if t < 2:
                theirs = message[pl.ds(pl.multiple_of(80 * (4 + t) + 8 * k, 8), 8), :]
            else:
                theirs = partner_ring(message, 2, pl.ds(pl.multiple_of(480 + 8 * k, 8), 8))
            return jnp.where(d == 0, own[2, t, rows, :], theirs)

        solver.prepare(bond_tile)

        def other_power(k, _):
            rows = pl.ds(pl.multiple_of(8 * k, 8), 8)
            column = message[pl.ds(pl.multiple_of(480 + 8 * k, 8), 8), :]
            lane = lanes()
            for t in range(2):
                at = 160 * (1 - d) + 80 * t + 8 * k
                power[t, rows, :] = message[pl.ds(pl.multiple_of(at, 8), 8), :]
            picked = jnp.where(
                d == 1,
                rolled(column, -(PART_AT[0] + DEEP), 1),
                rolled(column, -(PART_AT[1] + DEEP), 1),
            )
            power[2, rows, :] = jnp.where((lane < DEEP) | (lane >= 128 - DEEP), picked, 0.0)
            return 0

        lax.fori_loop(0, 10, other_power, 0)

        def own_power(l, t, rows, shared):
            if t not in shared:
                shared[t] = own[d, t, rows, :]
            return shared[t]

        def their_power(l, t, rows, shared):
            if t not in shared:
                shared[t] = power[t, rows, :]
            return shared[t]

        every = (0, 1, 2, 3)
        solver.first(0, every, own_power)
        solver.first(1, every, their_power)
        for b in (0, 1):
            solver.sweep(b, 0, every, own_power)
            solver.sweep(b, 1, every, their_power)

        def emit_own(l, t, k, rows, total):
            heat[d, l, t, rows, :] = total

        def emit_other(l, t, k, rows, total):
            heat[d, 3 + l, t, rows, :] = total

        solver.sweep(0, 0, every, own_power, emit_own)
        solver.sweep(0, 1, (1, 2, 3), their_power, emit_other)

        def write(k, _):
            rows = pl.ds(pl.multiple_of(8 * k, 8), 8)
            at = pl.ds(pl.multiple_of(8 * k + 8, 8), 8)
            for l in range(4):
                for t in range(2):
                    thermal[d, l, rows, 128 * t : 128 * t + 128] = heat[d, l, t, at, :]
            return 0

        lax.fori_loop(0, 8, write, 0)

        place_other(planes, layers_in, message, 0, d)
        plain = Solver(place, (layer_class, None, lateral, vertical, sink), d, v, cond)

        def own_sensor(l, t, rows, shared):
            return own[3 + 4 * d + l, t, rows, :]

        def their_sensor(l, t, rows, shared):
            return planes[l - 1, t, rows, :]

        def emit(l, t, k, rows, total):
            at = pl.ds(pl.multiple_of(8 * k - 8, 8), 8)
            sensed[d, l, at, 128 * t : 128 * t + 128] = total

        plain.partial_solve(own_sensor, their_sensor, emit)
        return 0

    lax.fori_loop(0, 2, frame, 0)


def peak_kernel(
    place, layer_class, lateral, vertical, sink, own, layers_in, message, heat,
    out, v, cond, planes,
):
    clear_pads(v)

    def frame(d, _):
        solver = Solver(place, (layer_class, None, lateral, vertical, sink), d, v, cond)

        def bond_tile(k, rows, t):
            if t < 2:
                theirs = message[pl.ds(pl.multiple_of(80 * (4 + t) + 8 * k, 8), 8), :]
            else:
                theirs = partner_ring(message, 2, pl.ds(pl.multiple_of(480 + 8 * k, 8), 8))
            return jnp.where(d == 0, own[2, t, rows, :], theirs)

        solver.prepare(bond_tile)
        place_other(planes, layers_in, message, 1, d)

        def own_peak(l, t, rows, shared):
            return own[11 + 4 * d + l, t, rows, :] * heat[d, l, t, rows, :]

        def their_peak(l, t, rows, shared):
            return planes[l - 1, t, rows, :] * heat[d, 3 + l, t, rows, :]

        def emit(l, t, k, rows, total):
            at = pl.ds(pl.multiple_of(8 * k - 8, 8), 8)
            out[d, l, at, 128 * t : 128 * t + 128] = total

        solver.partial_solve(own_peak, their_peak, emit)
        return 0

    lax.fori_loop(0, 2, frame, 0)


def call(kernel, tables, arrays, outs, scratch=(), flops=0, name=None):
    shapes = [jax.ShapeDtypeStruct(shape, F32) for shape in outs]
    return pl.pallas_call(
        kernel,
        out_shape=shapes,
        in_specs=[SMEM] * len(tables) + [VMEM] * len(arrays),
        out_specs=[VMEM] * len(shapes),
        scratch_shapes=[pltpu.VMEM(shape, F32) for shape in scratch],
        compiler_params=pltpu.CompilerParams(vmem_limit_bytes=48 << 20),
        cost_estimate=pl.CostEstimate(flops=flops, bytes_accessed=4 << 20, transcendentals=0),
        name=name,
    )(*tables, *arrays)


def pairs(count, odd):
    if odd:
        return [(i, ((i - 1) ^ 1) + 1) for i in range(1, count - 1)]
    return [(i, i ^ 1) for i in range(count)]


def local(
    block_ids,
    block_power,
    layer_class,
    power_share,
    lateral_k,
    vertical_k,
    sink_conductance,
    bond_conductance,
    peak_factors,
    sensor_weight,
):
    nx, ny = lax.axis_size("gx"), lax.axis_size("gy")
    facing = [(i, nx - 1 - i) for i in range(nx)]
    place = jnp.stack([lax.axis_index("gx"), lax.axis_index("gy")]).astype(jnp.int32)
    layers = (2, 3, 2, 64, 128)

    (sensor_out,) = call(flip_layers_kernel, (), (sensor_weight,), [layers], name="flip_sensor")
    sensor_in = lax.ppermute(sensor_out, "gx", facing)

    power, col_a, col_b = call(
        column_kernel,
        (place, block_power),
        (block_ids, bond_conductance, sensor_weight, peak_factors),
        [(2, 2, 64, 128), (64, 128), (64, 128)],
        name="columns",
    )
    (peak_out,) = call(flip_layers_kernel, (), (peak_factors,), [layers], name="flip_peak")
    col_a = lax.ppermute(col_a, "gy", pairs(ny, False))
    col_b = lax.ppermute(col_b, "gy", pairs(ny, True))
    fields = (power, bond_conductance, sensor_weight, peak_factors)
    row_a, row_b = call(
        row_kernel, (place,), fields + (col_a, col_b), [(264, 128), (264, 128)], name="rows"
    )
    row_a = lax.ppermute(row_a, "gx", pairs(nx, False))
    row_b = lax.ppermute(row_b, "gx", pairs(nx, True))
    own, message = call(
        build_kernel,
        (place,),
        fields + (col_a, col_b, row_a, row_b),
        [(19, 3, ROWS, 128), (688, 128)],
        name="build",
    )
    message = lax.ppermute(message, "gx", facing)
    peak_in = lax.ppermute(peak_out, "gx", facing)
    planes = (3, 3, ROWS, 128)
    v = (2, 2, 4, 3, ROWS + 16, 128)
    thermal, sensed, heat = call(
        thermal_sensor_kernel,
        (place, layer_class, power_share, lateral_k, vertical_k, sink_conductance),
        (own, sensor_in, message),
        [(2, 4, 64, 256), (2, 4, 64, 256), (2, 7, 3, ROWS, 128)],
        [v, planes, (3, ROWS, 128), planes],
        name="thermal_sensor",
    )
    (peak,) = call(
        peak_kernel,
        (place, layer_class, lateral_k, vertical_k, sink_conductance),
        (own, peak_in, message, heat),
        [(2, 4, 64, 256)],
        [v, planes, planes],
        name="peak",
    )
    return thermal, peak, sensed


def solution(mesh):
    return jax.shard_map(
        local,
        mesh=mesh,
        in_specs=(
            P(None, "gx", "gy"),
            P(),
            P(),
            P(),
            P(),
            P(),
            P(),
            P("gx", "gy"),
            P(None, None, "gx", "gy"),
            P(None, None, "gx", "gy"),
        ),
        out_specs=(P(None, None, "gx", "gy"),) * 3,
        check_vma=False,
    )
```

time: 376 us -> 98.4 us (0.26); the launches traced: 370 us -> 96.9 us
  starting transfers between devices: 175 us -> 19.2 us
  waiting for transfers between devices: 165 us -> 21.9 us
  Pallas kernels: 0 us -> 47.6 us
  other arithmetic: 15.5 us -> 0.08 us
  local copies, waits for them, and re-layouts: 13.1 us -> 7.43 us
    ppermute x48 -> x7, starting transfers between devices: 175 us -> 19.2 us  [the longest x1 5.76 us: local(): col_b = lax.ppermute(col_b, 'gy', pairs(ny, True))]
    ppermute x48 -> x7, waiting for transfers between devices: 165 us -> 21.9 us  [the longest x1 14.6 us: local(): message = lax.ppermute(message, 'gx', facing)]
    pallas_call x0 -> x7, Pallas kernels: none -> 47.6 us  [call(): pl.pallas_call(kernel, out_shape=shapes, in_specs=[SMEM] * len(tables) +...]
    div x11 -> x0, other arithmetic: 8.63 us -> none  [pointwise_iterative_update(): (source + neighbours(values, conductance_tuple, joined_counterpart)) / ma...]
    slice x37 -> x0, local copies, waits for them, and re-layouts: 7.81 us -> none  [the longest x2 2.4 us: local(): peak_heat_derivative = jnp.stack([peak_heat_factors_flipped[0], moved[1]])]
    unnamed x34 -> x30, local copies, waits for them, and re-layouts: 1.1 us -> 7.43 us
  transfers between devices with their start and end apart: 48 -> 7, of which waited for: 25 -> 4; matrix products, arithmetic and copies ran while one was open for 3% -> 0% of each run, Pallas kernels for 0% -> 32%
where the time goes in v1:
time: 98.4 us; the launch traced here: 96.9 us
  Pallas kernels  47.6 us (48%)
  waiting for transfers between devices  21.9 us (22%)
  starting transfers between devices  19.2 us (20%)
  local copies, waits for them, and re-layouts  7.43 us (8%)
    pallas_call x7, Pallas kernels, call(): pl.pallas_call(kernel, out_shape=shapes, in_specs=[SMEM] * len(tables) +...  47.6 us
    ppermute x1, waiting for transfers between devices, local(): message = lax.ppermute(message, 'gx', facing)  14.6 us
    unnamed x30, local copies, waits for them, and re-layouts  7.43 us
    ppermute x1, starting transfers between devices, local(): col_b = lax.ppermute(col_b, 'gy', pairs(ny, True))  5.76 us
    ppermute x1, waiting for transfers between devices, local(): sensor_in = lax.ppermute(sensor_out, 'gx', facing)  4.36 us
    ppermute x1, starting transfers between devices, local(): row_b = lax.ppermute(row_b, 'gx', pairs(nx, True))  4.01 us
    ppermute x1, starting transfers between devices, local(): sensor_in = lax.ppermute(sensor_out, 'gx', facing)  3.33 us
    ppermute x1, starting transfers between devices, local(): peak_in = lax.ppermute(peak_out, 'gx', facing)  2.2 us
  transfers between devices with their start and end apart: 7, of which 4 were waited for; matrix products, arithmetic and copies ran while one was open for 0% of the time, Pallas kernels for 32%

profile of v1, /device:TPU:111, one launch (start us, length us, event | category | flops | bytes accessed | tf_op | source)
XLA Modules:
  0.0 96.9 jit_solution(11043529326561062131)
XLA Ops:
  0.6 0.1 pad_add_fusion.place
  0.7 0.0 copy-start
  0.7 1.0 %copy-done = f32[2,4,64,256]{3,2,1,0:T(8,128)S(1)} copy-done((f32[2,4,64,256]{3,2,1,0:T(8,128)S(1)}, f32[2,4,64,256]{3,2,1,0:T(8,128)}, u32[]{:S(2)}) %copy-start) | copy-done | bytes 524312
  1.8 0.0 copy-start.3
  1.8 1.0 %copy-done.3 = f32[2,4,64,256]{3,2,1,0:T(8,128)S(1)} copy-done((f32[2,4,64,256]{3,2,1,0:T(8,128)S(1)}, f32[2,4,64,256]{3,2,1,0:T(8,128)}, u32[]{:S(2)}) %copy-start.3) | copy-done | bytes 524312
  2.8 0.0 copy-start.6
  2.8 0.8 copy-done.6
  3.6 0.0 copy-start.8
  3.6 0.9 copy-done.8
  4.5 0.0 copy-start.13
  4.5 0.7 copy-done.13
  5.2 0.0 copy-start.2
  5.2 1.7 %columns.1 = (f32[2,2,64,128]{3,2,1,0:T(8,128)S(1)}, f32[64,128]{1,0:T(8,128)S(1)}, f32[64,128]{1,0:T(8,128)S(1)}) custom-call(s32[2]{0:T(128)S(1)} %pad_add_fusion.place, f32[32]{0:T(128)S(1)} %copy-done.13, s32[2,64,256]{2,1,0:T(8,128)S(1)} %copy-done.8, f32[64,256]{1,0:T(8,128)S(1)} %copy-done.6, f32[2,4,64,256]{3,2,1,0:T(8,128)S(1)} %copy-done, ...), custom_call_target="tpu_custom_call" | custom-call | bytes 4194304 | tf_op jit(solution)/shard_map/columns/pallas_call | solution.py:535
  6.9 0.3 collective-permute-start
  7.2 5.8 %collective-permute-start.1 = (f32[64,128]{1,0:T(8,128)S(1)}, f32[64,128]{1,0:T(8,128)S(1)}, u32[]{:S(2)}, u32[]{:S(2)}) collective-permute-start(f32[64,128]{1,0:T(8,128)S(1)} %get-tuple-element.15), channel_id=1, source_target_pairs={{1,2},{2,1},{3,4},{4,3},{5,6},{6,5},{7,8},{8,7},{9,10},{10,9},{11,... | collective-permute-start | bytes 98312 | tf_op jit(solution)/shard_map/ppermute | solution.py:582
  12.9 0.0 collective-permute-done.col_a
  12.9 1.3 %collective-permute-done.1.col_b = f32[64,128]{1,0:T(8,128)S(1)} collective-permute-done((f32[64,128]{1,0:T(8,128)S(1)}, f32[64,128]{1,0:T(8,128)S(1)}, u32[]{:S(2)}, u32[]{:S(2)}) %collective-permute-start.1) | collective-permute-done | bytes 32800 | tf_op jit(solution)/shard_map/ppermute | solution.py:582
  14.2 0.0 copy-start.1
  14.2 1.0 %copy-done.1 = f32[2,4,64,256]{3,2,1,0:T(8,128)S(1)} copy-done((f32[2,4,64,256]{3,2,1,0:T(8,128)S(1)}, f32[2,4,64,256]{3,2,1,0:T(8,128)}, u32[]{:S(2)}) %copy-start.1) | copy-done | bytes 524312
  15.3 0.0 copy-start.4
  15.3 1.0 %copy-done.4 = f32[2,4,64,256]{3,2,1,0:T(8,128)S(1)} copy-done((f32[2,4,64,256]{3,2,1,0:T(8,128)S(1)}, f32[2,4,64,256]{3,2,1,0:T(8,128)}, u32[]{:S(2)}) %copy-start.4) | copy-done | bytes 524312
  16.3 0.0 copy-start.7
  16.3 0.8 copy-done.7
  17.1 0.0 copy-start.9
  17.2 0.0 copy-start.14
  17.2 0.7 rows.1
  17.9 1.9 %collective-permute-start.2 = (f32[264,128]{1,0:T(8,128)S(1)}, f32[264,128]{1,0:T(8,128)S(1)}, u32[]{:S(2)}, u32[]{:S(2)}) collective-permute-start(f32[264,128]{1,0:T(8,128)S(1)} %get-tuple-element.16), channel_id=1, source_target_pairs={{0,16},{16,0},{32,48},{48,32},{64,80},{80,64},{96,112},{112,96},{1... | collective-permute-start | bytes 405512 | tf_op jit(solution)/shard_map/ppermute | solution.py:587
  19.8 4.0 %collective-permute-start.3 = (f32[264,128]{1,0:T(8,128)S(1)}, f32[264,128]{1,0:T(8,128)S(1)}, u32[]{:S(2)}, u32[]{:S(2)}) collective-permute-start(f32[264,128]{1,0:T(8,128)S(1)} %get-tuple-element.17), channel_id=1, source_target_pairs={{16,32},{32,16},{48,64},{64,48},{80,96},{96,80},{112,128},{128,112... | collective-permute-start | bytes 405512 | tf_op jit(solution)/shard_map/ppermute | solution.py:588
  23.8 0.0 copy-done.2
  23.8 0.1 flip_sensor.1
  23.9 3.3 %collective-permute-start.4 = (f32[2,3,2,64,128]{4,3,2,1,0:T(8,128)S(1)}, f32[2,3,2,64,128]{4,3,2,1,0:T(8,128)S(1)}, u32[]{:S(2)}, u32[]{:S(2)}) collective-permute-start(f32[2,3,2,64,128]{4,3,2,1,0:T(8,128)S(1)} %flip_sensor.1), channel_id=1, source_target_pairs={{0,240},{16,224},{32,208},{48,192},{64,176},{80,160},{96,144},{112... | collective-permute-start | bytes 1179656 | tf_op jit(solution)/shard_map/ppermute | solution.py:571
  27.2 0.0 copy-done.5
  27.2 0.1 flip_peak.1
  27.3 2.2 %collective-permute-start.6 = (f32[2,3,2,64,128]{4,3,2,1,0:T(8,128)S(1)}, f32[2,3,2,64,128]{4,3,2,1,0:T(8,128)S(1)}, u32[]{:S(2)}, u32[]{:S(2)}) collective-permute-start(f32[2,3,2,64,128]{4,3,2,1,0:T(8,128)S(1)} %flip_peak.1), channel_id=1, source_target_pairs={{0,240},{16,224},{32,208},{48,192},{64,176},{80,160},{96,144},{112... | collective-permute-start | bytes 1179656 | tf_op jit(solution)/shard_map/ppermute | solution.py:597
  29.5 0.0 collective-permute-done.2.row_a
  29.5 1.6 %collective-permute-done.3.row_b = f32[264,128]{1,0:T(8,128)S(1)} collective-permute-done((f32[264,128]{1,0:T(8,128)S(1)}, f32[264,128]{1,0:T(8,128)S(1)}, u32[]{:S(2)}, u32[]{:S(2)}) %collective-permute-start.3) | collective-permute-done | bytes 135200 | tf_op jit(solution)/shard_map/ppermute | solution.py:588
  31.1 2.4 %build.1 = (f32[19,3,80,128]{3,2,1,0:T(8,128)S(1)}, f32[688,128]{1,0:T(8,128)S(1)}) custom-call(s32[2]{0:T(128)S(1)} %pad_add_fusion.place, f32[2,2,64,128]{3,2,1,0:T(8,128)S(1)} %get-tuple-element.13.power, f32[64,256]{1,0:T(8,128)S(1)} %copy-done.7, f32[2,4,64,256]{3,2,1,0:T(8,128)S(1)} %copy-done.2, f32[2,4,64,256]{3,2,1,0:T(8,128)S(1)} %copy-done.5, ...), custom_call_target="tpu_custom_call" | custom-call | bytes 4194304 | tf_op jit(solution)/shard_map/build/pallas_call | solution.py:535
  33.5 1.7 %collective-permute-start.5 = (f32[688,128]{1,0:T(8,128)S(1)}, f32[688,128]{1,0:T(8,128)S(1)}, u32[]{:S(2)}, u32[]{:S(2)}) collective-permute-start(f32[688,128]{1,0:T(8,128)S(1)} %get-tuple-element.19), channel_id=1, source_target_pairs={{0,240},{16,224},{32,208},{48,192},{64,176},{80,160},{96,144},{112... | collective-permute-start | bytes 1056776 | tf_op jit(solution)/shard_map/ppermute | solution.py:596
  35.2 4.4 %collective-permute-done.4.layers_in = f32[2,3,2,64,128]{4,3,2,1,0:T(8,128)S(1)} collective-permute-done((f32[2,3,2,64,128]{4,3,2,1,0:T(8,128)S(1)}, f32[2,3,2,64,128]{4,3,2,1,0:T(8,128)S(1)}, u32[]{:S(2)}, u32[]{:S(2)}) %collective-permute-start.4) | collective-permute-done | bytes 393248 | tf_op jit(solution)/shard_map/ppermute | solution.py:571
  39.5 14.6 %collective-permute-done.5.message = f32[688,128]{1,0:T(8,128)S(1)} collective-permute-done((f32[688,128]{1,0:T(8,128)S(1)}, f32[688,128]{1,0:T(8,128)S(1)}, u32[]{:S(2)}, u32[]{:S(2)}) %collective-permute-start.5) | collective-permute-done | bytes 352288 | tf_op jit(solution)/shard_map/ppermute | solution.py:596
  54.1 0.0 copy-done.9
  54.1 0.0 copy-done.10
  54.1 0.0 copy-done.11
  54.1 0.0 copy-done.12
  54.1 0.0 copy-done.14
  54.1 28.4 %thermal_sensor.1 = (f32[2,4,64,256]{3,2,1,0:T(8,128)}, f32[2,4,64,256]{3,2,1,0:T(8,128)}, f32[2,7,3,80,128]{4,3,2,1,0:T(8,128)S(1)}) custom-call(s32[2]{0:T(128)S(1)} %pad_add_fusion.place, s32[2,4]{1,0:T(2,128)S(1)} %copy-done.9, f32[4]{0:T(128)S(1)} %copy-done.14, f32[4]{0:T(128)S(1)} %copy-done.10, f32[4]{0:T(128)S(1)} %copy-done.11, f32[2]{0:T(128)S(1)} %copy-done.12, ...), custom_call_target="tpu_custom_call" | custom-call | bytes 4194304 | tf_op jit(solution)/shard_map/thermal_sensor/pallas_call | solution.py:535
  82.6 0.0 collective-permute-done.6.layers_in
  82.6 14.3 %peak.7 = f32[2,4,64,256]{3,2,1,0:T(8,128)} custom-call(s32[2]{0:T(128)S(1)} %pad_add_fusion.place, s32[2,4]{1,0:T(2,128)S(1)} %copy-done.9, f32[4]{0:T(128)S(1)} %copy-done.10, f32[4]{0:T(128)S(1)} %copy-done.11, f32[2]{0:T(128)S(1)} %copy-done.12, f32[19,3,80,128]{3,2,1,0:T(8,128)S(1)} %get-tuple-element.18.own, ...), custom_call_target="tpu_custom_call" | custom-call | bytes 4194304 | tf_op jit(solution)/shard_map/peak/pallas_call | solution.py:535
  (4 shorter events, 0.0 us)
Async XLA Ops:
  0.7 1.0 %copy-start = (f32[2,4,64,256]{3,2,1,0:T(8,128)S(1)}, f32[2,4,64,256]{3,2,1,0:T(8,128)}, u32[]{:S(2)}) copy-start(f32[2,4,64,256]{3,2,1,0:T(8,128)} %field.2) | copy-start | bytes 1572868
  1.8 1.0 %copy-start.3 = (f32[2,4,64,256]{3,2,1,0:T(8,128)S(1)}, f32[2,4,64,256]{3,2,1,0:T(8,128)}, u32[]{:S(2)}) copy-start(f32[2,4,64,256]{3,2,1,0:T(8,128)} %field.3) | copy-start | bytes 1572868
  2.8 0.8 copy-start.6
  3.6 0.9 copy-start.8
  4.5 0.7 copy-start.13
  5.2 18.6 %copy-start.2 = (f32[2,4,64,256]{3,2,1,0:T(8,128)S(1)}, f32[2,4,64,256]{3,2,1,0:T(8,128)}, u32[]{:S(2)}) copy-start(f32[2,4,64,256]{3,2,1,0:T(8,128)} %field.2) | copy-start | bytes 1572868
  5.2 22.0 %copy-start.5 = (f32[2,4,64,256]{3,2,1,0:T(8,128)S(1)}, f32[2,4,64,256]{3,2,1,0:T(8,128)}, u32[]{:S(2)}) copy-start(f32[2,4,64,256]{3,2,1,0:T(8,128)} %field.3) | copy-start | bytes 1572868
  6.9 6.0 %collective-permute-start = (f32[64,128]{1,0:T(8,128)S(1)}, f32[64,128]{1,0:T(8,128)S(1)}, u32[]{:S(2)}, u32[]{:S(2)}) collective-permute-start(f32[64,128]{1,0:T(8,128)S(1)} %get-tuple-element.14), channel_id=1, source_target_pairs={{0,1},{1,0},{2,3},{3,2},{4,5},{5,4},{6,7},{7,6},{8,9},{9,8},{10,11... | collective-permute-start | bytes 98312 | tf_op jit(solution)/shard_map/ppermute | solution.py:581
  7.2 7.1 %collective-permute-start.1 = (f32[64,128]{1,0:T(8,128)S(1)}, f32[64,128]{1,0:T(8,128)S(1)}, u32[]{:S(2)}, u32[]{:S(2)}) collective-permute-start(f32[64,128]{1,0:T(8,128)S(1)} %get-tuple-element.15), channel_id=1, source_target_pairs={{1,2},{2,1},{3,4},{4,3},{5,6},{6,5},{7,8},{8,7},{9,10},{10,9},{11,... | collective-permute-start | bytes 98312 | tf_op jit(solution)/shard_map/ppermute | solution.py:582
  14.2 1.0 %copy-start.1 = (f32[2,4,64,256]{3,2,1,0:T(8,128)S(1)}, f32[2,4,64,256]{3,2,1,0:T(8,128)}, u32[]{:S(2)}) copy-start(f32[2,4,64,256]{3,2,1,0:T(8,128)} %field.2) | copy-start | bytes 1572868
  15.3 1.0 %copy-start.4 = (f32[2,4,64,256]{3,2,1,0:T(8,128)S(1)}, f32[2,4,64,256]{3,2,1,0:T(8,128)}, u32[]{:S(2)}) copy-start(f32[2,4,64,256]{3,2,1,0:T(8,128)} %field.3) | copy-start | bytes 1572868
  16.3 0.8 copy-start.7
  17.1 37.0 %copy-start.9 = (s32[2,4]{1,0:T(2,128)S(1)}, s32[2,4]{1,0:T(2,128)}, u32[]{:S(2)}) copy-start(s32[2,4]{1,0:T(2,128)} %layer_class.3) | copy-start | bytes 100
  17.2 37.0 %copy-start.10 = (f32[4]{0:T(128)S(1)}, f32[4]{0:T(128)}, u32[]{:S(2)}) copy-start(f32[4]{0:T(128)} %lateral.3) | copy-start | bytes 52
  17.2 37.0 %copy-start.11 = (f32[4]{0:T(128)S(1)}, f32[4]{0:T(128)}, u32[]{:S(2)}) copy-start(f32[4]{0:T(128)} %vertical.3) | copy-start | bytes 52
  17.2 37.0 %copy-start.12 = (f32[2]{0:T(128)S(1)}, f32[2]{0:T(128)}, u32[]{:S(2)}) copy-start(f32[2]{0:T(128)} %sink.3) | copy-start | bytes 28
  17.2 37.0 %copy-start.14 = (f32[4]{0:T(128)S(1)}, f32[4]{0:T(128)}, u32[]{:S(2)}) copy-start(f32[4]{0:T(128)} %share.1) | copy-start | bytes 52
  17.9 11.6 %collective-permute-start.2 = (f32[264,128]{1,0:T(8,128)S(1)}, f32[264,128]{1,0:T(8,128)S(1)}, u32[]{:S(2)}, u32[]{:S(2)}) collective-permute-start(f32[264,128]{1,0:T(8,128)S(1)} %get-tuple-element.16), channel_id=1, source_target_pairs={{0,16},{16,0},{32,48},{48,32},{64,80},{80,64},{96,112},{112,96},{1... | collective-permute-start | bytes 405512 | tf_op jit(solution)/shard_map/ppermute | solution.py:587
  19.8 11.3 %collective-permute-start.3 = (f32[264,128]{1,0:T(8,128)S(1)}, f32[264,128]{1,0:T(8,128)S(1)}, u32[]{:S(2)}, u32[]{:S(2)}) collective-permute-start(f32[264,128]{1,0:T(8,128)S(1)} %get-tuple-element.17), channel_id=1, source_target_pairs={{16,32},{32,16},{48,64},{64,48},{80,96},{96,80},{112,128},{128,112... | collective-permute-start | bytes 405512 | tf_op jit(solution)/shard_map/ppermute | solution.py:588
  23.9 15.7 %collective-permute-start.4 = (f32[2,3,2,64,128]{4,3,2,1,0:T(8,128)S(1)}, f32[2,3,2,64,128]{4,3,2,1,0:T(8,128)S(1)}, u32[]{:S(2)}, u32[]{:S(2)}) collective-permute-start(f32[2,3,2,64,128]{4,3,2,1,0:T(8,128)S(1)} %flip_sensor.1), channel_id=1, source_target_pairs={{0,240},{16,224},{32,208},{48,192},{64,176},{80,160},{96,144},{112... | collective-permute-start | bytes 1179656 | tf_op jit(solution)/shard_map/ppermute | solution.py:571
  27.3 55.3 %collective-permute-start.6 = (f32[2,3,2,64,128]{4,3,2,1,0:T(8,128)S(1)}, f32[2,3,2,64,128]{4,3,2,1,0:T(8,128)S(1)}, u32[]{:S(2)}, u32[]{:S(2)}) collective-permute-start(f32[2,3,2,64,128]{4,3,2,1,0:T(8,128)S(1)} %flip_peak.1), channel_id=1, source_target_pairs={{0,240},{16,224},{32,208},{48,192},{64,176},{80,160},{96,144},{112... | collective-permute-start | bytes 1179656 | tf_op jit(solution)/shard_map/ppermute | solution.py:597
  33.5 20.6 %collective-permute-start.5 = (f32[688,128]{1,0:T(8,128)S(1)}, f32[688,128]{1,0:T(8,128)S(1)}, u32[]{:S(2)}, u32[]{:S(2)}) collective-permute-start(f32[688,128]{1,0:T(8,128)S(1)} %get-tuple-element.19), channel_id=1, source_target_pairs={{0,240},{16,224},{32,208},{48,192},{64,176},{80,160},{96,144},{112... | collective-permute-start | bytes 1056776 | tf_op jit(solution)/shard_map/ppermute | solution.py:596

commit v2 on v1

--- a/solution.py
+++ b/solution.py
@@ -70,6 +70,16 @@
                 for k in range(8):
                     out[d, l, t, 8 * (7 - k) : 8 * (8 - k), :] = mirrored(
                         field[d, l + 1, 8 * k : 8 * k + 8, 128 * t : 128 * t + 128]
+                    )
+
+
+def flip_own_kernel(own, out):
+    for d in range(2):
+        for l in range(3):
+            for t in range(2):
+                for k in range(8):
+                    out[d, l, t, 8 * (7 - k) : 8 * (8 - k), :] = mirrored(
+                        own[12 + 4 * d + l, t, 8 * k + 8 : 8 * k + 16, :]
                     )
 
 
@@ -300,61 +310,66 @@
 
         lax.fori_loop(0, 10, body, 0)
 
-    def sweep(self, b, side, layers, source, emit=None, core_only=False):
+    def sweep(self, b, work, core_only=False, unroll=2):
         v = self.v
 
-        def body(k, _):
+        def one(k, stores):
             rows = pl.ds(pl.multiple_of(8 * k, 8), 8)
             to = pl.ds(pl.multiple_of(8 * k + 8, 8), 8)
             row, ring = self.masks(k)
             lane = lanes()
-            shared = {}
-            for l in layers:
-                coef = self.coef[side][l]
-                centre = [v[b, side, l, t, to, :] for t in range(3)]
-                forward = [pltpu.roll(c, 1, 1) for c in centre]
-                backward = [pltpu.roll(c, 127, 1) for c in centre]
-                for t in range(2 if core_only else 3):
-                    left = jnp.where(lane == 0, forward[t - 1], forward[t])
-                    right = jnp.where(lane == 127, backward[(t + 1) % 3], backward[t])
-                    lateral = (left + right) + (
-                        v[b, side, l, t, pl.ds(8 * k + 7, 8), :]
-                        + v[b, side, l, t, pl.ds(8 * k + 9, 8), :]
-                    )
-                    s = source(l, t, rows, shared)
-                    if l < 3:
-                        total = s * coef[0] + coef[1] * lateral
-                        total = total + coef[2] * v[b, side, l + 1, t, to, :]
-                        if l > 0:
-                            total = total + coef[3] * v[b, side, l - 1, t, to, :]
-                    else:
-                        if coef[3] is not None:
-                            s = s * coef[3]
-                        total = s + coef[1] * lateral
-                        total = total + coef[2] * v[b, side, 2, t, to, :]
-                        total = total + self.cond[0, t, rows, :] * v[b, 1 - side, 3, t, to, :]
-                        total = total * self.cond[1 + side, t, rows, :]
-                    if not core_only:
-                        total = total * (ring if t == 2 else row)
-                    if emit is None:
-                        v[1 - b, side, l, t, to, :] = total
-                    else:
-                        emit(l, t, k, rows, total)
+            first_lane, last_lane = lane == 0, lane == 127
+            for side, layers, source, emit in work:
+                shared = {}
+                for l in layers:
+                    coef = self.coef[side][l]
+                    centre = [v[b, side, l, t, to, :] for t in range(3)]
+                    forward = [pltpu.roll(c, 1, 1) for c in centre]
+                    backward = [pltpu.roll(c, 127, 1) for c in centre]
+                    for t in range(2 if core_only else 3):
+                        left = jnp.where(first_lane, forward[t - 1], forward[t])
+                        right = jnp.where(last_lane, backward[(t + 1) % 3], backward[t])
+                        lateral = (left + right) + (
+                            v[b, side, l, t, pl.ds(8 * k + 7, 8), :]
+                            + v[b, side, l, t, pl.ds(8 * k + 9, 8), :]
+                        )
+                        s = source(l, t, rows, shared)
+                        if l < 3:
+                            total = s * coef[0] + coef[1] * lateral
+                            total = total + coef[2] * v[b, side, l + 1, t, to, :]
+                            if l > 0:
+                                total = total + coef[3] * v[b, side, l - 1, t, to, :]
+                        else:
+                            if coef[3] is not None:
+                                s = s * coef[3]
+                            total = s + coef[1] * lateral
+                            total = total + coef[2] * v[b, side, 2, t, to, :]
+                            total = total + self.cond[0, t, rows, :] * v[b, 1 - side, 3, t, to, :]
+                            total = total * self.cond[1 + side, t, rows, :]
+                        if not core_only:
+                            total = total * (ring if t == 2 else row)
+                        stores.append((emit, side, l, t, k, rows, to, total))
+
+        def body(j, _):
+            stores = []
+            for u in range(unroll):
+                one(j * unroll + u + (1 if core_only else 0), stores)
+            for emit, side, l, t, k, rows, to, total in stores:
+                if emit is None:
+                    v[1 - b, side, l, t, to, :] = total
+                else:
+                    emit(l, t, k, rows, total)
             return 0
 
-        if core_only:
-            lax.fori_loop(1, 9, body, 0)
-        else:
-            lax.fori_loop(0, 10, body, 0)
+        lax.fori_loop(0, (8 if core_only else 10) // unroll, body, 0)
 
     def partial_solve(self, own_source, other_source, emit):
         self.first(0, (0, 1, 2, 3), own_source)
         self.first(1, (1, 2, 3), other_source)
-        self.sweep(0, 0, (0, 1, 2, 3), own_source)
-        self.sweep(0, 1, (2, 3), other_source)
-        self.sweep(1, 0, (0, 1, 2, 3), own_source)
-        self.sweep(1, 1, (3,), other_source)
-        self.sweep(0, 0, (0, 1, 2, 3), own_source, emit, core_only=True)
+        every = (0, 1, 2, 3)
+        self.sweep(0, [(0, every, own_source, None), (1, (2, 3), other_source, None)])
+        self.sweep(1, [(0, every, own_source, None), (1, (3,), other_source, None)])
+        self.sweep(0, [(0, every, own_source, emit)], core_only=True)
 
 
 def clear_pads(v):
@@ -454,8 +469,7 @@
         solver.first(0, every, own_power)
         solver.first(1, every, their_power)
         for b in (0, 1):
-            solver.sweep(b, 0, every, own_power)
-            solver.sweep(b, 1, every, their_power)
+            solver.sweep(b, [(0, every, own_power, None), (1, every, their_power, None)])
 
         def emit_own(l, t, k, rows, total):
             heat[d, l, t, rows, :] = total
@@ -463,8 +477,7 @@
         def emit_other(l, t, k, rows, total):
             heat[d, 3 + l, t, rows, :] = total
 
-        solver.sweep(0, 0, every, own_power, emit_own)
-        solver.sweep(0, 1, (1, 2, 3), their_power, emit_other)
+        solver.sweep(0, [(0, every, own_power, emit_own), (1, (1, 2, 3), their_power, emit_other)])
 
         def write(k, _):
             rows = pl.ds(pl.multiple_of(8 * k, 8), 8)
@@ -530,7 +543,7 @@
     lax.fori_loop(0, 2, frame, 0)
 
 
-def call(kernel, tables, arrays, outs, scratch=(), flops=0, name=None):
+def call(kernel, tables, arrays, outs, scratch=(), flops=0, cost=1024, name=None):
     shapes = [jax.ShapeDtypeStruct(shape, F32) for shape in outs]
     return pl.pallas_call(
         kernel,
@@ -538,8 +551,8 @@
         in_specs=[SMEM] * len(tables) + [VMEM] * len(arrays),
         out_specs=[VMEM] * len(shapes),
         scratch_shapes=[pltpu.VMEM(shape, F32) for shape in scratch],
-        compiler_params=pltpu.CompilerParams(vmem_limit_bytes=48 << 20),
-        cost_estimate=pl.CostEstimate(flops=flops, bytes_accessed=4 << 20, transcendentals=0),
+        compiler_params=pltpu.CompilerParams(vmem_limit_bytes=16 << 20),
+        cost_estimate=pl.CostEstimate(flops=flops, bytes_accessed=cost, transcendentals=0),
         name=name,
     )(*tables, *arrays)
 
@@ -577,7 +590,6 @@
         [(2, 2, 64, 128), (64, 128), (64, 128)],
         name="columns",
     )
-    (peak_out,) = call(flip_layers_kernel, (), (peak_factors,), [layers], name="flip_peak")
     col_a = lax.ppermute(col_a, "gy", pairs(ny, False))
     col_b = lax.ppermute(col_b, "gy", pairs(ny, True))
     fields = (power, bond_conductance, sensor_weight, peak_factors)
@@ -586,6 +598,7 @@
     )
     row_a = lax.ppermute(row_a, "gx", pairs(nx, False))
     row_b = lax.ppermute(row_b, "gx", pairs(nx, True))
+    row_a, row_b, sensor_in = lax.optimization_barrier((row_a, row_b, sensor_in))
     own, message = call(
         build_kernel,
         (place,),
@@ -594,6 +607,7 @@
         name="build",
     )
     message = lax.ppermute(message, "gx", facing)
+    (peak_out,) = call(flip_own_kernel, (), (own,), [layers], flops=10**11, cost=64 << 20, name="flip_peak")
     peak_in = lax.ppermute(peak_out, "gx", facing)
     planes = (3, 3, ROWS, 128)
     v = (2, 2, 4, 3, ROWS + 16, 128)
@@ -603,6 +617,7 @@
         (own, sensor_in, message),
         [(2, 4, 64, 256), (2, 4, 64, 256), (2, 7, 3, ROWS, 128)],
         [v, planes, (3, ROWS, 128), planes],
+        cost=64 << 20, flops=10**11,
         name="thermal_sensor",
     )
     (peak,) = call(

time: 98.4 us -> 76 us (0.77)
  Pallas kernels: 47.6 us -> 30.9 us
  waiting for transfers between devices: 21.9 us -> 16.4 us
    pallas_call x7, Pallas kernels: 47.6 us -> 30.9 us  [call(): pl.pallas_call(kernel, out_shape=shapes, in_specs=[SMEM] * len(tables) +...]
    ppermute x1, waiting for transfers between devices: 14.6 us -> 8.72 us  [local(): message = lax.ppermute(message, 'gx', facing)]
    ppermute x1, waiting for transfers between devices: 4.36 us -> 0.01 us  [local(): sensor_in = lax.ppermute(sensor_out, 'gx', facing)]
    ppermute x1, waiting for transfers between devices: 1.64 us -> 5.78 us  [local(): row_b = lax.ppermute(row_b, 'gx', pairs(nx, True))]
    ppermute x1, waiting for transfers between devices: 0.01 us -> 1.28 us  [local(): col_a = lax.ppermute(col_a, 'gy', pairs(ny, False))]
    ppermute x1, starting transfers between devices: 2.2 us -> 3.21 us  [local(): peak_in = lax.ppermute(peak_out, 'gx', facing)]
    unnamed x30 -> x28, local copies, waits for them, and re-layouts: 7.43 us -> 7.42 us
  transfers between devices with their start and end apart: 7 -> 7, of which waited for: 4 -> 4; matrix products, arithmetic and copies ran while one was open for 0% -> 0% of each run, Pallas kernels for 32% -> 25%
where the time goes in v2:
time: 76 us; the launch traced here: 75.1 us
  Pallas kernels  30.9 us (41%)
  starting transfers between devices  19.6 us (26%)
  waiting for transfers between devices  16.4 us (22%)
  local copies, waits for them, and re-layouts  7.42 us (10%)
    pallas_call x7, Pallas kernels, call(): pl.pallas_call(kernel, out_shape=shapes, in_specs=[SMEM] * len(tables) +...  30.9 us
    ppermute x1, waiting for transfers between devices, local(): message = lax.ppermute(message, 'gx', facing)  8.72 us
    unnamed x28, local copies, waits for them, and re-layouts  7.42 us
    ppermute x1, waiting for transfers between devices, local(): row_b = lax.ppermute(row_b, 'gx', pairs(nx, True))  5.78 us
    ppermute x1, starting transfers between devices, local(): col_b = lax.ppermute(col_b, 'gy', pairs(ny, True))  4.89 us
    ppermute x1, starting transfers between devices, local(): row_b = lax.ppermute(row_b, 'gx', pairs(nx, True))  4.13 us
    ppermute x1, starting transfers between devices, local(): peak_in = lax.ppermute(peak_out, 'gx', facing)  3.21 us
    ppermute x1, starting transfers between devices, local(): sensor_in = lax.ppermute(sensor_out, 'gx', facing)  2.58 us
  transfers between devices with their start and end apart: 7, of which 4 were waited for; matrix products, arithmetic and copies ran while one was open for 0% of the time, Pallas kernels for 25%

profile of v2, /device:TPU:111, one launch (start us, length us, event | category | flops | bytes accessed | tf_op | source)
XLA Modules:
  0.0 75.1 jit_solution(2603248643212794403)
XLA Ops:
  0.6 0.0 copy-start
  0.6 1.0 %copy-done = f32[2,4,64,256]{3,2,1,0:T(8,128)S(1)} copy-done((f32[2,4,64,256]{3,2,1,0:T(8,128)S(1)}, f32[2,4,64,256]{3,2,1,0:T(8,128)}, u32[]{:S(2)}) %copy-start) | copy-done | bytes 524312
  1.7 0.0 copy-start.2
  1.7 0.1 flip_sensor.1
  1.7 2.6 %collective-permute-start.4 = (f32[2,3,2,64,128]{4,3,2,1,0:T(8,128)S(1)}, f32[2,3,2,64,128]{4,3,2,1,0:T(8,128)S(1)}, u32[]{:S(2)}, u32[]{:S(2)}) collective-permute-start(f32[2,3,2,64,128]{4,3,2,1,0:T(8,128)S(1)} %flip_sensor.1), channel_id=1, source_target_pairs={{0,240},{16,224},{32,208},{48,192},{64,176},{80,160},{96,144},{112... | collective-permute-start | bytes 1179656 | tf_op jit(solution)/shard_map/ppermute | solution.py:584
  4.3 0.1 pad_add_fusion.place
  4.4 0.0 copy-start.1
  4.4 1.0 %copy-done.1 = f32[2,4,64,256]{3,2,1,0:T(8,128)S(1)} copy-done((f32[2,4,64,256]{3,2,1,0:T(8,128)S(1)}, f32[2,4,64,256]{3,2,1,0:T(8,128)}, u32[]{:S(2)}) %copy-start.1) | copy-done | bytes 524312
  5.4 0.0 copy-start.3
  5.4 1.0 %copy-done.3 = f32[2,4,64,256]{3,2,1,0:T(8,128)S(1)} copy-done((f32[2,4,64,256]{3,2,1,0:T(8,128)S(1)}, f32[2,4,64,256]{3,2,1,0:T(8,128)}, u32[]{:S(2)}) %copy-start.3) | copy-done | bytes 524312
  6.5 0.0 copy-start.5
  6.5 0.8 %copy-done.5 = f32[64,256]{1,0:T(8,128)S(1)} copy-done((f32[64,256]{1,0:T(8,128)S(1)}, f32[64,256]{1,0:T(8,128)}, u32[]{:S(2)}) %copy-start.5) | copy-done | bytes 65560
  7.3 0.0 copy-start.7
  7.3 0.9 %copy-done.7 = s32[2,64,256]{2,1,0:T(8,128)S(1)} copy-done((s32[2,64,256]{2,1,0:T(8,128)S(1)}, s32[2,64,256]{2,1,0:T(8,128)}, u32[]{:S(2)}) %copy-start.7) | copy-done | bytes 131096
  8.2 0.0 copy-start.9
  8.2 0.7 copy-done.9
  8.9 1.7 %columns.1 = (f32[2,2,64,128]{3,2,1,0:T(8,128)S(1)}, f32[64,128]{1,0:T(8,128)S(1)}, f32[64,128]{1,0:T(8,128)S(1)}) custom-call(s32[2]{0:T(128)S(1)} %pad_add_fusion.place, f32[32]{0:T(128)S(1)} %copy-done.9, s32[2,64,256]{2,1,0:T(8,128)S(1)} %copy-done.7, f32[64,256]{1,0:T(8,128)S(1)} %copy-done.5, f32[2,4,64,256]{3,2,1,0:T(8,128)S(1)} %copy-done.1, ...), custom_call_target="tpu_custom_call" | custom-call | bytes 1024 | tf_op jit(solution)/shard_map/columns/pallas_call | solution.py:548
  10.6 1.2 %collective-permute-start = (f32[64,128]{1,0:T(8,128)S(1)}, f32[64,128]{1,0:T(8,128)S(1)}, u32[]{:S(2)}, u32[]{:S(2)}) collective-permute-start(f32[64,128]{1,0:T(8,128)S(1)} %get-tuple-element.17), channel_id=1, source_target_pairs={{0,1},{1,0},{2,3},{3,2},{4,5},{5,4},{6,7},{7,6},{8,9},{9,8},{10,11... | collective-permute-start | bytes 98312 | tf_op jit(solution)/shard_map/ppermute | solution.py:593
  11.7 4.9 %collective-permute-start.1 = (f32[64,128]{1,0:T(8,128)S(1)}, f32[64,128]{1,0:T(8,128)S(1)}, u32[]{:S(2)}, u32[]{:S(2)}) collective-permute-start(f32[64,128]{1,0:T(8,128)S(1)} %get-tuple-element.18), channel_id=1, source_target_pairs={{1,2},{2,1},{3,4},{4,3},{5,6},{6,5},{7,8},{8,7},{9,10},{10,9},{11,... | collective-permute-start | bytes 98312 | tf_op jit(solution)/shard_map/ppermute | solution.py:594
  16.6 1.3 %collective-permute-done.col_a = f32[64,128]{1,0:T(8,128)S(1)} collective-permute-done((f32[64,128]{1,0:T(8,128)S(1)}, f32[64,128]{1,0:T(8,128)S(1)}, u32[]{:S(2)}, u32[]{:S(2)}) %collective-permute-start) | collective-permute-done | bytes 32800 | tf_op jit(solution)/shard_map/ppermute | solution.py:593
  17.9 0.6 collective-permute-done.1.col_b
  18.5 0.0 copy-done.2
  18.5 1.0 %copy-done.4 = f32[2,4,64,256]{3,2,1,0:T(8,128)S(1)} copy-done((f32[2,4,64,256]{3,2,1,0:T(8,128)S(1)}, f32[2,4,64,256]{3,2,1,0:T(8,128)}, u32[]{:S(2)}) %copy-start.4) | copy-done | bytes 524312
  19.6 0.0 copy-start.6
  19.6 0.8 %copy-done.6 = f32[64,256]{1,0:T(8,128)S(1)} copy-done((f32[64,256]{1,0:T(8,128)S(1)}, f32[64,256]{1,0:T(8,128)}, u32[]{:S(2)}) %copy-start.6) | copy-done | bytes 65560
  20.4 0.7 rows.1
  21.1 1.3 %collective-permute-start.2 = (f32[264,128]{1,0:T(8,128)S(1)}, f32[264,128]{1,0:T(8,128)S(1)}, u32[]{:S(2)}, u32[]{:S(2)}) collective-permute-start(f32[264,128]{1,0:T(8,128)S(1)} %get-tuple-element.19), channel_id=1, source_target_pairs={{0,16},{16,0},{32,48},{48,32},{64,80},{80,64},{96,112},{112,96},{1... | collective-permute-start | bytes 405512 | tf_op jit(solution)/shard_map/ppermute | solution.py:599
  22.4 4.1 %collective-permute-start.3 = (f32[264,128]{1,0:T(8,128)S(1)}, f32[264,128]{1,0:T(8,128)S(1)}, u32[]{:S(2)}, u32[]{:S(2)}) collective-permute-start(f32[264,128]{1,0:T(8,128)S(1)} %get-tuple-element.20), channel_id=1, source_target_pairs={{16,32},{32,16},{48,64},{64,48},{80,96},{96,80},{112,128},{128,112... | collective-permute-start | bytes 405512 | tf_op jit(solution)/shard_map/ppermute | solution.py:600
  26.6 0.0 collective-permute-done.2.row_a
  26.6 5.8 %collective-permute-done.3.row_b = f32[264,128]{1,0:T(8,128)S(1)} collective-permute-done((f32[264,128]{1,0:T(8,128)S(1)}, f32[264,128]{1,0:T(8,128)S(1)}, u32[]{:S(2)}, u32[]{:S(2)}) %collective-permute-start.3) | collective-permute-done | bytes 135200 | tf_op jit(solution)/shard_map/ppermute | solution.py:600
  32.4 0.0 collective-permute-done.4.layers_in
  32.4 2.4 %build.1 = (f32[19,3,80,128]{3,2,1,0:T(8,128)S(1)}, f32[688,128]{1,0:T(8,128)S(1)}) custom-call(s32[2]{0:T(128)S(1)} %pad_add_fusion.place, f32[2,2,64,128]{3,2,1,0:T(8,128)S(1)} %get-tuple-element.16.power, f32[64,256]{1,0:T(8,128)S(1)} %copy-done.6, f32[2,4,64,256]{3,2,1,0:T(8,128)S(1)} %copy-done.2, f32[2,4,64,256]{3,2,1,0:T(8,128)S(1)} %copy-done.4, ...), custom_call_target="tpu_custom_call" | custom-call | bytes 1024 | tf_op jit(solution)/shard_map/build/pallas_call | solution.py:548
  34.7 2.3 %collective-permute-start.5 = (f32[688,128]{1,0:T(8,128)S(1)}, f32[688,128]{1,0:T(8,128)S(1)}, u32[]{:S(2)}, u32[]{:S(2)}) collective-permute-start(f32[688,128]{1,0:T(8,128)S(1)} %get-tuple-element.25), channel_id=1, source_target_pairs={{0,240},{16,224},{32,208},{48,192},{64,176},{80,160},{96,144},{112... | collective-permute-start | bytes 1056776 | tf_op jit(solution)/shard_map/ppermute | solution.py:609
  37.1 0.0 copy-start.8
  37.1 0.0 copy-start.10
  37.1 0.0 copy-start.11
  37.1 0.0 copy-start.13
  37.1 0.1 flip_peak.1
  37.1 3.2 %collective-permute-start.6 = (f32[2,3,2,64,128]{4,3,2,1,0:T(8,128)S(1)}, f32[2,3,2,64,128]{4,3,2,1,0:T(8,128)S(1)}, u32[]{:S(2)}, u32[]{:S(2)}) collective-permute-start(f32[2,3,2,64,128]{4,3,2,1,0:T(8,128)S(1)} %flip_peak.1), channel_id=1, source_target_pairs={{0,240},{16,224},{32,208},{48,192},{64,176},{80,160},{96,144},{112... | collective-permute-start | bytes 1179656 | tf_op jit(solution)/shard_map/ppermute | solution.py:611
  40.3 8.7 %collective-permute-done.5.message = f32[688,128]{1,0:T(8,128)S(1)} collective-permute-done((f32[688,128]{1,0:T(8,128)S(1)}, f32[688,128]{1,0:T(8,128)S(1)}, u32[]{:S(2)}, u32[]{:S(2)}) %collective-permute-start.5) | collective-permute-done | bytes 352288 | tf_op jit(solution)/shard_map/ppermute | solution.py:609
  49.1 0.0 copy-done.8
  49.1 0.0 copy-done.10
  49.1 0.0 copy-done.11
  49.1 0.0 copy-done.12
  49.1 0.0 copy-done.13
  49.1 16.7 %thermal_sensor.1 = (f32[2,4,64,256]{3,2,1,0:T(8,128)}, f32[2,4,64,256]{3,2,1,0:T(8,128)}, f32[2,7,3,80,128]{4,3,2,1,0:T(8,128)S(1)}) custom-call(s32[2]{0:T(128)S(1)} %pad_add_fusion.place, s32[2,4]{1,0:T(2,128)S(1)} %copy-done.8, f32[4]{0:T(128)S(1)} %copy-done.13, f32[4]{0:T(128)S(1)} %copy-done.10, f32[4]{0:T(128)S(1)} %copy-done.11, f32[2]{0:T(128)S(1)} %copy-done.12, ...), custom_call_target="tpu_custom_call" | custom-call | flops 99999997952 | bytes 67108864 | tf_op jit(solution)/shard_map/thermal_sensor/pallas_call | solution.py:548
  65.8 0.0 collective-permute-done.6.layers_in
  65.8 9.3 %peak.7 = f32[2,4,64,256]{3,2,1,0:T(8,128)} custom-call(s32[2]{0:T(128)S(1)} %pad_add_fusion.place, s32[2,4]{1,0:T(2,128)S(1)} %copy-done.8, f32[4]{0:T(128)S(1)} %copy-done.10, f32[4]{0:T(128)S(1)} %copy-done.11, f32[2]{0:T(128)S(1)} %copy-done.12, f32[19,3,80,128]{3,2,1,0:T(8,128)S(1)} %get-tuple-element.23.own, ...), custom_call_target="tpu_custom_call" | custom-call | bytes 1024 | tf_op jit(solution)/shard_map/peak/pallas_call | solution.py:548
  (2 shorter events, 0.0 us)
Async XLA Ops:
  0.6 1.0 %copy-start = (f32[2,4,64,256]{3,2,1,0:T(8,128)S(1)}, f32[2,4,64,256]{3,2,1,0:T(8,128)}, u32[]{:S(2)}) copy-start(f32[2,4,64,256]{3,2,1,0:T(8,128)} %sensor.5) | copy-start | bytes 1572868
  1.7 16.9 %copy-start.2 = (f32[2,4,64,256]{3,2,1,0:T(8,128)S(1)}, f32[2,4,64,256]{3,2,1,0:T(8,128)}, u32[]{:S(2)}) copy-start(f32[2,4,64,256]{3,2,1,0:T(8,128)} %sensor.5) | copy-start | bytes 1572868
  1.7 30.6 %collective-permute-start.4 = (f32[2,3,2,64,128]{4,3,2,1,0:T(8,128)S(1)}, f32[2,3,2,64,128]{4,3,2,1,0:T(8,128)S(1)}, u32[]{:S(2)}, u32[]{:S(2)}) collective-permute-start(f32[2,3,2,64,128]{4,3,2,1,0:T(8,128)S(1)} %flip_sensor.1), channel_id=1, source_target_pairs={{0,240},{16,224},{32,208},{48,192},{64,176},{80,160},{96,144},{112... | collective-permute-start | bytes 1179656 | tf_op jit(solution)/shard_map/ppermute | solution.py:584
  4.4 1.0 %copy-start.1 = (f32[2,4,64,256]{3,2,1,0:T(8,128)S(1)}, f32[2,4,64,256]{3,2,1,0:T(8,128)}, u32[]{:S(2)}) copy-start(f32[2,4,64,256]{3,2,1,0:T(8,128)} %sensor.5) | copy-start | bytes 1572868
  5.4 1.0 %copy-start.3 = (f32[2,4,64,256]{3,2,1,0:T(8,128)S(1)}, f32[2,4,64,256]{3,2,1,0:T(8,128)}, u32[]{:S(2)}) copy-start(f32[2,4,64,256]{3,2,1,0:T(8,128)} %peak.6) | copy-start | bytes 1572868
  6.5 0.8 %copy-start.5 = (f32[64,256]{1,0:T(8,128)S(1)}, f32[64,256]{1,0:T(8,128)}, u32[]{:S(2)}) copy-start(f32[64,256]{1,0:T(8,128)} %bond.5) | copy-start | bytes 196612
  7.3 0.9 %copy-start.7 = (s32[2,64,256]{2,1,0:T(8,128)S(1)}, s32[2,64,256]{2,1,0:T(8,128)}, u32[]{:S(2)}) copy-start(s32[2,64,256]{2,1,0:T(8,128)} %ids.1) | copy-start | bytes 393220
  8.2 0.7 copy-start.9
  10.6 7.3 %collective-permute-start = (f32[64,128]{1,0:T(8,128)S(1)}, f32[64,128]{1,0:T(8,128)S(1)}, u32[]{:S(2)}, u32[]{:S(2)}) collective-permute-start(f32[64,128]{1,0:T(8,128)S(1)} %get-tuple-element.17), channel_id=1, source_target_pairs={{0,1},{1,0},{2,3},{3,2},{4,5},{5,4},{6,7},{7,6},{8,9},{9,8},{10,11... | collective-permute-start | bytes 98312 | tf_op jit(solution)/shard_map/ppermute | solution.py:593
  11.7 6.8 %collective-permute-start.1 = (f32[64,128]{1,0:T(8,128)S(1)}, f32[64,128]{1,0:T(8,128)S(1)}, u32[]{:S(2)}, u32[]{:S(2)}) collective-permute-start(f32[64,128]{1,0:T(8,128)S(1)} %get-tuple-element.18), channel_id=1, source_target_pairs={{1,2},{2,1},{3,4},{4,3},{5,6},{6,5},{7,8},{8,7},{9,10},{10,9},{11,... | collective-permute-start | bytes 98312 | tf_op jit(solution)/shard_map/ppermute | solution.py:594
  18.5 1.0 %copy-start.4 = (f32[2,4,64,256]{3,2,1,0:T(8,128)S(1)}, f32[2,4,64,256]{3,2,1,0:T(8,128)}, u32[]{:S(2)}) copy-start(f32[2,4,64,256]{3,2,1,0:T(8,128)} %peak.6) | copy-start | bytes 1572868
  19.6 0.8 %copy-start.6 = (f32[64,256]{1,0:T(8,128)S(1)}, f32[64,256]{1,0:T(8,128)}, u32[]{:S(2)}) copy-start(f32[64,256]{1,0:T(8,128)} %bond.5) | copy-start | bytes 196612
  21.1 5.5 %collective-permute-start.2 = (f32[264,128]{1,0:T(8,128)S(1)}, f32[264,128]{1,0:T(8,128)S(1)}, u32[]{:S(2)}, u32[]{:S(2)}) collective-permute-start(f32[264,128]{1,0:T(8,128)S(1)} %get-tuple-element.19), channel_id=1, source_target_pairs={{0,16},{16,0},{32,48},{48,32},{64,80},{80,64},{96,112},{112,96},{1... | collective-permute-start | bytes 405512 | tf_op jit(solution)/shard_map/ppermute | solution.py:599
  22.4 9.9 %collective-permute-start.3 = (f32[264,128]{1,0:T(8,128)S(1)}, f32[264,128]{1,0:T(8,128)S(1)}, u32[]{:S(2)}, u32[]{:S(2)}) collective-permute-start(f32[264,128]{1,0:T(8,128)S(1)} %get-tuple-element.20), channel_id=1, source_target_pairs={{16,32},{32,16},{48,64},{64,48},{80,96},{96,80},{112,128},{128,112... | collective-permute-start | bytes 405512 | tf_op jit(solution)/shard_map/ppermute | solution.py:600
  34.7 14.3 %collective-permute-start.5 = (f32[688,128]{1,0:T(8,128)S(1)}, f32[688,128]{1,0:T(8,128)S(1)}, u32[]{:S(2)}, u32[]{:S(2)}) collective-permute-start(f32[688,128]{1,0:T(8,128)S(1)} %get-tuple-element.25), channel_id=1, source_target_pairs={{0,240},{16,224},{32,208},{48,192},{64,176},{80,160},{96,144},{112... | collective-permute-start | bytes 1056776 | tf_op jit(solution)/shard_map/ppermute | solution.py:609
  37.1 12.0 %copy-start.8 = (s32[2,4]{1,0:T(2,128)S(1)}, s32[2,4]{1,0:T(2,128)}, u32[]{:S(2)}) copy-start(s32[2,4]{1,0:T(2,128)} %layer_class.3) | copy-start | bytes 100
  37.1 12.0 %copy-start.10 = (f32[4]{0:T(128)S(1)}, f32[4]{0:T(128)}, u32[]{:S(2)}) copy-start(f32[4]{0:T(128)} %lateral.3) | copy-start | bytes 52
  37.1 12.0 %copy-start.11 = (f32[4]{0:T(128)S(1)}, f32[4]{0:T(128)}, u32[]{:S(2)}) copy-start(f32[4]{0:T(128)} %vertical.3) | copy-start | bytes 52
  37.1 12.0 %copy-start.12 = (f32[2]{0:T(128)S(1)}, f32[2]{0:T(128)}, u32[]{:S(2)}) copy-start(f32[2]{0:T(128)} %sink.3) | copy-start | bytes 28
  37.1 12.0 %copy-start.13 = (f32[4]{0:T(128)S(1)}, f32[4]{0:T(128)}, u32[]{:S(2)}) copy-start(f32[4]{0:T(128)} %share.1) | copy-start | bytes 52
  37.1 28.7 %collective-permute-start.6 = (f32[2,3,2,64,128]{4,3,2,1,0:T(8,128)S(1)}, f32[2,3,2,64,128]{4,3,2,1,0:T(8,128)S(1)}, u32[]{:S(2)}, u32[]{:S(2)}) collective-permute-start(f32[2,3,2,64,128]{4,3,2,1,0:T(8,128)S(1)} %flip_peak.1), channel_id=1, source_target_pairs={{0,240},{16,224},{32,208},{48,192},{64,176},{80,160},{96,144},{112... | collective-permute-start | bytes 1179656 | tf_op jit(solution)/shard_map/ppermute | solution.py:611

commit v3 on v2

v3 whole, which is shorter than its diff:
```python
import jax
import jax.numpy as jnp
from jax import lax
from jax.experimental import pallas as pl
from jax.experimental.pallas import tpu as pltpu
from jax.sharding import PartitionSpec as P


BLOCKS = 32
ROWS = 80
DEEP = 6
NEAR = 3
F32 = jnp.float32

VMEM = pl.BlockSpec(memory_space=pltpu.VMEM)
SMEM = pl.BlockSpec(memory_space=pltpu.SMEM)

STRIP_H = [DEEP] * 3 + [NEAR] * 16
STRIP_AT = [sum(STRIP_H[:n]) for n in range(19)]
PART_H = [DEEP] * 3 + [2, 1] * 4
PART_AT = [2 * sum(PART_H[:n]) for n in range(11)]


def lanes():
    return lax.broadcasted_iota(jnp.int32, (8, 128), 1)


def sublanes():
    return lax.broadcasted_iota(jnp.int32, (8, 128), 0)


def rolled(x, shift, axis):
    size = x.shape[axis]
    shift %= size
    return x if shift == 0 else pltpu.roll(x, shift, axis)


def mirrored(x):
    return jnp.take_along_axis(x, 7 - sublanes(), axis=0)


def ring_tile(from_right, from_left, n):
    h, at = STRIP_H[n], STRIP_AT[n]
    lane = lanes()
    return jnp.where(
        lane < h,
        rolled(from_right, -at, 1),
        jnp.where(lane >= 128 - h, rolled(from_left, 128 - h - at, 1), 0.0),
    )


def gather_kernel(
    place, block_power, ids, bond, sensor, peak, own, first_out, to_a, to_b, table, blocks, sems
):
    copies = [
        pltpu.make_async_copy(block_power, table, sems.at[0]),
        pltpu.make_async_copy(ids, blocks, sems.at[1]),
    ]
    for n in range(2, 19):
        for t in range(2):
            cut = pl.ds(128 * t, 128)
            if n == 2:
                source = bond.at[:, cut]
            else:
                field, m = (sensor, n - 3) if n < 11 else (peak, n - 11)
                source = field.at[m // 4, m % 4, :, cut]
            copies.append(
                pltpu.make_async_copy(source, own.at[n, t, pl.ds(8, 64), :], sems.at[len(copies)])
            )
    for copy in copies:
        copy.start()
    copies[0].wait()
    copies[1].wait()
    values = [table[n] for n in range(BLOCKS)]

    def look_up(k):
        stores = []
        for d in range(2):
            for t in range(2):
                index = blocks[d, tile_rows(k), 128 * t : 128 * t + 128]
                level = values
                bit = 1
                while len(level) > 1:
                    odd = (index & bit) != 0
                    level = [
                        jnp.where(odd, level[2 * n + 1], level[2 * n])
                        for n in range(len(level) // 2)
                    ]
                    bit *= 2
                stores.append((own, (d, t, tile_rows(k, 8)), level[0]))
                stores.append((first_out, (6 + d, t, tile_rows(7 - k)), mirrored(level[0])))
        return stores

    tile_loop(0, 8, 1, look_up)
    for copy in copies[2:]:
        copy.wait()
    even = (place[1] & 1) == 0

    def pack(k):
        lane = lanes()
        stores = []
        right_edge = jnp.zeros((8, 128), F32)
        left_edge = jnp.zeros((8, 128), F32)
        for n in range(19):
            h, at = STRIP_H[n], STRIP_AT[n]
            here = (lane >= at) & (lane < at + h)
            tiles = [own[n, t, tile_rows(k, 8), :] for t in range(2)]
            left_edge = jnp.where(here, rolled(tiles[0], at, 1), left_edge)
            right_edge = jnp.where(here, rolled(tiles[1], at - (128 - h), 1), right_edge)
            slot = 8 if n == 2 else 3 * ((n - 3) // 4) + (n - 3) % 4 - 1
            if n == 2 or (3 <= n < 11 and (n - 3) % 4 > 0):
                for t in range(2):
                    stores.append((first_out, (slot, t, tile_rows(7 - k)), mirrored(tiles[t])))
        stores.append((to_a, (tile_rows(k),), jnp.where(even, right_edge, left_edge)))
        stores.append((to_b, (tile_rows(k),), jnp.where(even, left_edge, right_edge)))
        return stores

    tile_loop(0, 8, 2, pack)


def sides(place, axis, from_a, from_b, rows):
    even = (place[axis] & 1) == 0
    a, b = from_a[rows, :], from_b[rows, :]
    return jnp.where(even, a, b), jnp.where(even, b, a)


def row_kernel(place, own, col_a, col_b, to_a, to_b, peak_out):
    even = (place[0] & 1) == 0
    row = sublanes()
    strips = []
    for first in (0, 56):
        rows = slice(first, first + 8)
        right, left = sides(place, 1, col_a, col_b, rows)

        def tile(n, t):
            if t < 2:
                return own[n, t, first + 8 : first + 16, :]
            return ring_tile(right, left, n)

        strip = []
        for t in range(3):
            for n in range(3):
                strip.append(tile(n, t))
            for m in range(8):
                x, y = tile(3 + 2 * m, t), tile(4 + 2 * m, t)
                if first == 0:
                    strip.append(jnp.where(row < 4, x, rolled(y, 4, 0)))
                else:
                    strip.append(jnp.where(row >= 4, x, rolled(y, -4, 0)))
        strips.append(strip)
    top, bottom = strips
    for n in range(33):
        rows = slice(8 * n, 8 * n + 8)
        to_a[rows, :] = jnp.where(even, bottom[n], top[n])
        to_b[rows, :] = jnp.where(even, top[n], bottom[n])

    def flip(k):
        return [
            (peak_out, (3 * d + l, t, tile_rows(7 - k)), mirrored(own[12 + 4 * d + l, t, tile_rows(k, 8), :]))
            for d in range(2)
            for l in range(3)
            for t in range(2)
        ]

    tile_loop(0, 8, 2, flip)


def build_kernel(place, start, col_a, col_b, row_a, row_b, own, message):
    def core(k):
        right, left = sides(place, 1, col_a, col_b, tile_rows(k))
        return [(own, (n, 2, tile_rows(k, 8)), ring_tile(right, left, n)) for n in range(19)]

    tile_loop(0, 8, 2, core)
    for t in range(3):
        for n in range(11):
            at = 8 * (11 * t + n)
            below, above = sides(place, 0, row_a, row_b, slice(at, at + 8))
            if n < 3:
                own[n, t, 0:8, :] = above
                own[n, t, 72:80, :] = below
            else:
                m = 3 + 2 * (n - 3)
                own[m, t, 0:8, :] = above
                own[m, t, 72:80, :] = below
                own[m + 1, t, 0:8, :] = rolled(above, 4, 0)
                own[m + 1, t, 72:80, :] = rolled(below, -4, 0)

    planes = [0, 1, 2]
    for field in range(2):
        for d in range(2):
            planes += [3 + 8 * field + 4 * d + 3, 3 + 8 * field + 4 * d + 2]

    def pack(k):
        lane = lanes()
        column = jnp.zeros((8, 128), F32)
        for slot, n in enumerate(planes):
            h, at = PART_H[slot], PART_AT[slot]
            here = (lane >= at) & (lane < at + 2 * h)
            column = jnp.where(here, rolled(own[n, 2, tile_rows(k), :], at + h, 1), column)
        return [(message, (tile_rows(9 - k),), mirrored(column))]

    tile_loop(0, 10, 5, pack)
    row = sublanes()
    for n in range(3):
        for t in range(2):
            at = 80 + 16 * (2 * n + t)
            message[at : at + 8, :] = mirrored(own[n, t, 72:80, :])
            message[at + 8 : at + 16, :] = mirrored(own[n, t, 0:8, :])
    for field in range(2):
        for d in range(2):
            n = 3 + 8 * field + 4 * d
            for t in range(2):
                above = jnp.where(
                    row >= 4, own[n + 3, t, 0:8, :], rolled(own[n + 2, t, 0:8, :], 4, 0)
                )
                below = jnp.where(
                    row < 4, own[n + 3, t, 72:80, :], rolled(own[n + 2, t, 72:80, :], 4, 0)
                )
                at = 176 + 16 * (4 * field + 2 * d + t)
                message[at : at + 8, :] = mirrored(below)
                message[at + 8 : at + 16, :] = mirrored(above)


def partner_ring(message, slot, rows):
    h, at = PART_H[slot], PART_AT[slot]
    lane = lanes()
    return jnp.where(
        (lane < h) | (lane >= 128 - h), rolled(message[rows, :], -(at + h), 1), 0.0
    )


def tile_loop(start, stop, unroll, body):
    def step(j, _):
        stores = []
        for u in range(unroll):
            stores += body(start + unroll * j + u)
        for ref, index, value in stores:
            ref[index] = value
        return 0

    lax.fori_loop(0, (stop - start) // unroll, step, 0)


def tile_rows(k, add=0):
    return pl.ds(pl.multiple_of(8 * k + add, 8), 8)


class Solver:
    def __init__(self, place, tables, d, v, cond):
        self.place, self.d, self.v, self.cond = place, d, v, cond
        layer_class, share, lateral, vertical, sink = tables
        self.coef = []
        for side in range(2):
            die = d if side == 0 else 1 - d
            classes = [layer_class[die, l] for l in range(4)]
            coefs = []
            for l in range(4):
                g = lateral[classes[l]]
                up = vertical[classes[l]] if l < 3 else jnp.float32(0)
                down = vertical[classes[l - 1]] if l > 0 else jnp.float32(0)
                diagonal = 4 * g + up + down
                if l == 0:
                    diagonal = diagonal + sink[die]
                part = share[classes[l]] if share is not None else None
                if l < 3:
                    inverse = 1.0 / jnp.full((8, 128), diagonal, F32)
                    scale = inverse if part is None else inverse * part
                    coefs.append((scale, g * inverse, up * inverse, down * inverse))
                else:
                    coefs.append((diagonal, g, down, part))
            self.coef.append(coefs)
        gy = place[1]
        right = jnp.where(gy == 15, 0.0, 1.0).astype(F32)
        left = jnp.where(gy == 0, 0.0, 1.0).astype(F32)
        self.ring = jnp.where(lanes() < 64, right, left)

    def prepare(self, bond_tile):
        def body(k):
            stores = []
            for t in range(3):
                bond = bond_tile(k, t)
                stores.append((self.cond, (self.d, 0, t, tile_rows(k)), bond))
                for side in range(2):
                    value = 1.0 / (self.coef[side][3][0] + bond)
                    stores.append((self.cond, (self.d, 1 + side, t, tile_rows(k)), value))
            return stores

        tile_loop(0, 10, 5, body)

    def zero_outside(self, b, planes):
        zero = jnp.zeros((8, 128), F32)
        for here, first in ((self.place[0] == 0, 8), (self.place[0] == 15, 80)):

            @pl.when(here)
            def _():
                for side, l in planes:
                    for t in range(3):
                        self.v[side][self.d, b, l, t, first : first + 8, :] = zero

    def first(self, work, unroll=2):
        def body(k):
            stores = []
            for side, layers, source in work:
                for t in range(3):
                    shared = {}
                    for l in layers:
                        s = source(l, t, tile_rows(k), shared)
                        coef = self.coef[side][l]
                        if l < 3:
                            s = s * coef[0]
                        else:
                            if coef[3] is not None:
                                s = s * coef[3]
                            s = s * self.cond[self.d, 1 + side, t, tile_rows(k)]
                        if t == 2:
                            s = s * self.ring
                        stores.append((self.v[side], (self.d, 0, l, t, tile_rows(k, 8)), s))
            return stores

        tile_loop(0, 10, unroll, body)
        self.zero_outside(0, [(side, l) for side, layers, _ in work for l in layers])

    def sweep(self, b, work, core_only=False, unroll=2):
        v, d = self.v, self.d

        def body(k):
            stores = []
            rows, to = tile_rows(k), tile_rows(k, 8)
            lane = lanes()
            first_lane, last_lane = lane == 0, lane == 127
            seen = {}

            def value(side, l, t):
                if (side, l, t) not in seen:
                    seen[side, l, t] = v[side][d, b, l, t, to, :]
                return seen[side, l, t]

            for side, layers, source, emit in work:
                shared = {}
                for l in layers:
                    coef = self.coef[side][l]
                    forward = [pltpu.roll(value(side, l, t), 1, 1) for t in range(3)]
                    backward = [pltpu.roll(value(side, l, t), 127, 1) for t in range(3)]
                    for t in range(2 if core_only else 3):
                        left = jnp.where(first_lane, forward[t - 1], forward[t])
                        right = jnp.where(last_lane, backward[(t + 1) % 3], backward[t])
                        around = (left + right) + (
                            v[side][d, b, l, t, pl.ds(8 * k + 7, 8), :]
                            + v[side][d, b, l, t, pl.ds(8 * k + 9, 8), :]
                        )
                        s = source(l, t, rows, shared)
                        if l < 3:
                            total = s * coef[0] + coef[1] * around
                            total = total + coef[2] * value(side, l + 1, t)
                            if l > 0:
                                total = total + coef[3] * value(side, l - 1, t)
                        else:
                            if coef[3] is not None:
                                s = s * coef[3]
                            total = (s + coef[1] * around) + coef[2] * value(side, 2, t)
                            total = total + self.cond[d, 0, t, rows] * value(1 - side, 3, t)
                            total = total * self.cond[d, 1 + side, t, rows]
                        if t == 2:
                            total = total * self.ring
                        if emit is None:
                            stores.append((v[side], (d, 1 - b, l, t, to), total))
                        else:
                            stores += emit(l, t, k, total)
            return stores

        if core_only:
            tile_loop(1, 9, unroll, body)
        else:
            tile_loop(0, 10, unroll, body)
            kept = [(side, l) for side, layers, _, emit in work if emit is None for l in layers]
            self.zero_outside(1 - b, kept)

    def solve_own(self, own_source, other_source, emit):
        every = (0, 1, 2, 3)
        self.first([(0, every, own_source), (1, (1, 2, 3), other_source)])
        self.sweep(0, [(0, every, own_source, None), (1, (2, 3), other_source, None)])
        self.sweep(1, [(0, every, own_source, None), (1, (3,), other_source, None)])
        self.sweep(0, [(0, every, own_source, emit)], core_only=True)

    def solve_before(self, own_source, emit):
        self.first([(0, (0, 1, 2, 3), own_source)])
        self.sweep(0, [(0, (0, 1, 2), own_source, None)])
        self.sweep(1, [(0, (0, 1), own_source, None)])
        self.sweep(0, [(0, (0,), own_source, emit)], core_only=True, unroll=4)

    def solve_after(self, own_source, other_source, emit):
        self.first([(1, (1, 2, 3), other_source)])
        self.sweep(0, [(0, (3,), own_source, None), (1, (2, 3), other_source, None)])
        self.sweep(1, [(0, (2, 3), own_source, None), (1, (3,), other_source, None)])
        self.sweep(0, [(0, (1, 2, 3), own_source, emit)], core_only=True)


def clear_pads(v):
    zero = jnp.zeros((8, 128), F32)
    for d in range(2):
        for b in range(2):
            for l in range(4):
                for t in range(3):
                    v[d, b, l, t, 0:8, :] = zero
                    v[d, b, l, t, 88:96, :] = zero


def place_other(planes, layers_in, message, field, d):
    other = 1 - d
    zero = jnp.zeros((8, 128), F32)

    def body(k):
        return [
            (planes, (l, t, tile_rows(k, 8)), layers_in(3 * other + l, t, tile_rows(k)))
            for l in range(3)
            for t in range(2)
        ]

    tile_loop(0, 8, 4, body)

    def ring(k):
        column = message[tile_rows(k), :]
        lane = lanes()
        stores = [(planes, (0, 2, tile_rows(k)), zero)]
        for slot_in, l, h in ((0, 2, 2), (1, 1, 1)):
            ats = [PART_AT[3 + 4 * field + 2 * die + slot_in] + h for die in range(2)]
            picked = jnp.where(other == 0, rolled(column, -ats[0], 1), rolled(column, -ats[1], 1))
            inside = (lane < h) | (lane >= 128 - h)
            stores.append((planes, (l, 2, tile_rows(k)), jnp.where(inside, picked, 0.0)))
        return stores

    tile_loop(0, 10, 5, ring)
    for t in range(2):
        planes[0, t, 0:8, :] = zero
        planes[0, t, 72:80, :] = zero
        at = 176 + 64 * field + 32 * other + 16 * t
        above = message[pl.ds(pl.multiple_of(at, 8), 8), :]
        below = message[pl.ds(pl.multiple_of(at + 8, 8), 8), :]
        planes[2, t, 0:8, :] = above
        planes[2, t, 72:80, :] = below
        planes[1, t, 0:8, :] = rolled(above, 4, 0)
        planes[1, t, 72:80, :] = rolled(below, -4, 0)


def place_deep(planes, first_in, message):
    def body(k):
        return [
            (planes, (n, t, tile_rows(k, 8)), first_in[6 + n, t, tile_rows(k), :])
            for n in range(3)
            for t in range(2)
        ]

    tile_loop(0, 8, 4, body)

    def ring(k):
        return [
            (planes, (n, 2, tile_rows(k)), partner_ring(message, n, tile_rows(k)))
            for n in range(3)
        ]

    tile_loop(0, 10, 5, ring)
    for n in range(3):
        for t in range(2):
            at = 80 + 16 * (2 * n + t)
            planes[n, t, 0:8, :] = message[at : at + 8, :]
            planes[n, t, 72:80, :] = message[at + 8 : at + 16, :]


def thermal_sensor_kernel(
    place, layer_class, share, lateral, vertical, sink, own, first_in, message,
    thermal, sensed, heat, weighted, early, cond, v_peak, v_own, v_other, planes, deep,
):
    for v in (v_own, v_other, v_peak):
        clear_pads(v)
    place_deep(deep, first_in, message)

    def frame(d, _):
        v = (v_own, v_other)
        solver = Solver(place, (layer_class, share, lateral, vertical, sink), d, v, cond)
        solver.prepare(
            lambda k, t: jnp.where(d == 0, own[2, t, tile_rows(k), :], deep[2, t, tile_rows(k), :])
        )

        def own_power(l, t, rows, shared):
            if t not in shared:
                shared[t] = own[d, t, rows, :]
            return shared[t]

        def their_power(l, t, rows, shared):
            if t not in shared:
                shared[t] = deep[1 - d, t, rows, :]
            return shared[t]

        every = (0, 1, 2, 3)
        solver.first([(0, every, own_power), (1, every, their_power)])
        for b in (0, 1):
            solver.sweep(b, [(0, every, own_power, None), (1, every, their_power, None)])

        def emit_own(l, t, k, total):
            peak = own[11 + 4 * d + l, t, tile_rows(k), :]
            stores = [(weighted, (d, l, t, tile_rows(k)), total * peak)]
            if t < 2:
                stores.append((v_own, (d, 1, l, t, tile_rows(k, 8)), total))
            return stores

        def emit_other(l, t, k, total):
            return [(heat, (d, l - 1, t, tile_rows(k)), total)]

        solver.sweep(
            0, [(0, every, own_power, emit_own), (1, (1, 2, 3), their_power, emit_other)]
        )

        def write(k):
            return [
                (
                    thermal,
                    (d, l, tile_rows(k), slice(128 * t, 128 * t + 128)),
                    v_own[d, 1, l, t, tile_rows(k, 16), :],
                )
                for l in range(4)
                for t in range(2)
            ]

        tile_loop(0, 8, 4, write)

        plain = (layer_class, None, lateral, vertical, sink)

        def layers_in(n, t, rows):
            return first_in[n, t, rows, :]

        place_other(planes, layers_in, message, 0, d)

        def own_sensor(l, t, rows, shared):
            return own[3 + 4 * d + l, t, rows, :]

        def their_sensor(l, t, rows, shared):
            return planes[l - 1, t, rows, :]

        def emit(l, t, k, total):
            return [(sensed, (d, l, tile_rows(k, -8), slice(128 * t, 128 * t + 128)), total)]

        Solver(place, plain, d, v, cond).solve_own(own_sensor, their_sensor, emit)

        def own_peak(l, t, rows, shared):
            return weighted[d, l, t, rows, :]

        def emit_early(l, t, k, total):
            return [(early, (d, t, tile_rows(k, -8)), total)]

        Solver(place, plain, d, (v_peak, None), cond).solve_before(own_peak, emit_early)
        return 0

    lax.fori_loop(0, 2, frame, 0)


def peak_kernel(
    place, layer_class, lateral, vertical, sink, layers_in, message, heat, weighted, early, cond,
    v_start, out, v_peak, v_other, planes,
):
    clear_pads(v_other)

    def frame(d, _):
        plain = (layer_class, None, lateral, vertical, sink)
        solver = Solver(place, plain, d, (v_peak, v_other), cond)

        def layers(n, t, rows):
            return layers_in[n, t, rows, :]

        place_other(planes, layers, message, 1, d)

        def own_peak(l, t, rows, shared):
            return weighted[d, l, t, rows, :]

        def their_peak(l, t, rows, shared):
            return planes[l - 1, t, rows, :] * heat[d, l - 1, t, rows, :]

        def emit(l, t, k, total):
            return [(out, (d, l, tile_rows(k, -8), slice(128 * t, 128 * t + 128)), total)]

        solver.solve_after(own_peak, their_peak, emit)

        def write(k):
            return [
                (
                    out,
                    (d, 0, tile_rows(k), slice(128 * t, 128 * t + 128)),
                    early[d, t, tile_rows(k), :],
                )
                for t in range(2)
            ]

        tile_loop(0, 8, 8, write)
        return 0

    lax.fori_loop(0, 2, frame, 0)


PLANES = (19, 3, ROWS, 128)
FIELD = (2, 4, 64, 256)
V = (2, 2, 4, 3, ROWS + 16, 128)
OTHER = (3, 3, ROWS, 128)
KEPT = [
    (2, 3, 3, ROWS, 128),
    (2, 4, 3, ROWS, 128),
    (2, 2, 64, 128),
    (2, 3, 3, ROWS, 128),
    V,
]


def call(kernel, tables, arrays, outs, scratch=(), flops=0, aliases={}, hbm=0, name=None):
    shapes = [jax.ShapeDtypeStruct(shape, F32) for shape in outs]
    arrays = [
        pltpu.with_memory_space_constraint(x, pltpu.HBM) if i < hbm else x
        for i, x in enumerate(arrays)
    ]
    anywhere = pl.BlockSpec(memory_space=pltpu.HBM)
    return pl.pallas_call(
        kernel,
        out_shape=shapes,
        in_specs=[SMEM] * len(tables) + [anywhere] * hbm + [VMEM] * (len(arrays) - hbm),
        out_specs=[VMEM] * len(shapes),
        scratch_shapes=[pltpu.VMEM(x, F32) if isinstance(x, tuple) else x for x in scratch],
        input_output_aliases={len(tables) + i: o for i, o in aliases.items()},
        compiler_params=pltpu.CompilerParams(vmem_limit_bytes=16 << 20),
        cost_estimate=pl.CostEstimate(flops=flops, bytes_accessed=1024, transcendentals=0),
        name=name,
    )(*tables, *arrays)


def pairs(count, odd):
    if odd:
        return [(i, ((i - 1) ^ 1) + 1) for i in range(1, count - 1)]
    return [(i, i ^ 1) for i in range(count)]


def local(
    block_ids,
    block_power,
    layer_class,
    power_share,
    lateral_k,
    vertical_k,
    sink_conductance,
    bond_conductance,
    peak_factors,
    sensor_weight,
):
    nx, ny = lax.axis_size("gx"), lax.axis_size("gy")
    facing = [(i, nx - 1 - i) for i in range(nx)]
    place = jnp.stack([lax.axis_index("gx"), lax.axis_index("gy")]).astype(jnp.int32)
    own, first_out, col_a, col_b = call(
        gather_kernel,
        (place,),
        (block_power, block_ids, bond_conductance, sensor_weight, peak_factors),
        [PLANES, (9, 2, 64, 128), (64, 128), (64, 128)],
        [
            pltpu.SMEM((BLOCKS,), F32),
            pltpu.VMEM((2, 64, 256), jnp.int32),
            pltpu.SemaphoreType.DMA((36,)),
        ],
        hbm=5,
        name="gather",
    )
    first_in = lax.ppermute(first_out, "gx", facing)
    col_a = lax.ppermute(col_a, "gy", pairs(ny, False))
    col_b = lax.ppermute(col_b, "gy", pairs(ny, True))
    row_a, row_b, peak_out = call(
        row_kernel,
        (place,),
        (own, col_a, col_b),
        [(264, 128), (264, 128), (6, 2, 64, 128)],
        name="rows",
    )
    row_a = lax.ppermute(row_a, "gx", pairs(nx, False))
    row_b = lax.ppermute(row_b, "gx", pairs(nx, True))
    peak_in = lax.ppermute(peak_out, "gx", facing)
    own, message = call(
        build_kernel,
        (place,),
        (own, col_a, col_b, row_a, row_b),
        [PLANES, (304, 128)],
        aliases={0: 0},
        name="build",
    )
    message = lax.ppermute(message, "gx", facing)
    state = call(
        thermal_sensor_kernel,
        (place, layer_class, power_share, lateral_k, vertical_k, sink_conductance),
        (own, first_in, message),
        [FIELD, FIELD] + KEPT,
        [V, V, OTHER, OTHER],
        flops=10**11,
        name="thermal_sensor",
    )
    thermal, sensed, *kept = state
    peak, _ = call(
        peak_kernel,
        (place, layer_class, lateral_k, vertical_k, sink_conductance),
        (peak_in, message, *kept),
        [FIELD, V],
        [V, OTHER],
        aliases={6: 1},
        name="peak",
    )
    return thermal, peak, sensed


def solution(mesh):
    return jax.shard_map(
        local,
        mesh=mesh,
        in_specs=(
            P(None, "gx", "gy"),
            P(),
            P(),
            P(),
            P(),
            P(),
            P(),
            P("gx", "gy"),
            P(None, None, "gx", "gy"),
            P(None, None, "gx", "gy"),
        ),
        out_specs=(P(None, None, "gx", "gy"),) * 3,
        check_vma=False,
    )
```

time: 76 us -> 66.6 us (0.88)
  the two profiles are of different devices: /device:TPU:111 before, /device:TPU:144 now
where the time goes in v3:
time: 66.6 us; the launch traced here: 66.5 us
  waiting for transfers between devices  26.2 us (39%)
  Pallas kernels  25.7 us (39%)
  starting transfers between devices  13.7 us (21%)
  between operations  0.74 us (1%)
    pallas_call x5, Pallas kernels, call(): pl.pallas_call(kernel, out_shape=shapes, in_specs=[SMEM] * len(tables) +...  25.7 us
    ppermute x1, waiting for transfers between devices, local(): col_a = lax.ppermute(col_a, 'gy', pairs(ny, False))  13.6 us
    ppermute x1, waiting for transfers between devices, local(): row_b = lax.ppermute(row_b, 'gx', pairs(nx, True))  8.01 us
    ppermute x1, starting transfers between devices, local(): peak_in = lax.ppermute(peak_out, 'gx', facing)  5.35 us
    ppermute x1, waiting for transfers between devices, local(): message = lax.ppermute(message, 'gx', facing)  4.64 us
    ppermute x1, starting transfers between devices, local(): col_a = lax.ppermute(col_a, 'gy', pairs(ny, False))  2.18 us
    ppermute x1, starting transfers between devices, local(): first_in = lax.ppermute(first_out, 'gx', facing)  2.06 us
    ppermute x1, starting transfers between devices, local(): col_b = lax.ppermute(col_b, 'gy', pairs(ny, True))  1.91 us
  transfers between devices with their start and end apart: 7, of which 3 were waited for; matrix products, arithmetic and copies ran while one was open for 0% of the time, Pallas kernels for 27%

profile of v3, /device:TPU:144, one launch (start us, length us, event | category | flops | bytes accessed | tf_op | source)
XLA Modules:
  0.0 66.5 jit_solution(17141907779178206484)
XLA Ops:
  0.6 0.1 pad_add_fusion.place
  0.7 2.7 %gather.1 = (f32[19,3,80,128]{3,2,1,0:T(8,128)S(1)}, f32[9,2,64,128]{3,2,1,0:T(8,128)S(1)}, f32[64,128]{1,0:T(8,128)S(1)}, f32[64,128]{1,0:T(8,128)S(1)}) custom-call(s32[2]{0:T(128)S(1)} %pad_add_fusion.place, f32[32]{0:T(128)} %block_power.1, s32[2,64,256]{2,1,0:T(8,128)} %ids.1, f32[64,256]{1,0:T(8,128)} %bond.1, f32[2,4,64,256]{3,2,1,0:T(8,128)} %sensor.1, ...), custom_call_target="tpu_custom_call" | custom-call | bytes 1024 | tf_op jit(solution)/shard_map/gather/pallas_call | solution.py:618
  3.4 2.1 %collective-permute-start.4 = (f32[9,2,64,128]{3,2,1,0:T(8,128)S(1)}, f32[9,2,64,128]{3,2,1,0:T(8,128)S(1)}, u32[]{:S(2)}, u32[]{:S(2)}) collective-permute-start(f32[9,2,64,128]{3,2,1,0:T(8,128)S(1)} %get-tuple-element.26), channel_id=1, source_target_pairs={{0,240},{16,224},{32,208},{48,192},{64,176},{80,160},{96,144},{112... | collective-permute-start | bytes 1769480 | tf_op jit(solution)/shard_map/ppermute | solution.py:665
  5.5 2.2 %collective-permute-start = (f32[64,128]{1,0:T(8,128)S(1)}, f32[64,128]{1,0:T(8,128)S(1)}, u32[]{:S(2)}, u32[]{:S(2)}) collective-permute-start(f32[64,128]{1,0:T(8,128)S(1)} %get-tuple-element.21), channel_id=1, source_target_pairs={{0,1},{1,0},{2,3},{3,2},{4,5},{5,4},{6,7},{7,6},{8,9},{9,8},{10,11... | collective-permute-start | bytes 98312 | tf_op jit(solution)/shard_map/ppermute | solution.py:666
  7.6 1.9 %collective-permute-start.1 = (f32[64,128]{1,0:T(8,128)S(1)}, f32[64,128]{1,0:T(8,128)S(1)}, u32[]{:S(2)}, u32[]{:S(2)}) collective-permute-start(f32[64,128]{1,0:T(8,128)S(1)} %get-tuple-element.22), channel_id=1, source_target_pairs={{1,2},{2,1},{3,4},{4,3},{5,6},{6,5},{7,8},{8,7},{9,10},{10,9},{11,... | collective-permute-start | bytes 98312 | tf_op jit(solution)/shard_map/ppermute | solution.py:667
  9.6 13.6 %collective-permute-done.col_a = f32[64,128]{1,0:T(8,128)S(1)} collective-permute-done((f32[64,128]{1,0:T(8,128)S(1)}, f32[64,128]{1,0:T(8,128)S(1)}, u32[]{:S(2)}, u32[]{:S(2)}) %collective-permute-start) | collective-permute-done | bytes 32800 | tf_op jit(solution)/shard_map/ppermute | solution.py:666
  23.1 0.0 collective-permute-done.1.col_b
  23.1 0.0 copy-start
  23.1 0.0 copy-start.1
  23.1 0.0 copy-start.2
  23.1 0.0 copy-start.3
  23.1 0.0 copy-start.4
  23.2 0.7 %rows.1 = (f32[264,128]{1,0:T(8,128)S(1)}, f32[264,128]{1,0:T(8,128)S(1)}, f32[6,2,64,128]{3,2,1,0:T(8,128)S(1)}) custom-call(s32[2]{0:T(128)S(1)} %pad_add_fusion.place, f32[19,3,80,128]{3,2,1,0:T(8,128)S(1)} %get-tuple-element.20.own.start, f32[64,128]{1,0:T(8,128)S(1)} %collective-permute-done.col_a, f32[64,128]{1,0:T(8,128)S(1)} %collective-permute-done.1.col_b), custom_call_target="tpu_custom_call" | custom-call | bytes 1024 | tf_op jit(solution)/shard_map/rows/pallas_call | solution.py:618
  23.9 0.2 collective-permute-start.2
  24.1 1.9 %collective-permute-start.3 = (f32[264,128]{1,0:T(8,128)S(1)}, f32[264,128]{1,0:T(8,128)S(1)}, u32[]{:S(2)}, u32[]{:S(2)}) collective-permute-start(f32[264,128]{1,0:T(8,128)S(1)} %get-tuple-element.24), channel_id=1, source_target_pairs={{16,32},{32,16},{48,64},{64,48},{80,96},{96,80},{112,128},{128,112... | collective-permute-start | bytes 405512 | tf_op jit(solution)/shard_map/ppermute | solution.py:676
  26.0 0.0 collective-permute-done.2.row_a
  26.0 8.0 %collective-permute-done.3.row_b = f32[264,128]{1,0:T(8,128)S(1)} collective-permute-done((f32[264,128]{1,0:T(8,128)S(1)}, f32[264,128]{1,0:T(8,128)S(1)}, u32[]{:S(2)}, u32[]{:S(2)}) %collective-permute-start.3) | collective-permute-done | bytes 135200 | tf_op jit(solution)/shard_map/ppermute | solution.py:676
  34.0 1.4 %build.1 = (f32[19,3,80,128]{3,2,1,0:T(8,128)S(1)}, f32[304,128]{1,0:T(8,128)S(1)}) custom-call(s32[2]{0:T(128)S(1)} %pad_add_fusion.place, f32[19,3,80,128]{3,2,1,0:T(8,128)S(1)} %get-tuple-element.20.own.start, f32[64,128]{1,0:T(8,128)S(1)} %collective-permute-done.col_a, ...), custom_call_target="tpu_custom_call", output_to_operand_aliasing={{0}: (1, {})} | custom-call | bytes 1024 | tf_op jit(solution)/shard_map/build/pallas_call | solution.py:618
  35.5 0.1 collective-permute-start.5
  35.6 5.3 %collective-permute-start.6 = (f32[6,2,64,128]{3,2,1,0:T(8,128)S(1)}, f32[6,2,64,128]{3,2,1,0:T(8,128)S(1)}, u32[]{:S(2)}, u32[]{:S(2)}) collective-permute-start(f32[6,2,64,128]{3,2,1,0:T(8,128)S(1)} %get-tuple-element.29), channel_id=1, source_target_pairs={{0,240},{16,224},{32,208},{48,192},{64,176},{80,160},{96,144},{112... | collective-permute-start | bytes 1179656 | tf_op jit(solution)/shard_map/ppermute | solution.py:677
  40.9 4.6 %collective-permute-done.5.message = f32[304,128]{1,0:T(8,128)S(1)} collective-permute-done((f32[304,128]{1,0:T(8,128)S(1)}, f32[304,128]{1,0:T(8,128)S(1)}, u32[]{:S(2)}, u32[]{:S(2)}) %collective-permute-start.5) | collective-permute-done | bytes 155680 | tf_op jit(solution)/shard_map/ppermute | solution.py:686
  45.6 0.0 collective-permute-done.4.first_in
  45.6 0.0 copy-done
  45.6 0.0 copy-done.1
  45.6 0.0 copy-done.2
  45.6 0.0 copy-done.3
  45.6 0.0 copy-done.4
  45.6 15.5 %thermal_sensor.1 = (f32[2,4,64,256]{3,2,1,0:T(8,128)}, f32[2,4,64,256]{3,2,1,0:T(8,128)}, f32[2,3,3,80,128]{4,3,2,1,0:T(8,128)S(1)}, f32[2,4,3,80,128]{4,3,2,1,...) custom-call(s32[2]{0:T(128)S(1)} %pad_add_fusion.place, ...), custom_call_target="tpu_custom_call" | custom-call | flops 99999997952 | bytes 1024 | tf_op jit(solution)/shard_map/thermal_sensor/pallas_call | solution.py:618
  61.1 0.0 collective-permute-done.6.layers_in
  61.1 5.4 %peak.3 = (f32[2,4,64,256]{3,2,1,0:T(8,128)}, f32[2,2,4,3,96,128]{5,4,3,2,1,0:T(8,128)S(1)}) custom-call(s32[2]{0:T(128)S(1)} %pad_add_fusion.place, s32[2,4]{1,0:T(2,128)S(1)} %copy-done, f32[4]{0:T(128)S(1)} %copy-done.1, f32[4]{0:T(128)S(1)} %copy-done.2, f32[2]{0:T(128)S(1)} %copy-done.3, ...), custom_call_target="tpu_custom_call", output_to_operand_aliasing={{1}: (11, {})} | custom-call | bytes 1024 | tf_op jit(solution)/shard_map/peak/pallas_call | solution.py:618
Async XLA Ops:
  3.4 42.2 %collective-permute-start.4 = (f32[9,2,64,128]{3,2,1,0:T(8,128)S(1)}, f32[9,2,64,128]{3,2,1,0:T(8,128)S(1)}, u32[]{:S(2)}, u32[]{:S(2)}) collective-permute-start(f32[9,2,64,128]{3,2,1,0:T(8,128)S(1)} %get-tuple-element.26), channel_id=1, source_target_pairs={{0,240},{16,224},{32,208},{48,192},{64,176},{80,160},{96,144},{112... | collective-permute-start | bytes 1769480 | tf_op jit(solution)/shard_map/ppermute | solution.py:665
  5.5 17.7 %collective-permute-start = (f32[64,128]{1,0:T(8,128)S(1)}, f32[64,128]{1,0:T(8,128)S(1)}, u32[]{:S(2)}, u32[]{:S(2)}) collective-permute-start(f32[64,128]{1,0:T(8,128)S(1)} %get-tuple-element.21), channel_id=1, source_target_pairs={{0,1},{1,0},{2,3},{3,2},{4,5},{5,4},{6,7},{7,6},{8,9},{9,8},{10,11... | collective-permute-start | bytes 98312 | tf_op jit(solution)/shard_map/ppermute | solution.py:666
  7.6 15.5 %collective-permute-start.1 = (f32[64,128]{1,0:T(8,128)S(1)}, f32[64,128]{1,0:T(8,128)S(1)}, u32[]{:S(2)}, u32[]{:S(2)}) collective-permute-start(f32[64,128]{1,0:T(8,128)S(1)} %get-tuple-element.22), channel_id=1, source_target_pairs={{1,2},{2,1},{3,4},{4,3},{5,6},{6,5},{7,8},{8,7},{9,10},{10,9},{11,... | collective-permute-start | bytes 98312 | tf_op jit(solution)/shard_map/ppermute | solution.py:667
  23.1 22.5 %copy-start = (s32[2,4]{1,0:T(2,128)S(1)}, s32[2,4]{1,0:T(2,128)}, u32[]{:S(2)}) copy-start(s32[2,4]{1,0:T(2,128)} %layer_class.3) | copy-start | bytes 100
  23.1 22.5 %copy-start.1 = (f32[4]{0:T(128)S(1)}, f32[4]{0:T(128)}, u32[]{:S(2)}) copy-start(f32[4]{0:T(128)} %lateral.3) | copy-start | bytes 52
  23.1 22.5 %copy-start.2 = (f32[4]{0:T(128)S(1)}, f32[4]{0:T(128)}, u32[]{:S(2)}) copy-start(f32[4]{0:T(128)} %vertical.3) | copy-start | bytes 52
  23.1 22.5 %copy-start.3 = (f32[2]{0:T(128)S(1)}, f32[2]{0:T(128)}, u32[]{:S(2)}) copy-start(f32[2]{0:T(128)} %sink.3) | copy-start | bytes 28
  23.1 22.5 %copy-start.4 = (f32[4]{0:T(128)S(1)}, f32[4]{0:T(128)}, u32[]{:S(2)}) copy-start(f32[4]{0:T(128)} %share.1) | copy-start | bytes 52
  23.9 2.1 %collective-permute-start.2 = (f32[264,128]{1,0:T(8,128)S(1)}, f32[264,128]{1,0:T(8,128)S(1)}, u32[]{:S(2)}, u32[]{:S(2)}) collective-permute-start(f32[264,128]{1,0:T(8,128)S(1)} %get-tuple-element.23), channel_id=1, source_target_pairs={{0,16},{16,0},{32,48},{48,32},{64,80},{80,64},{96,112},{112,96},{1... | collective-permute-start | bytes 405512 | tf_op jit(solution)/shard_map/ppermute | solution.py:675
  24.1 9.9 %collective-permute-start.3 = (f32[264,128]{1,0:T(8,128)S(1)}, f32[264,128]{1,0:T(8,128)S(1)}, u32[]{:S(2)}, u32[]{:S(2)}) collective-permute-start(f32[264,128]{1,0:T(8,128)S(1)} %get-tuple-element.24), channel_id=1, source_target_pairs={{16,32},{32,16},{48,64},{64,48},{80,96},{96,80},{112,128},{128,112... | collective-permute-start | bytes 405512 | tf_op jit(solution)/shard_map/ppermute | solution.py:676
  35.5 10.1 %collective-permute-start.5 = (f32[304,128]{1,0:T(8,128)S(1)}, f32[304,128]{1,0:T(8,128)S(1)}, u32[]{:S(2)}, u32[]{:S(2)}) collective-permute-start(f32[304,128]{1,0:T(8,128)S(1)} %get-tuple-element.27), channel_id=1, source_target_pairs={{0,240},{16,224},{32,208},{48,192},{64,176},{80,160},{96,144},{112... | collective-permute-start | bytes 466952 | tf_op jit(solution)/shard_map/ppermute | solution.py:686
  35.6 25.5 %collective-permute-start.6 = (f32[6,2,64,128]{3,2,1,0:T(8,128)S(1)}, f32[6,2,64,128]{3,2,1,0:T(8,128)S(1)}, u32[]{:S(2)}, u32[]{:S(2)}) collective-permute-start(f32[6,2,64,128]{3,2,1,0:T(8,128)S(1)} %get-tuple-element.29), channel_id=1, source_target_pairs={{0,240},{16,224},{32,208},{48,192},{64,176},{80,160},{96,144},{112... | collective-permute-start | bytes 1179656 | tf_op jit(solution)/shard_map/ppermute | solution.py:677

commit v4 on v3

v4 whole, which is shorter than its diff:
```python
import jax
import jax.numpy as jnp
from jax import lax
from jax.experimental import pallas as pl
from jax.experimental.pallas import tpu as pltpu
from jax.sharding import PartitionSpec as P


BLOCKS = 32
ROWS = 80
DEEP = 6
NEAR = 3
F32 = jnp.float32

VMEM = pl.BlockSpec(memory_space=pltpu.VMEM)
SMEM = pl.BlockSpec(memory_space=pltpu.SMEM)

STRIP_H = [DEEP] * 3 + [NEAR] * 16
STRIP_AT = [sum(STRIP_H[:n]) for n in range(19)]
PART_H = [DEEP] * 3 + [2, 1] * 4
PART_AT = [2 * sum(PART_H[:n]) for n in range(11)]


def lanes():
    return lax.broadcasted_iota(jnp.int32, (8, 128), 1)


def sublanes():
    return lax.broadcasted_iota(jnp.int32, (8, 128), 0)


def rolled(x, shift, axis):
    size = x.shape[axis]
    shift %= size
    return x if shift == 0 else pltpu.roll(x, shift, axis)


def mirrored(x):
    return jnp.take_along_axis(x, 7 - sublanes(), axis=0)


def ring_tile(from_right, from_left, n):
    h, at = STRIP_H[n], STRIP_AT[n]
    lane = lanes()
    return jnp.where(
        lane < h,
        rolled(from_right, -at, 1),
        jnp.where(lane >= 128 - h, rolled(from_left, 128 - h - at, 1), 0.0),
    )


def gather_kernel(
    place, block_power, ids, bond, sensor, peak, own, to_a, to_b, table, blocks, sems
):
    copies = [
        pltpu.make_async_copy(block_power, table, sems.at[0]),
        pltpu.make_async_copy(ids, blocks, sems.at[1]),
    ]
    for n in range(2, 19):
        for t in range(2):
            cut = pl.ds(128 * t, 128)
            if n == 2:
                source = bond.at[:, cut]
            else:
                field, m = (sensor, n - 3) if n < 11 else (peak, n - 11)
                source = field.at[m // 4, m % 4, :, cut]
            copies.append(
                pltpu.make_async_copy(source, own.at[n, t, pl.ds(8, 64), :], sems.at[len(copies)])
            )
    for copy in copies:
        copy.start()
    copies[0].wait()
    copies[1].wait()
    values = [table[n] for n in range(BLOCKS)]

    def look_up(k):
        stores = []
        for d in range(2):
            for t in range(2):
                index = blocks[d, tile_rows(k), 128 * t : 128 * t + 128]
                level = values
                bit = 1
                while len(level) > 1:
                    odd = (index & bit) != 0
                    level = [
                        jnp.where(odd, level[2 * n + 1], level[2 * n])
                        for n in range(len(level) // 2)
                    ]
                    bit *= 2
                stores.append((own, (d, t, tile_rows(k, 8)), level[0]))
        return stores

    tile_loop(0, 8, 1, look_up)
    for copy in copies[2:]:
        copy.wait()
    even = (place[1] & 1) == 0

    def pack(k):
        lane = lanes()
        stores = []
        right_edge = jnp.zeros((8, 128), F32)
        left_edge = jnp.zeros((8, 128), F32)
        for n in range(19):
            h, at = STRIP_H[n], STRIP_AT[n]
            here = (lane >= at) & (lane < at + h)
            tiles = [own[n, t, tile_rows(k, 8), :] for t in range(2)]
            left_edge = jnp.where(here, rolled(tiles[0], at, 1), left_edge)
            right_edge = jnp.where(here, rolled(tiles[1], at - (128 - h), 1), right_edge)
        stores.append((to_a, (tile_rows(k),), jnp.where(even, right_edge, left_edge)))
        stores.append((to_b, (tile_rows(k),), jnp.where(even, left_edge, right_edge)))
        return stores

    tile_loop(0, 8, 2, pack)


def sides(place, axis, from_a, from_b, rows):
    even = (place[axis] & 1) == 0
    a, b = from_a[rows, :], from_b[rows, :]
    return jnp.where(even, a, b), jnp.where(even, b, a)


def mirror_into(out, own, planes):
    def flip(k):
        return [
            (out, (slot, t, tile_rows(7 - k)), mirrored(own[n, t, tile_rows(k, 8), :]))
            for slot, n in enumerate(planes)
            for t in range(2)
        ]

    tile_loop(0, 8, 2, flip)


def deep_kernel(own, out):
    mirror_into(out, own, (0, 1, 2))


def layers_kernel(own, row_a, deep_in, sensor_out, peak_out):
    mirror_into(sensor_out, own, (4, 5, 6, 8, 9, 10))
    mirror_into(peak_out, own, (12, 13, 14, 16, 17, 18))


def row_kernel(place, own, col_a, col_b, deep_out, to_a, to_b):
    even = (place[0] & 1) == 0
    row = sublanes()
    strips = []
    for first in (0, 56):
        rows = slice(first, first + 8)
        right, left = sides(place, 1, col_a, col_b, rows)

        def tile(n, t):
            if t < 2:
                return own[n, t, first + 8 : first + 16, :]
            return ring_tile(right, left, n)

        strip = []
        for t in range(3):
            for n in range(3):
                strip.append(tile(n, t))
            for m in range(8):
                x, y = tile(3 + 2 * m, t), tile(4 + 2 * m, t)
                if first == 0:
                    strip.append(jnp.where(row < 4, x, rolled(y, 4, 0)))
                else:
                    strip.append(jnp.where(row >= 4, x, rolled(y, -4, 0)))
        strips.append(strip)
    top, bottom = strips
    for n in range(33):
        rows = slice(8 * n, 8 * n + 8)
        to_a[rows, :] = jnp.where(even, bottom[n], top[n])
        to_b[rows, :] = jnp.where(even, top[n], bottom[n])


def build_kernel(place, start, col_a, col_b, row_a, row_b, own, message):
    def core(k):
        right, left = sides(place, 1, col_a, col_b, tile_rows(k))
        return [(own, (n, 2, tile_rows(k, 8)), ring_tile(right, left, n)) for n in range(19)]

    tile_loop(0, 8, 2, core)
    for t in range(3):
        for n in range(11):
            at = 8 * (11 * t + n)
            below, above = sides(place, 0, row_a, row_b, slice(at, at + 8))
            if n < 3:
                own[n, t, 0:8, :] = above
                own[n, t, 72:80, :] = below
            else:
                m = 3 + 2 * (n - 3)
                own[m, t, 0:8, :] = above
                own[m, t, 72:80, :] = below
                own[m + 1, t, 0:8, :] = rolled(above, 4, 0)
                own[m + 1, t, 72:80, :] = rolled(below, -4, 0)

    planes = [0, 1, 2]
    for field in range(2):
        for d in range(2):
            planes += [3 + 8 * field + 4 * d + 3, 3 + 8 * field + 4 * d + 2]

    def pack(k):
        lane = lanes()
        column = jnp.zeros((8, 128), F32)
        for slot, n in enumerate(planes):
            h, at = PART_H[slot], PART_AT[slot]
            here = (lane >= at) & (lane < at + 2 * h)
            column = jnp.where(here, rolled(own[n, 2, tile_rows(k), :], at + h, 1), column)
        return [(message, (tile_rows(9 - k),), mirrored(column))]

    tile_loop(0, 10, 5, pack)
    row = sublanes()
    for n in range(3):
        for t in range(2):
            at = 80 + 16 * (2 * n + t)
            message[at : at + 8, :] = mirrored(own[n, t, 72:80, :])
            message[at + 8 : at + 16, :] = mirrored(own[n, t, 0:8, :])
    for field in range(2):
        for d in range(2):
            n = 3 + 8 * field + 4 * d
            for t in range(2):
                above = jnp.where(
                    row >= 4, own[n + 3, t, 0:8, :], rolled(own[n + 2, t, 0:8, :], 4, 0)
                )
                below = jnp.where(
                    row < 4, own[n + 3, t, 72:80, :], rolled(own[n + 2, t, 72:80, :], 4, 0)
                )
                at = 176 + 16 * (4 * field + 2 * d + t)
                message[at : at + 8, :] = mirrored(below)
                message[at + 8 : at + 16, :] = mirrored(above)


def partner_ring(message, slot, rows):
    h, at = PART_H[slot], PART_AT[slot]
    lane = lanes()
    return jnp.where(
        (lane < h) | (lane >= 128 - h), rolled(message[rows, :], -(at + h), 1), 0.0
    )


class Stores(list):
    def append(self, store):
        ref, index, value = store
        ref[index] = value

    def __iadd__(self, stores):
        for store in stores:
            self.append(store)
        return self


def tile_loop(start, stop, unroll, body):
    def step(j, _):
        stores = []
        for u in range(unroll):
            stores += body(start + unroll * j + u)
        for ref, index, value in stores:
            ref[index] = value
        return 0

    lax.fori_loop(0, (stop - start) // unroll, step, 0)


def tile_rows(k, add=0):
    return pl.ds(pl.multiple_of(8 * k + add, 8), 8)


class Solver:
    def __init__(self, place, tables, d, v, cond):
        self.place, self.d, self.v, self.cond = place, d, v, cond
        layer_class, share, lateral, vertical, sink = tables
        self.coef = []
        for side in range(2):
            die = d if side == 0 else 1 - d
            classes = [layer_class[die, l] for l in range(4)]
            coefs = []
            for l in range(4):
                g = lateral[classes[l]]
                up = vertical[classes[l]] if l < 3 else jnp.float32(0)
                down = vertical[classes[l - 1]] if l > 0 else jnp.float32(0)
                diagonal = 4 * g + up + down
                if l == 0:
                    diagonal = diagonal + sink[die]
                part = share[classes[l]] if share is not None else None
                if l < 3:
                    inverse = 1.0 / jnp.full((8, 128), diagonal, F32)
                    scale = inverse if part is None else inverse * part
                    coefs.append((scale, g * inverse, up * inverse, down * inverse))
                else:
                    coefs.append((diagonal, g, down, part))
            self.coef.append(coefs)
        gy = place[1]
        right = jnp.where(gy == 15, 0.0, 1.0).astype(F32)
        left = jnp.where(gy == 0, 0.0, 1.0).astype(F32)
        self.ring = jnp.where(lanes() < 64, right, left)

    def scaled(self, side, l, t, k, s):
        coef = self.coef[side][l]
        if l < 3:
            s = s * coef[0]
        else:
            if coef[3] is not None:
                s = s * coef[3]
            s = s * self.cond[self.d, 1 + side, t, tile_rows(k)]
        return s * self.ring if t == 2 else s


def prepare(solvers, bond_tile):
    def body(k):
        stores = []
        for solver in solvers:
            for t in range(3):
                bond = bond_tile(solver.d, k, t)
                stores.append((solver.cond, (solver.d, 0, t, tile_rows(k)), bond))
                for side in range(2):
                    value = 1.0 / (solver.coef[side][3][0] + bond)
                    stores.append((solver.cond, (solver.d, 1 + side, t, tile_rows(k)), value))
        return stores

    tile_loop(0, 10, 2, body)


def zero_outside(place, written):
    zero = jnp.zeros((8, 128), F32)
    for here, first in ((place[0] == 0, 8), (place[0] == 15, 80)):

        @pl.when(here)
        def _():
            for ref, at in written:
                for t in range(3):
                    ref[(*at, t, slice(first, first + 8))] = zero


def first(work, unroll=5):
    def body(k):
        stores = []
        for solver, side, layers, source in work:
            for t in range(3):
                shared = {}
                for l in layers:
                    value = solver.scaled(side, l, t, k, source(l, t, tile_rows(k), shared))
                    at = (solver.d, 0, l, t, tile_rows(k, 8))
                    stores.append((solver.v[side], at, value))
        return stores

    tile_loop(0, 10, unroll, body)
    written = [(o.v[side], (o.d, 0, l)) for o, side, layers, _ in work for l in layers]
    zero_outside(work[0][0].place, written)


def sweep(b, work, core_only=False, unroll=5):
    def body(k):
        stores = Stores()
        rows, to = tile_rows(k), tile_rows(k, 8)
        lane = lanes()
        first_lane, last_lane = lane == 0, lane == 127
        seen = {}

        for solver, side, layers, source, emit in work:
            v, d, cond = solver.v, solver.d, solver.cond

            def value(side, l, t):
                key = (id(v[side]), d, l, t)
                if key not in seen:
                    seen[key] = v[side][d, b, l, t, to, :]
                return seen[key]

            shared = {}
            for l in layers:
                coef = solver.coef[side][l]
                forward = [pltpu.roll(value(side, l, t), 1, 1) for t in range(3)]
                backward = [pltpu.roll(value(side, l, t), 127, 1) for t in range(3)]
                for t in range(2 if core_only else 3):
                    left = jnp.where(first_lane, forward[t - 1], forward[t])
                    right = jnp.where(last_lane, backward[(t + 1) % 3], backward[t])
                    around = (left + right) + (
                        v[side][d, b, l, t, pl.ds(8 * k + 7, 8), :]
                        + v[side][d, b, l, t, pl.ds(8 * k + 9, 8), :]
                    )
                    s = source(l, t, rows, shared)
                    if l < 3:
                        total = s * coef[0] + coef[1] * around
                        total = total + coef[2] * value(side, l + 1, t)
                        if l > 0:
                            total = total + coef[3] * value(side, l - 1, t)
                    else:
                        if coef[3] is not None:
                            s = s * coef[3]
                        total = (s + coef[1] * around) + coef[2] * value(side, 2, t)
                        total = total + cond[d, 0, t, rows] * value(1 - side, 3, t)
                        total = total * cond[d, 1 + side, t, rows]
                    if t == 2:
                        total = total * solver.ring
                    if emit is None:
                        stores.append((v[side], (d, 1 - b, l, t, to), total))
                    else:
                        stores += emit(l, t, k, total)
        return stores

    if core_only:
        tile_loop(1, 9, unroll, body)
    else:
        tile_loop(0, 10, unroll, body)
        written = [
            (o.v[side], (o.d, 1 - b, l))
            for o, side, layers, _, emit in work
            if emit is None
            for l in layers
        ]
        if written:
            zero_outside(work[0][0].place, written)


def place_other(planes, layers_in, message, field, d):
    other = 1 - d
    zero = jnp.zeros((8, 128), F32)

    def body(k):
        return [
            (planes, (d, l, t, tile_rows(k, 8)), layers_in(3 * other + l, t, tile_rows(k)))
            for l in range(3)
            for t in range(2)
        ]

    tile_loop(0, 8, 4, body)

    def ring(k):
        column = message[tile_rows(k), :]
        lane = lanes()
        stores = [(planes, (d, 0, 2, tile_rows(k)), zero)]
        for slot_in, l, h in ((0, 2, 2), (1, 1, 1)):
            at = PART_AT[3 + 4 * field + 2 * other + slot_in] + h
            inside = (lane < h) | (lane >= 128 - h)
            tile = jnp.where(inside, rolled(column, -at, 1), 0.0)
            stores.append((planes, (d, l, 2, tile_rows(k)), tile))
        return stores

    tile_loop(0, 10, 5, ring)
    for t in range(2):
        planes[d, 0, t, 0:8, :] = zero
        planes[d, 0, t, 72:80, :] = zero
        at = 176 + 64 * field + 32 * other + 16 * t
        above = message[at : at + 8, :]
        below = message[at + 8 : at + 16, :]
        planes[d, 2, t, 0:8, :] = above
        planes[d, 2, t, 72:80, :] = below
        planes[d, 1, t, 0:8, :] = rolled(above, 4, 0)
        planes[d, 1, t, 72:80, :] = rolled(below, -4, 0)


def place_deep(planes, deep_in, message):
    def body(k):
        return [
            (planes, (n, t, tile_rows(k, 8)), deep_in[n, t, tile_rows(k), :])
            for n in range(3)
            for t in range(2)
        ]

    tile_loop(0, 8, 4, body)

    def ring(k):
        return [
            (planes, (n, 2, tile_rows(k)), partner_ring(message, n, tile_rows(k)))
            for n in range(3)
        ]

    tile_loop(0, 10, 5, ring)
    for n in range(3):
        for t in range(2):
            at = 80 + 16 * (2 * n + t)
            planes[n, t, 0:8, :] = message[at : at + 8, :]
            planes[n, t, 72:80, :] = message[at + 8 : at + 16, :]


EVERY = (0, 1, 2, 3)


def shared_source(ref, *at):
    def source(l, t, rows, shared):
        if t not in shared:
            shared[t] = ref[(*at, t, rows)]
        return shared[t]

    return source


def layer_source(ref, first_layer, *at):
    def source(l, t, rows, shared):
        *head, last = at
        return ref[(*head, last + l - first_layer, t, rows)]

    return source


def thermal_sensor_kernel(
    place, layer_class, share, lateral, vertical, sink, own, deep_in, sensor_in, message,
    thermal, sensed, heat, weighted, early, cond, v_peak,
    v_own, v_other, s_own, s_other, planes, deep, block, sems,
):
    place_deep(deep, deep_in, message)
    plain = (layer_class, None, lateral, vertical, sink)
    with_share = (layer_class, share, lateral, vertical, sink)
    both = range(2)
    hot = [Solver(place, with_share, d, (v_own, v_other), cond) for d in both]
    sense = [Solver(place, plain, d, (s_own, s_other), cond) for d in both]
    weigh = [Solver(place, plain, d, (v_peak, None), cond) for d in both]
    prepare(hot, lambda d, k, t: (own if d == 0 else deep)[2, t, tile_rows(k), :])

    def layers_in(n, t, rows):
        return sensor_in[n, t, rows, :]

    for d in both:
        place_other(planes, layers_in, message, 0, d)
    own_power = [shared_source(own, d) for d in both]
    their_power = [shared_source(deep, 1 - d) for d in both]
    own_sensor = [layer_source(own, 0, 3 + 4 * d) for d in both]
    their_sensor = [layer_source(planes, 1, d, 0) for d in both]
    own_peak = [layer_source(weighted, 0, d, 0) for d in both]

    first(
        [(hot[d], 0, EVERY, own_power[d]) for d in both]
        + [(hot[d], 1, EVERY, their_power[d]) for d in both]
        + [(sense[d], 0, EVERY, own_sensor[d]) for d in both]
        + [(sense[d], 1, (1, 2, 3), their_sensor[d]) for d in both]
    )
    for b, reach in ((0, (2, 3)), (1, (3,))):
        sweep(
            b,
            [(hot[d], 0, EVERY, own_power[d], None) for d in both]
            + [(hot[d], 1, EVERY, their_power[d], None) for d in both]
            + [(sense[d], 0, EVERY, own_sensor[d], None) for d in both]
            + [(sense[d], 1, reach, their_sensor[d], None) for d in both],
        )

    def emit_own(d):
        def emit(l, t, k, total):
            peak = own[11 + 4 * d + l, t, tile_rows(k), :]
            stores = [(weighted, (d, l, t, tile_rows(k)), total * peak)]
            if t < 2:
                stores.append((v_own, (d, 1, l, t, tile_rows(k, 8)), total))
            return stores

        return emit

    def emit_other(d):
        return lambda l, t, k, total: [(heat, (d, l - 1, t, tile_rows(k)), total)]

    def emit_block(d):
        return lambda l, t, k, total: [(block, (d, l, t, tile_rows(k, -8)), total)]

    def emit_early(d):
        return lambda l, t, k, total: [(early, (d, t, tile_rows(k, -8)), total)]

    sweep(
        0,
        [(hot[d], 0, EVERY, own_power[d], emit_own(d)) for d in both]
        + [(hot[d], 1, (1, 2, 3), their_power[d], emit_other(d)) for d in both],
    )
    copies = []

    def send(source, out, d, l, t):
        to = out.at[d, l, :, pl.ds(128 * t, 128)]
        copies.append(pltpu.make_async_copy(source, to, sems.at[len(copies)]))
        copies[-1].start()

    for d in both:
        for l in EVERY:
            for t in range(2):
                send(v_own.at[d, 1, l, t, pl.ds(16, 64), :], thermal, d, l, t)
    sweep(
        0,
        [(sense[d], 0, EVERY, own_sensor[d], emit_block(d)) for d in both],
        core_only=True,
        unroll=4,
    )
    for d in both:
        for l in EVERY:
            for t in range(2):
                send(block.at[d, l, t], sensed, d, l, t)
    first([(weigh[d], 0, EVERY, own_peak[d]) for d in both], unroll=5)
    sweep(0, [(weigh[d], 0, (0, 1, 2), own_peak[d], None) for d in both], unroll=5)
    sweep(1, [(weigh[d], 0, (0, 1), own_peak[d], None) for d in both], unroll=5)
    sweep(
        0,
        [(weigh[d], 0, (0,), own_peak[d], emit_early(d)) for d in both],
        core_only=True,
        unroll=4,
    )
    for copy in copies:
        copy.wait()


def peak_kernel(
    place, layer_class, lateral, vertical, sink, peak_in, message, heat, weighted, early, cond,
    v_start, out, v_peak, v_other, planes, block, sems,
):
    plain = (layer_class, None, lateral, vertical, sink)
    both = range(2)
    copies = []

    def send(source, d, l, t):
        to = out.at[d, l, :, pl.ds(128 * t, 128)]
        copies.append(pltpu.make_async_copy(source, to, sems.at[len(copies)]))
        copies[-1].start()

    for d in both:
        for t in range(2):
            send(early.at[d, t], d, 0, t)
    solver = [Solver(place, plain, d, (v_peak, v_other), cond) for d in both]

    def layers_in(n, t, rows):
        return peak_in[n, t, rows, :]

    for d in both:
        place_other(planes, layers_in, message, 1, d)
    own_peak = [layer_source(weighted, 0, d, 0) for d in both]

    def their_peak(d):
        def source(l, t, rows, shared):
            return planes[d, l - 1, t, rows, :] * heat[d, l - 1, t, rows, :]

        return source

    def emit_block(d):
        return lambda l, t, k, total: [(block, (d, l - 1, t, tile_rows(k, -8)), total)]

    first([(solver[d], 1, (1, 2, 3), their_peak(d)) for d in both], unroll=5)
    sweep(
        0,
        [(solver[d], 0, (3,), own_peak[d], None) for d in both]
        + [(solver[d], 1, (2, 3), their_peak(d), None) for d in both],
        unroll=5,
    )
    sweep(
        1,
        [(solver[d], 0, (2, 3), own_peak[d], None) for d in both]
        + [(solver[d], 1, (3,), their_peak(d), None) for d in both],
        unroll=5,
    )
    for d in both:
        sweep(
            0,
            [(solver[d], 0, (1, 2, 3), own_peak[d], emit_block(d))],
            core_only=True,
            unroll=4,
        )
        for l in (1, 2, 3):
            for t in range(2):
                send(block.at[d, l - 1, t], d, l, t)
    for copy in copies:
        copy.wait()


PLANES = (19, 3, ROWS, 128)
FIELD = (2, 4, 64, 256)
V = (2, 2, 4, 3, ROWS + 16, 128)
OTHER = (2, 3, 3, ROWS, 128)
DEEP_PLANES = (3, 3, ROWS, 128)
KEPT = [
    (2, 3, 3, ROWS, 128),
    (2, 4, 3, ROWS, 128),
    (2, 2, 64, 128),
    (2, 3, 3, ROWS, 128),
    V,
]


def call(kernel, tables, arrays, outs, scratch=(), flops=0, aliases={}, hbm=0, hbm_out=0, vmem=16, name=None):
    shapes = [jax.ShapeDtypeStruct(shape, F32) for shape in outs]
    arrays = [
        pltpu.with_memory_space_constraint(x, pltpu.HBM) if i < hbm else x
        for i, x in enumerate(arrays)
    ]
    anywhere = pl.BlockSpec(memory_space=pltpu.HBM)
    return pl.pallas_call(
        kernel,
        out_shape=shapes,
        in_specs=[SMEM] * len(tables) + [anywhere] * hbm + [VMEM] * (len(arrays) - hbm),
        out_specs=[anywhere] * hbm_out + [VMEM] * (len(shapes) - hbm_out),
        scratch_shapes=[pltpu.VMEM(x, F32) if isinstance(x, tuple) else x for x in scratch],
        input_output_aliases={len(tables) + i: o for i, o in aliases.items()},
        compiler_params=pltpu.CompilerParams(vmem_limit_bytes=vmem << 20),
        cost_estimate=pl.CostEstimate(flops=flops, bytes_accessed=1024, transcendentals=0),
        name=name,
    )(*tables, *arrays)


def pairs(count, odd):
    if odd:
        return [(i, ((i - 1) ^ 1) + 1) for i in range(1, count - 1)]
    return [(i, i ^ 1) for i in range(count)]


def local(
    block_ids,
    block_power,
    layer_class,
    power_share,
    lateral_k,
    vertical_k,
    sink_conductance,
    bond_conductance,
    peak_factors,
    sensor_weight,
):
    nx, ny = lax.axis_size("gx"), lax.axis_size("gy")
    facing = [(i, nx - 1 - i) for i in range(nx)]
    place = jnp.stack([lax.axis_index("gx"), lax.axis_index("gy")]).astype(jnp.int32)
    own, col_a, col_b = call(
        gather_kernel,
        (place,),
        (block_power, block_ids, bond_conductance, sensor_weight, peak_factors),
        [PLANES, (64, 128), (64, 128)],
        [
            pltpu.SMEM((BLOCKS,), F32),
            pltpu.VMEM((2, 64, 256), jnp.int32),
            pltpu.SemaphoreType.DMA((36,)),
        ],
        hbm=5,
        name="gather",
    )
    col_a = lax.ppermute(col_a, "gy", pairs(ny, False))
    col_b = lax.ppermute(col_b, "gy", pairs(ny, True))
    (deep_out,) = call(
        deep_kernel, (), (own,), [(3, 2, 64, 128)], flops=10**11, name="deep_out"
    )
    deep_in = lax.ppermute(deep_out, "gx", facing)
    row_a, row_b = call(
        row_kernel, (place,), (own, col_a, col_b, deep_out), [(264, 128), (264, 128)], flops=10**11, name="rows"
    )
    layers = (6, 2, 64, 128)
    sensor_out, peak_out = call(
        layers_kernel, (), (own, row_a, deep_in), [layers, layers], flops=10**11, name="layers_out"
    )
    row_a = lax.ppermute(row_a, "gx", pairs(nx, False))
    row_b = lax.ppermute(row_b, "gx", pairs(nx, True))
    sensor_in = lax.ppermute(sensor_out, "gx", facing)
    own, message = call(
        build_kernel,
        (place,),
        (own, col_a, col_b, row_a, row_b),
        [PLANES, (304, 128)],
        aliases={0: 0},
        flops=10**11,
        name="build",
    )
    peak_out, _ = lax.optimization_barrier((peak_out, message))
    message = lax.ppermute(message, "gx", facing)
    peak_in = lax.ppermute(peak_out, "gx", facing)
    thermal, sensed, *kept = call(
        thermal_sensor_kernel,
        (place, layer_class, power_share, lateral_k, vertical_k, sink_conductance),
        (own, deep_in, sensor_in, message),
        [FIELD, FIELD] + KEPT,
        [V, V, V, V, OTHER, DEEP_PLANES, (2, 4, 2, 64, 128), pltpu.SemaphoreType.DMA((32,))],
        flops=10**11,
        hbm_out=2,
        vmem=24,
        name="thermal_sensor",
    )
    peak, _ = call(
        peak_kernel,
        (place, layer_class, lateral_k, vertical_k, sink_conductance),
        (peak_in, message, *kept),
        [FIELD, V],
        [V, OTHER, (2, 3, 2, 64, 128), pltpu.SemaphoreType.DMA((16,))],
        aliases={6: 1},
        hbm_out=1,
        name="peak",
    )
    return thermal, peak, sensed


def solution(mesh):
    return jax.shard_map(
        local,
        mesh=mesh,
        in_specs=(
            P(None, "gx", "gy"),
            P(),
            P(),
            P(),
            P(),
            P(),
            P(),
            P("gx", "gy"),
            P(None, None, "gx", "gy"),
            P(None, None, "gx", "gy"),
        ),
        out_specs=(P(None, None, "gx", "gy"),) * 3,
        check_vma=False,
    )
```

time: 66.6 us -> 52.3 us (0.79)
  the two profiles are of different devices: /device:TPU:144 before, /device:TPU:111 now
where the time goes in v4:
time: 52.3 us; the launch traced here: 51.9 us
  starting transfers between devices  21.7 us (41%)
  Pallas kernels  17.9 us (34%)
  waiting for transfers between devices  11.4 us (22%)
  between operations  0.79 us (2%)
    pallas_call x7, Pallas kernels, call(): pl.pallas_call(kernel, out_shape=shapes, in_specs=[SMEM] * len(tables) +...  17.9 us
    ppermute x1, waiting for transfers between devices, local(): message = lax.ppermute(message, 'gx', facing)  8.77 us
    ppermute x1, starting transfers between devices, local(): col_b = lax.ppermute(col_b, 'gy', pairs(ny, True))  5.76 us
    ppermute x1, starting transfers between devices, local(): row_b = lax.ppermute(row_b, 'gx', pairs(nx, True))  4.28 us
    ppermute x1, starting transfers between devices, local(): deep_in = lax.ppermute(deep_out, 'gx', facing)  3.14 us
    ppermute x1, starting transfers between devices, local(): peak_in = lax.ppermute(peak_out, 'gx', facing)  2.81 us
    ppermute x1, starting transfers between devices, local(): sensor_in = lax.ppermute(sensor_out, 'gx', facing)  2.78 us
    ppermute x1, starting transfers between devices, local(): message = lax.ppermute(message, 'gx', facing)  2.64 us
  transfers between devices with their start and end apart: 8, of which 3 were waited for; matrix products, arithmetic and copies ran while one was open for 0% of the time, Pallas kernels for 22%

profile of v4, /device:TPU:111, one launch (start us, length us, event | category | flops | bytes accessed | tf_op | source)
XLA Modules:
  0.0 51.9 jit_solution(1128374611939864028)
XLA Ops:
  0.6 0.1 pad_add_fusion.place
  0.7 2.7 %gather.1 = (f32[19,3,80,128]{3,2,1,0:T(8,128)S(1)}, f32[64,128]{1,0:T(8,128)S(1)}, f32[64,128]{1,0:T(8,128)S(1)}) custom-call(s32[2]{0:T(128)S(1)} %pad_add_fusion.place, f32[32]{0:T(128)} %block_power.1, s32[2,64,256]{2,1,0:T(8,128)} %ids.1, f32[64,256]{1,0:T(8,128)} %bond.1, f32[2,4,64,256]{3,2,1,0:T(8,128)} %sensor.1, f32[2,4,64,256]{3,2,1,0:T(8,128)} %peak.2), custom_call_target="tpu_custom_call" | custom-call | bytes 1024 | tf_op jit(solution)/shard_map/gather/pallas_call | solution.py:671
  3.4 0.3 collective-permute-start
  3.6 5.8 %collective-permute-start.1 = (f32[64,128]{1,0:T(8,128)S(1)}, f32[64,128]{1,0:T(8,128)S(1)}, u32[]{:S(2)}, u32[]{:S(2)}) collective-permute-start(f32[64,128]{1,0:T(8,128)S(1)} %get-tuple-element.23), channel_id=1, source_target_pairs={{1,2},{2,1},{3,4},{4,3},{5,6},{6,5},{7,8},{8,7},{9,10},{10,9},{11,... | collective-permute-start | bytes 98312 | tf_op jit(solution)/shard_map/ppermute | solution.py:719
  9.4 3.1 %collective-permute-start.4 = (f32[3,2,64,128]{3,2,1,0:T(8,128)S(1)}, f32[3,2,64,128]{3,2,1,0:T(8,128)S(1)}, u32[]{:S(2)}, u32[]{:S(2)}) collective-permute-start(f32[3,2,64,128]{3,2,1,0:T(8,128)S(1)} %deep_out.1), channel_id=1, source_target_pairs={{0,240},{16,224},{32,208},{48,192},{64,176},{80,160},{96,144},{112... | collective-permute-start | bytes 589832 | tf_op jit(solution)/shard_map/ppermute | solution.py:723
  12.6 0.0 collective-permute-done.col_a
  12.6 0.0 collective-permute-done.1.col_b
  12.6 0.7 %rows.1 = (f32[264,128]{1,0:T(8,128)S(1)}, f32[264,128]{1,0:T(8,128)S(1)}) custom-call(s32[2]{0:T(128)S(1)} %pad_add_fusion.place, f32[19,3,80,128]{3,2,1,0:T(8,128)S(1)} %get-tuple-element.21.own.start, f32[64,128]{1,0:T(8,128)S(1)} %collective-permute-done.col_a, f32[64,128]{1,0:T(8,128)S(1)} %collective-permute-done.1.col_b, f32[3,2,64,128]{3,2,1,0:T(8,128)S(1)} %deep_out.1), custom_call_target="tpu_custom_call" | custom-call | flops 99999997952 | bytes 1024 | tf_op jit(solution)/shard_map/rows/pallas_call | solution.py:671
  13.3 4.3 %collective-permute-start.3 = (f32[264,128]{1,0:T(8,128)S(1)}, f32[264,128]{1,0:T(8,128)S(1)}, u32[]{:S(2)}, u32[]{:S(2)}) collective-permute-start(f32[264,128]{1,0:T(8,128)S(1)} %get-tuple-element.25), channel_id=1, source_target_pairs={{16,32},{32,16},{48,64},{64,48},{80,96},{96,80},{112,128},{128,112... | collective-permute-start | bytes 405512 | tf_op jit(solution)/shard_map/ppermute | solution.py:732
  17.6 0.1 collective-permute-start.2
  17.7 2.5 %collective-permute-done.4.deep_in = f32[3,2,64,128]{3,2,1,0:T(8,128)S(1)} collective-permute-done((f32[3,2,64,128]{3,2,1,0:T(8,128)S(1)}, f32[3,2,64,128]{3,2,1,0:T(8,128)S(1)}, u32[]{:S(2)}, u32[]{:S(2)}) %collective-permute-start.4) | collective-permute-done | bytes 196640 | tf_op jit(solution)/shard_map/ppermute | solution.py:723
  20.2 0.1 layers_out.1
  20.3 0.0 copy-start
  20.3 0.0 copy-start.1
  20.3 0.0 copy-start.2
  20.3 0.0 copy-start.3
  20.3 0.0 copy-start.4
  20.3 2.8 %collective-permute-start.5 = (f32[6,2,64,128]{3,2,1,0:T(8,128)S(1)}, f32[6,2,64,128]{3,2,1,0:T(8,128)S(1)}, u32[]{:S(2)}, u32[]{:S(2)}) collective-permute-start(f32[6,2,64,128]{3,2,1,0:T(8,128)S(1)} %get-tuple-element.27), channel_id=1, source_target_pairs={{0,240},{16,224},{32,208},{48,192},{64,176},{80,160},{96,144},{112... | collective-permute-start | bytes 1179656 | tf_op jit(solution)/shard_map/ppermute | solution.py:733
  23.1 0.1 collective-permute-done.3.row_b
  23.2 0.0 collective-permute-done.2.row_a
  23.2 1.4 %build.1 = (f32[19,3,80,128]{3,2,1,0:T(8,128)S(1)}, f32[304,128]{1,0:T(8,128)S(1)}) custom-call(s32[2]{0:T(128)S(1)} %pad_add_fusion.place, f32[19,3,80,128]{3,2,1,0:T(8,128)S(1)} %get-tuple-element.21.own.start, f32[64,128]{1,0:T(8,128)S(1)} %collective-permute-done.col_a, ...), custom_call_target="tpu_custom_call", output_to_operand_aliasing={{0}: (1, {})} | custom-call | flops 99999997952 | bytes 1024 | tf_op jit(solution)/shard_map/build/pallas_call | solution.py:671
  24.7 2.6 %collective-permute-start.6 = (f32[304,128]{1,0:T(8,128)S(1)}, f32[304,128]{1,0:T(8,128)S(1)}, u32[]{:S(2)}, u32[]{:S(2)}) collective-permute-start(f32[304,128]{1,0:T(8,128)S(1)} %get-tuple-element.28), channel_id=1, source_target_pairs={{0,240},{16,224},{32,208},{48,192},{64,176},{80,160},{96,144},{112... | collective-permute-start | bytes 466952 | tf_op jit(solution)/shard_map/ppermute | solution.py:744
  27.3 2.8 %collective-permute-start.7 = (f32[6,2,64,128]{3,2,1,0:T(8,128)S(1)}, f32[6,2,64,128]{3,2,1,0:T(8,128)S(1)}, u32[]{:S(2)}, u32[]{:S(2)}) collective-permute-start(f32[6,2,64,128]{3,2,1,0:T(8,128)S(1)} %get-tuple-element.31), channel_id=1, source_target_pairs={{0,240},{16,224},{32,208},{48,192},{64,176},{80,160},{96,144},{112... | collective-permute-start | bytes 1179656 | tf_op jit(solution)/shard_map/ppermute | solution.py:745
  30.1 8.8 %collective-permute-done.6.message = f32[304,128]{1,0:T(8,128)S(1)} collective-permute-done((f32[304,128]{1,0:T(8,128)S(1)}, f32[304,128]{1,0:T(8,128)S(1)}, u32[]{:S(2)}, u32[]{:S(2)}) %collective-permute-start.6) | collective-permute-done | bytes 155680 | tf_op jit(solution)/shard_map/ppermute | solution.py:744
  38.9 0.0 collective-permute-done.5.sensor_in
  38.9 0.0 copy-done
  38.9 0.0 copy-done.1
  38.9 0.0 copy-done.2
  38.9 0.0 copy-done.3
  38.9 0.0 copy-done.4
  38.9 9.2 %thermal_sensor.1 = (f32[2,4,64,256]{3,2,1,0:T(8,128)}, f32[2,4,64,256]{3,2,1,0:T(8,128)}, f32[2,3,3,80,128]{4,3,2,1,0:T(8,128)S(1)}, f32[2,4,3,80,128]{4,3,2,1,...) custom-call(s32[2]{0:T(128)S(1)} %pad_add_fusion.place, ...), custom_call_target="tpu_custom_call" | custom-call | flops 99999997952 | bytes 1024 | tf_op jit(solution)/shard_map/thermal_sensor/pallas_call | solution.py:671
  48.2 0.0 collective-permute-done.7.peak_in
  48.2 3.7 %peak.3 = (f32[2,4,64,256]{3,2,1,0:T(8,128)}, f32[2,2,4,3,96,128]{5,4,3,2,1,0:T(8,128)S(1)}) custom-call(s32[2]{0:T(128)S(1)} %pad_add_fusion.place, s32[2,4]{1,0:T(2,128)S(1)} %copy-done, f32[4]{0:T(128)S(1)} %copy-done.1, f32[4]{0:T(128)S(1)} %copy-done.2, f32[2]{0:T(128)S(1)} %copy-done.3, ...), custom_call_target="tpu_custom_call", output_to_operand_aliasing={{1}: (11, {})} | custom-call | bytes 1024 | tf_op jit(solution)/shard_map/peak/pallas_call | solution.py:671
  (1 shorter events, 0.0 us)
Async XLA Ops:
  3.4 9.2 %collective-permute-start = (f32[64,128]{1,0:T(8,128)S(1)}, f32[64,128]{1,0:T(8,128)S(1)}, u32[]{:S(2)}, u32[]{:S(2)}) collective-permute-start(f32[64,128]{1,0:T(8,128)S(1)} %get-tuple-element.22), channel_id=1, source_target_pairs={{0,1},{1,0},{2,3},{3,2},{4,5},{5,4},{6,7},{7,6},{8,9},{9,8},{10,11... | collective-permute-start | bytes 98312 | tf_op jit(solution)/shard_map/ppermute | solution.py:718
  3.6 8.9 %collective-permute-start.1 = (f32[64,128]{1,0:T(8,128)S(1)}, f32[64,128]{1,0:T(8,128)S(1)}, u32[]{:S(2)}, u32[]{:S(2)}) collective-permute-start(f32[64,128]{1,0:T(8,128)S(1)} %get-tuple-element.23), channel_id=1, source_target_pairs={{1,2},{2,1},{3,4},{4,3},{5,6},{6,5},{7,8},{8,7},{9,10},{10,9},{11,... | collective-permute-start | bytes 98312 | tf_op jit(solution)/shard_map/ppermute | solution.py:719
  9.4 10.7 %collective-permute-start.4 = (f32[3,2,64,128]{3,2,1,0:T(8,128)S(1)}, f32[3,2,64,128]{3,2,1,0:T(8,128)S(1)}, u32[]{:S(2)}, u32[]{:S(2)}) collective-permute-start(f32[3,2,64,128]{3,2,1,0:T(8,128)S(1)} %deep_out.1), channel_id=1, source_target_pairs={{0,240},{16,224},{32,208},{48,192},{64,176},{80,160},{96,144},{112... | collective-permute-start | bytes 589832 | tf_op jit(solution)/shard_map/ppermute | solution.py:723
  13.3 9.9 %collective-permute-start.3 = (f32[264,128]{1,0:T(8,128)S(1)}, f32[264,128]{1,0:T(8,128)S(1)}, u32[]{:S(2)}, u32[]{:S(2)}) collective-permute-start(f32[264,128]{1,0:T(8,128)S(1)} %get-tuple-element.25), channel_id=1, source_target_pairs={{16,32},{32,16},{48,64},{64,48},{80,96},{96,80},{112,128},{128,112... | collective-permute-start | bytes 405512 | tf_op jit(solution)/shard_map/ppermute | solution.py:732
  17.6 5.7 %collective-permute-start.2 = (f32[264,128]{1,0:T(8,128)S(1)}, f32[264,128]{1,0:T(8,128)S(1)}, u32[]{:S(2)}, u32[]{:S(2)}) collective-permute-start(f32[264,128]{1,0:T(8,128)S(1)} %get-tuple-element.24.row_a), channel_id=1, source_target_pairs={{0,16},{16,0},{32,48},{48,32},{64,80},{80,64},{96,112},{112,96},{1... | collective-permute-start | bytes 405512 | tf_op jit(solution)/shard_map/ppermute | solution.py:731
  20.3 18.6 %copy-start = (s32[2,4]{1,0:T(2,128)S(1)}, s32[2,4]{1,0:T(2,128)}, u32[]{:S(2)}) copy-start(s32[2,4]{1,0:T(2,128)} %layer_class.3) | copy-start | bytes 100
  20.3 18.6 %copy-start.1 = (f32[4]{0:T(128)S(1)}, f32[4]{0:T(128)}, u32[]{:S(2)}) copy-start(f32[4]{0:T(128)} %lateral.3) | copy-start | bytes 52
  20.3 18.6 %copy-start.2 = (f32[4]{0:T(128)S(1)}, f32[4]{0:T(128)}, u32[]{:S(2)}) copy-start(f32[4]{0:T(128)} %vertical.3) | copy-start | bytes 52
  20.3 18.6 %copy-start.3 = (f32[2]{0:T(128)S(1)}, f32[2]{0:T(128)}, u32[]{:S(2)}) copy-start(f32[2]{0:T(128)} %sink.3) | copy-start | bytes 28
  20.3 18.6 %copy-start.4 = (f32[4]{0:T(128)S(1)}, f32[4]{0:T(128)}, u32[]{:S(2)}) copy-start(f32[4]{0:T(128)} %share.1) | copy-start | bytes 52
  20.3 18.6 %collective-permute-start.5 = (f32[6,2,64,128]{3,2,1,0:T(8,128)S(1)}, f32[6,2,64,128]{3,2,1,0:T(8,128)S(1)}, u32[]{:S(2)}, u32[]{:S(2)}) collective-permute-start(f32[6,2,64,128]{3,2,1,0:T(8,128)S(1)} %get-tuple-element.27), channel_id=1, source_target_pairs={{0,240},{16,224},{32,208},{48,192},{64,176},{80,160},{96,144},{112... | collective-permute-start | bytes 1179656 | tf_op jit(solution)/shard_map/ppermute | solution.py:733
  24.7 14.2 %collective-permute-start.6 = (f32[304,128]{1,0:T(8,128)S(1)}, f32[304,128]{1,0:T(8,128)S(1)}, u32[]{:S(2)}, u32[]{:S(2)}) collective-permute-start(f32[304,128]{1,0:T(8,128)S(1)} %get-tuple-element.28), channel_id=1, source_target_pairs={{0,240},{16,224},{32,208},{48,192},{64,176},{80,160},{96,144},{112... | collective-permute-start | bytes 466952 | tf_op jit(solution)/shard_map/ppermute | solution.py:744
  27.3 20.9 %collective-permute-start.7 = (f32[6,2,64,128]{3,2,1,0:T(8,128)S(1)}, f32[6,2,64,128]{3,2,1,0:T(8,128)S(1)}, u32[]{:S(2)}, u32[]{:S(2)}) collective-permute-start(f32[6,2,64,128]{3,2,1,0:T(8,128)S(1)} %get-tuple-element.31), channel_id=1, source_target_pairs={{0,240},{16,224},{32,208},{48,192},{64,176},{80,160},{96,144},{112... | collective-permute-start | bytes 1179656 | tf_op jit(solution)/shard_map/ppermute | solution.py:745

commit v5 on v4

--- a/solution.py
+++ b/solution.py
@@ -90,7 +90,7 @@
                 stores.append((own, (d, t, tile_rows(k, 8)), level[0]))
         return stores
 
-    tile_loop(0, 8, 1, look_up)
+    tile_loop(0, 8, 2, look_up)
     for copy in copies[2:]:
         copy.wait()
     even = (place[1] & 1) == 0
@@ -110,7 +110,7 @@
         stores.append((to_b, (tile_rows(k),), jnp.where(even, left_edge, right_edge)))
         return stores
 
-    tile_loop(0, 8, 2, pack)
+    tile_loop(0, 8, 4, pack)
 
 
 def sides(place, axis, from_a, from_b, rows):
@@ -134,7 +134,7 @@
     mirror_into(out, own, (0, 1, 2))
 
 
-def layers_kernel(own, row_a, deep_in, sensor_out, peak_out):
+def layers_kernel(own, row_a, sensor_out, peak_out):
     mirror_into(sensor_out, own, (4, 5, 6, 8, 9, 10))
     mirror_into(peak_out, own, (12, 13, 14, 16, 17, 18))
 
@@ -170,12 +170,12 @@
         to_b[rows, :] = jnp.where(even, top[n], bottom[n])
 
 
-def build_kernel(place, start, col_a, col_b, row_a, row_b, own, message):
+def build_kernel(place, start, col_a, col_b, row_a, row_b, deep_in, own, message):
     def core(k):
         right, left = sides(place, 1, col_a, col_b, tile_rows(k))
         return [(own, (n, 2, tile_rows(k, 8)), ring_tile(right, left, n)) for n in range(19)]
 
-    tile_loop(0, 8, 2, core)
+    tile_loop(0, 8, 4, core)
     for t in range(3):
         for n in range(11):
             at = 8 * (11 * t + n)
@@ -726,7 +726,7 @@
     )
     layers = (6, 2, 64, 128)
     sensor_out, peak_out = call(
-        layers_kernel, (), (own, row_a, deep_in), [layers, layers], flops=10**11, name="layers_out"
+        layers_kernel, (), (own, row_a), [layers, layers], flops=10**11, name="layers_out"
     )
     row_a = lax.ppermute(row_a, "gx", pairs(nx, False))
     row_b = lax.ppermute(row_b, "gx", pairs(nx, True))
@@ -734,7 +734,7 @@
     own, message = call(
         build_kernel,
         (place,),
-        (own, col_a, col_b, row_a, row_b),
+        (own, col_a, col_b, row_a, row_b, deep_in),
         [PLANES, (304, 128)],
         aliases={0: 0},
         flops=10**11,

time: 52.3 us -> 52.2 us (level)
  the two profiles are of different devices: /device:TPU:111 before, /device:TPU:121 now
where the time goes in v5:
time: 52.2 us; the launch traced here: 51.9 us
  starting transfers between devices  22.4 us (43%)
  Pallas kernels  19.5 us (37%)
  waiting for transfers between devices  9.16 us (18%)
  between operations  0.77 us (1%)
    pallas_call x7, Pallas kernels, call(): pl.pallas_call(kernel, out_shape=shapes, in_specs=[SMEM] * len(tables) +...  19.5 us
    ppermute x1, waiting for transfers between devices, local(): message = lax.ppermute(message, 'gx', facing)  9.14 us
    ppermute x1, starting transfers between devices, local(): col_b = lax.ppermute(col_b, 'gy', pairs(ny, True))  5.46 us
    ppermute x1, starting transfers between devices, local(): deep_in = lax.ppermute(deep_out, 'gx', facing)  4.27 us
    ppermute x1, starting transfers between devices, local(): message = lax.ppermute(message, 'gx', facing)  3.14 us
    ppermute x1, starting transfers between devices, local(): row_a = lax.ppermute(row_a, 'gx', pairs(nx, False))  2.4 us
    ppermute x1, starting transfers between devices, local(): sensor_in = lax.ppermute(sensor_out, 'gx', facing)  2.4 us
    ppermute x1, starting transfers between devices, local(): peak_in = lax.ppermute(peak_out, 'gx', facing)  2.31 us
  transfers between devices with their start and end apart: 8, of which 1 were waited for; matrix products, arithmetic and copies ran while one was open for 0% of the time, Pallas kernels for 25%

profile of v5, /device:TPU:121, one launch (start us, length us, event | category | flops | bytes accessed | tf_op | source)
XLA Modules:
  0.0 51.9 jit_solution(13067862089045138543)
XLA Ops:
  0.6 0.1 pad_add_fusion.place
  0.7 2.5 %gather.1 = (f32[19,3,80,128]{3,2,1,0:T(8,128)S(1)}, f32[64,128]{1,0:T(8,128)S(1)}, f32[64,128]{1,0:T(8,128)S(1)}) custom-call(s32[2]{0:T(128)S(1)} %pad_add_fusion.place, f32[32]{0:T(128)} %block_power.1, s32[2,64,256]{2,1,0:T(8,128)} %ids.1, f32[64,256]{1,0:T(8,128)} %bond.1, f32[2,4,64,256]{3,2,1,0:T(8,128)} %sensor.1, f32[2,4,64,256]{3,2,1,0:T(8,128)} %peak.2), custom_call_target="tpu_custom_call" | custom-call | bytes 1024 | tf_op jit(solution)/shard_map/gather/pallas_call | solution.py:671
  3.2 0.5 %collective-permute-start = (f32[64,128]{1,0:T(8,128)S(1)}, f32[64,128]{1,0:T(8,128)S(1)}, u32[]{:S(2)}, u32[]{:S(2)}) collective-permute-start(f32[64,128]{1,0:T(8,128)S(1)} %get-tuple-element.22), channel_id=1, source_target_pairs={{0,1},{1,0},{2,3},{3,2},{4,5},{5,4},{6,7},{7,6},{8,9},{9,8},{10,11... | collective-permute-start | bytes 98312 | tf_op jit(solution)/shard_map/ppermute | solution.py:718
  3.8 5.5 %collective-permute-start.1 = (f32[64,128]{1,0:T(8,128)S(1)}, f32[64,128]{1,0:T(8,128)S(1)}, u32[]{:S(2)}, u32[]{:S(2)}) collective-permute-start(f32[64,128]{1,0:T(8,128)S(1)} %get-tuple-element.23), channel_id=1, source_target_pairs={{1,2},{2,1},{3,4},{4,3},{5,6},{6,5},{7,8},{8,7},{9,10},{10,9},{11,... | collective-permute-start | bytes 98312 | tf_op jit(solution)/shard_map/ppermute | solution.py:719
  9.3 0.7 %deep_out.1 = f32[3,2,64,128]{3,2,1,0:T(8,128)} custom-call(f32[19,3,80,128]{3,2,1,0:T(8,128)S(1)} %get-tuple-element.21.own.start), custom_call_target="tpu_custom_call" | custom-call | flops 99999997952 | bytes 1024 | tf_op jit(solution)/shard_map/deep_out/pallas_call | solution.py:671
  10.0 4.3 %collective-permute-start.4 = (f32[3,2,64,128]{3,2,1,0:T(8,128)}, f32[3,2,64,128]{3,2,1,0:T(8,128)}, u32[]{:S(2)}, u32[]{:S(2)}) collective-permute-start(f32[3,2,64,128]{3,2,1,0:T(8,128)} %deep_out.1), channel_id=1, source_target_pairs={{0,240},{16,224},{32,208},{48,192},{64,176},{80,160},{96,144},{112... | collective-permute-start | bytes 589832 | tf_op jit(solution)/shard_map/ppermute | solution.py:723
  14.2 0.0 collective-permute-done.col_a
  14.2 0.0 collective-permute-done.1.col_b
  14.2 1.1 %rows.1 = (f32[264,128]{1,0:T(8,128)S(1)}, f32[264,128]{1,0:T(8,128)S(1)}) custom-call(s32[2]{0:T(128)S(1)} %pad_add_fusion.place, f32[19,3,80,128]{3,2,1,0:T(8,128)S(1)} %get-tuple-element.21.own.start, f32[64,128]{1,0:T(8,128)S(1)} %collective-permute-done.col_a, f32[64,128]{1,0:T(8,128)S(1)} %collective-permute-done.1.col_b, f32[3,2,64,128]{3,2,1,0:T(8,128)} %deep_out.1), custom_call_target="tpu_custom_call" | custom-call | flops 99999997952 | bytes 1024 | tf_op jit(solution)/shard_map/rows/pallas_call | solution.py:671
  15.4 1.9 %collective-permute-start.3 = (f32[264,128]{1,0:T(8,128)S(1)}, f32[264,128]{1,0:T(8,128)S(1)}, u32[]{:S(2)}, u32[]{:S(2)}) collective-permute-start(f32[264,128]{1,0:T(8,128)S(1)} %get-tuple-element.25), channel_id=1, source_target_pairs={{16,32},{32,16},{48,64},{64,48},{80,96},{96,80},{112,128},{128,112... | collective-permute-start | bytes 405512 | tf_op jit(solution)/shard_map/ppermute | solution.py:732
  17.3 2.4 %collective-permute-start.2 = (f32[264,128]{1,0:T(8,128)S(1)}, f32[264,128]{1,0:T(8,128)S(1)}, u32[]{:S(2)}, u32[]{:S(2)}) collective-permute-start(f32[264,128]{1,0:T(8,128)S(1)} %get-tuple-element.24.row_a), channel_id=1, source_target_pairs={{0,16},{16,0},{32,48},{48,32},{64,80},{80,64},{96,112},{112,96},{1... | collective-permute-start | bytes 405512 | tf_op jit(solution)/shard_map/ppermute | solution.py:731
  19.7 0.1 layers_out.1
  19.8 0.0 copy-start
  19.8 0.0 copy-start.1
  19.8 0.0 copy-start.2
  19.8 0.0 copy-start.3
  19.9 0.0 copy-start.4
  19.9 2.4 %collective-permute-start.5 = (f32[6,2,64,128]{3,2,1,0:T(8,128)S(1)}, f32[6,2,64,128]{3,2,1,0:T(8,128)S(1)}, u32[]{:S(2)}, u32[]{:S(2)}) collective-permute-start(f32[6,2,64,128]{3,2,1,0:T(8,128)S(1)} %get-tuple-element.27), channel_id=1, source_target_pairs={{0,240},{16,224},{32,208},{48,192},{64,176},{80,160},{96,144},{112... | collective-permute-start | bytes 1179656 | tf_op jit(solution)/shard_map/ppermute | solution.py:733
  22.3 0.0 collective-permute-done.3.row_b
  22.3 0.0 collective-permute-done.2.row_a
  22.3 0.0 collective-permute-done.4.deep_in
  22.3 1.7 %build.1 = (f32[19,3,80,128]{3,2,1,0:T(8,128)S(1)}, f32[304,128]{1,0:T(8,128)S(1)}) custom-call(s32[2]{0:T(128)S(1)} %pad_add_fusion.place, f32[19,3,80,128]{3,2,1,0:T(8,128)S(1)} %get-tuple-element.21.own.start, f32[64,128]{1,0:T(8,128)S(1)} %collective-permute-done.col_a, ...), custom_call_target="tpu_custom_call", output_to_operand_aliasing={{0}: (1, {})} | custom-call | flops 99999997952 | bytes 1024 | tf_op jit(solution)/shard_map/build/pallas_call | solution.py:671
  24.0 3.1 %collective-permute-start.6 = (f32[304,128]{1,0:T(8,128)S(1)}, f32[304,128]{1,0:T(8,128)S(1)}, u32[]{:S(2)}, u32[]{:S(2)}) collective-permute-start(f32[304,128]{1,0:T(8,128)S(1)} %get-tuple-element.28), channel_id=1, source_target_pairs={{0,240},{16,224},{32,208},{48,192},{64,176},{80,160},{96,144},{112... | collective-permute-start | bytes 466952 | tf_op jit(solution)/shard_map/ppermute | solution.py:744
  27.1 2.3 %collective-permute-start.7 = (f32[6,2,64,128]{3,2,1,0:T(8,128)S(1)}, f32[6,2,64,128]{3,2,1,0:T(8,128)S(1)}, u32[]{:S(2)}, u32[]{:S(2)}) collective-permute-start(f32[6,2,64,128]{3,2,1,0:T(8,128)S(1)} %get-tuple-element.31), channel_id=1, source_target_pairs={{0,240},{16,224},{32,208},{48,192},{64,176},{80,160},{96,144},{112... | collective-permute-start | bytes 1179656 | tf_op jit(solution)/shard_map/ppermute | solution.py:745
  29.4 9.1 %collective-permute-done.6.message = f32[304,128]{1,0:T(8,128)S(1)} collective-permute-done((f32[304,128]{1,0:T(8,128)S(1)}, f32[304,128]{1,0:T(8,128)S(1)}, u32[]{:S(2)}, u32[]{:S(2)}) %collective-permute-start.6) | collective-permute-done | bytes 155680 | tf_op jit(solution)/shard_map/ppermute | solution.py:744
  38.6 0.0 collective-permute-done.5.sensor_in
  38.6 0.0 copy-done
  38.6 0.0 copy-done.1
  38.6 0.0 copy-done.2
  38.6 0.0 copy-done.3
  38.6 0.0 copy-done.4
  38.6 9.6 %thermal_sensor.1 = (f32[2,4,64,256]{3,2,1,0:T(8,128)}, f32[2,4,64,256]{3,2,1,0:T(8,128)}, f32[2,3,3,80,128]{4,3,2,1,0:T(8,128)S(1)}, f32[2,4,3,80,128]{4,3,2,1,...) custom-call(s32[2]{0:T(128)S(1)} %pad_add_fusion.place, ...), custom_call_target="tpu_custom_call" | custom-call | flops 99999997952 | bytes 1024 | tf_op jit(solution)/shard_map/thermal_sensor/pallas_call | solution.py:671
  48.2 0.0 collective-permute-done.7.peak_in
  48.2 3.7 %peak.3 = (f32[2,4,64,256]{3,2,1,0:T(8,128)}, f32[2,2,4,3,96,128]{5,4,3,2,1,0:T(8,128)S(1)}) custom-call(s32[2]{0:T(128)S(1)} %pad_add_fusion.place, s32[2,4]{1,0:T(2,128)S(1)} %copy-done, f32[4]{0:T(128)S(1)} %copy-done.1, f32[4]{0:T(128)S(1)} %copy-done.2, f32[2]{0:T(128)S(1)} %copy-done.3, ...), custom_call_target="tpu_custom_call", output_to_operand_aliasing={{1}: (11, {})} | custom-call | bytes 1024 | tf_op jit(solution)/shard_map/peak/pallas_call | solution.py:671
Async XLA Ops:
  3.2 11.0 %collective-permute-start = (f32[64,128]{1,0:T(8,128)S(1)}, f32[64,128]{1,0:T(8,128)S(1)}, u32[]{:S(2)}, u32[]{:S(2)}) collective-permute-start(f32[64,128]{1,0:T(8,128)S(1)} %get-tuple-element.22), channel_id=1, source_target_pairs={{0,1},{1,0},{2,3},{3,2},{4,5},{5,4},{6,7},{7,6},{8,9},{9,8},{10,11... | collective-permute-start | bytes 98312 | tf_op jit(solution)/shard_map/ppermute | solution.py:718
  3.8 10.5 %collective-permute-start.1 = (f32[64,128]{1,0:T(8,128)S(1)}, f32[64,128]{1,0:T(8,128)S(1)}, u32[]{:S(2)}, u32[]{:S(2)}) collective-permute-start(f32[64,128]{1,0:T(8,128)S(1)} %get-tuple-element.23), channel_id=1, source_target_pairs={{1,2},{2,1},{3,4},{4,3},{5,6},{6,5},{7,8},{8,7},{9,10},{10,9},{11,... | collective-permute-start | bytes 98312 | tf_op jit(solution)/shard_map/ppermute | solution.py:719
  10.0 12.3 %collective-permute-start.4 = (f32[3,2,64,128]{3,2,1,0:T(8,128)}, f32[3,2,64,128]{3,2,1,0:T(8,128)}, u32[]{:S(2)}, u32[]{:S(2)}) collective-permute-start(f32[3,2,64,128]{3,2,1,0:T(8,128)} %deep_out.1), channel_id=1, source_target_pairs={{0,240},{16,224},{32,208},{48,192},{64,176},{80,160},{96,144},{112... | collective-permute-start | bytes 589832 | tf_op jit(solution)/shard_map/ppermute | solution.py:723
  15.4 6.9 %collective-permute-start.3 = (f32[264,128]{1,0:T(8,128)S(1)}, f32[264,128]{1,0:T(8,128)S(1)}, u32[]{:S(2)}, u32[]{:S(2)}) collective-permute-start(f32[264,128]{1,0:T(8,128)S(1)} %get-tuple-element.25), channel_id=1, source_target_pairs={{16,32},{32,16},{48,64},{64,48},{80,96},{96,80},{112,128},{128,112... | collective-permute-start | bytes 405512 | tf_op jit(solution)/shard_map/ppermute | solution.py:732
  17.3 5.0 %collective-permute-start.2 = (f32[264,128]{1,0:T(8,128)S(1)}, f32[264,128]{1,0:T(8,128)S(1)}, u32[]{:S(2)}, u32[]{:S(2)}) collective-permute-start(f32[264,128]{1,0:T(8,128)S(1)} %get-tuple-element.24.row_a), channel_id=1, source_target_pairs={{0,16},{16,0},{32,48},{48,32},{64,80},{80,64},{96,112},{112,96},{1... | collective-permute-start | bytes 405512 | tf_op jit(solution)/shard_map/ppermute | solution.py:731
  19.8 18.8 %copy-start = (s32[2,4]{1,0:T(2,128)S(1)}, s32[2,4]{1,0:T(2,128)}, u32[]{:S(2)}) copy-start(s32[2,4]{1,0:T(2,128)} %layer_class.3) | copy-start | bytes 100
  19.8 18.7 %copy-start.1 = (f32[4]{0:T(128)S(1)}, f32[4]{0:T(128)}, u32[]{:S(2)}) copy-start(f32[4]{0:T(128)} %lateral.3) | copy-start | bytes 52
  19.8 18.7 %copy-start.2 = (f32[4]{0:T(128)S(1)}, f32[4]{0:T(128)}, u32[]{:S(2)}) copy-start(f32[4]{0:T(128)} %vertical.3) | copy-start | bytes 52
  19.8 18.7 %copy-start.3 = (f32[2]{0:T(128)S(1)}, f32[2]{0:T(128)}, u32[]{:S(2)}) copy-start(f32[2]{0:T(128)} %sink.3) | copy-start | bytes 28
  19.9 18.7 %copy-start.4 = (f32[4]{0:T(128)S(1)}, f32[4]{0:T(128)}, u32[]{:S(2)}) copy-start(f32[4]{0:T(128)} %share.1) | copy-start | bytes 52
  19.9 18.7 %collective-permute-start.5 = (f32[6,2,64,128]{3,2,1,0:T(8,128)S(1)}, f32[6,2,64,128]{3,2,1,0:T(8,128)S(1)}, u32[]{:S(2)}, u32[]{:S(2)}) collective-permute-start(f32[6,2,64,128]{3,2,1,0:T(8,128)S(1)} %get-tuple-element.27), channel_id=1, source_target_pairs={{0,240},{16,224},{32,208},{48,192},{64,176},{80,160},{96,144},{112... | collective-permute-start | bytes 1179656 | tf_op jit(solution)/shard_map/ppermute | solution.py:733
  24.0 14.6 %collective-permute-start.6 = (f32[304,128]{1,0:T(8,128)S(1)}, f32[304,128]{1,0:T(8,128)S(1)}, u32[]{:S(2)}, u32[]{:S(2)}) collective-permute-start(f32[304,128]{1,0:T(8,128)S(1)} %get-tuple-element.28), channel_id=1, source_target_pairs={{0,240},{16,224},{32,208},{48,192},{64,176},{80,160},{96,144},{112... | collective-permute-start | bytes 466952 | tf_op jit(solution)/shard_map/ppermute | solution.py:744
  27.1 21.1 %collective-permute-start.7 = (f32[6,2,64,128]{3,2,1,0:T(8,128)S(1)}, f32[6,2,64,128]{3,2,1,0:T(8,128)S(1)}, u32[]{:S(2)}, u32[]{:S(2)}) collective-permute-start(f32[6,2,64,128]{3,2,1,0:T(8,128)S(1)} %get-tuple-element.31), channel_id=1, source_target_pairs={{0,240},{16,224},{32,208},{48,192},{64,176},{80,160},{96,144},{112... | collective-permute-start | bytes 1179656 | tf_op jit(solution)/shard_map/ppermute | solution.py:745

commit v6 on v5

--- a/solution.py
+++ b/solution.py
@@ -131,11 +131,11 @@
 
 
 def deep_kernel(own, out):
-    mirror_into(out, own, (0, 1, 2))
+    mirror_into(out, own, (0, 1, 2, 4, 8))
 
 
 def layers_kernel(own, row_a, sensor_out, peak_out):
-    mirror_into(sensor_out, own, (4, 5, 6, 8, 9, 10))
+    mirror_into(sensor_out, own, (5, 6, 9, 10))
     mirror_into(peak_out, own, (12, 13, 14, 16, 17, 18))
 
 
@@ -503,7 +503,10 @@
     prepare(hot, lambda d, k, t: (own if d == 0 else deep)[2, t, tile_rows(k), :])
 
     def layers_in(n, t, rows):
-        return sensor_in[n, t, rows, :]
+        die, l = divmod(n, 3)
+        if l == 0:
+            return deep_in[3 + die, t, rows, :]
+        return sensor_in[2 * die + l - 1, t, rows, :]
 
     for d in both:
         place_other(planes, layers_in, message, 0, d)
@@ -718,7 +721,7 @@
     col_a = lax.ppermute(col_a, "gy", pairs(ny, False))
     col_b = lax.ppermute(col_b, "gy", pairs(ny, True))
     (deep_out,) = call(
-        deep_kernel, (), (own,), [(3, 2, 64, 128)], flops=10**11, name="deep_out"
+        deep_kernel, (), (own,), [(5, 2, 64, 128)], flops=10**11, name="deep_out"
     )
     deep_in = lax.ppermute(deep_out, "gx", facing)
     row_a, row_b = call(
@@ -726,7 +729,7 @@
     )
     layers = (6, 2, 64, 128)
     sensor_out, peak_out = call(
-        layers_kernel, (), (own, row_a), [layers, layers], flops=10**11, name="layers_out"
+        layers_kernel, (), (own, row_a), [(4, 2, 64, 128), layers], flops=10**11, name="layers_out"
     )
     row_a = lax.ppermute(row_a, "gx", pairs(nx, False))
     row_b = lax.ppermute(row_b, "gx", pairs(nx, True))

time: 52.2 us -> 51.4 us (0.985)
  the two profiles are of different devices: /device:TPU:121 before, /device:TPU:111 now
where the time goes in v6:
time: 51.4 us; the launch traced here: 51.1 us
  starting transfers between devices  22 us (43%)
  Pallas kernels  19.7 us (38%)
  waiting for transfers between devices  8.64 us (17%)
  between operations  0.77 us (1%)
    pallas_call x7, Pallas kernels, call(): pl.pallas_call(kernel, out_shape=shapes, in_specs=[SMEM] * len(tables) +...  19.7 us
    ppermute x1, starting transfers between devices, local(): col_b = lax.ppermute(col_b, 'gy', pairs(ny, True))  5.76 us
    ppermute x1, waiting for transfers between devices, local(): message = lax.ppermute(message, 'gx', facing)  4.89 us
    ppermute x1, starting transfers between devices, local(): row_b = lax.ppermute(row_b, 'gx', pairs(nx, True))  4.22 us
    ppermute x1, waiting for transfers between devices, local(): row_b = lax.ppermute(row_b, 'gx', pairs(nx, True))  3.74 us
    ppermute x1, starting transfers between devices, local(): peak_in = lax.ppermute(peak_out, 'gx', facing)  3.16 us
    ppermute x1, starting transfers between devices, local(): sensor_in = lax.ppermute(sensor_out, 'gx', facing)  3.14 us
    ppermute x1, starting transfers between devices, local(): deep_in = lax.ppermute(deep_out, 'gx', facing)  3.05 us
  transfers between devices with their start and end apart: 8, of which 2 were waited for; matrix products, arithmetic and copies ran while one was open for 0% of the time, Pallas kernels for 26%

profile of v6, /device:TPU:111, one launch (start us, length us, event | category | flops | bytes accessed | tf_op | source)
XLA Modules:
  0.0 51.1 jit_solution(8242493527393677665)
XLA Ops:
  0.6 0.1 pad_add_fusion.place
  0.7 2.5 %gather.1 = (f32[19,3,80,128]{3,2,1,0:T(8,128)S(1)}, f32[64,128]{1,0:T(8,128)S(1)}, f32[64,128]{1,0:T(8,128)S(1)}) custom-call(s32[2]{0:T(128)S(1)} %pad_add_fusion.place, f32[32]{0:T(128)} %block_power.1, s32[2,64,256]{2,1,0:T(8,128)} %ids.1, f32[64,256]{1,0:T(8,128)} %bond.1, f32[2,4,64,256]{3,2,1,0:T(8,128)} %sensor.1, f32[2,4,64,256]{3,2,1,0:T(8,128)} %peak.2), custom_call_target="tpu_custom_call" | custom-call | bytes 1024 | tf_op jit(solution)/shard_map/gather/pallas_call | solution.py:674
  3.2 0.3 collective-permute-start
  3.5 5.8 %collective-permute-start.1 = (f32[64,128]{1,0:T(8,128)S(1)}, f32[64,128]{1,0:T(8,128)S(1)}, u32[]{:S(2)}, u32[]{:S(2)}) collective-permute-start(f32[64,128]{1,0:T(8,128)S(1)} %get-tuple-element.23), channel_id=1, source_target_pairs={{1,2},{2,1},{3,4},{4,3},{5,6},{6,5},{7,8},{8,7},{9,10},{10,9},{11,... | collective-permute-start | bytes 98312 | tf_op jit(solution)/shard_map/ppermute | solution.py:722
  9.3 0.8 %deep_out.1 = f32[5,2,64,128]{3,2,1,0:T(8,128)} custom-call(f32[19,3,80,128]{3,2,1,0:T(8,128)S(1)} %get-tuple-element.21.own.start), custom_call_target="tpu_custom_call" | custom-call | flops 99999997952 | bytes 1024 | tf_op jit(solution)/shard_map/deep_out/pallas_call | solution.py:674
  10.0 3.1 %collective-permute-start.4 = (f32[5,2,64,128]{3,2,1,0:T(8,128)}, f32[5,2,64,128]{3,2,1,0:T(8,128)}, u32[]{:S(2)}, u32[]{:S(2)}) collective-permute-start(f32[5,2,64,128]{3,2,1,0:T(8,128)} %deep_out.1), channel_id=1, source_target_pairs={{0,240},{16,224},{32,208},{48,192},{64,176},{80,160},{96,144},{112... | collective-permute-start | bytes 983048 | tf_op jit(solution)/shard_map/ppermute | solution.py:726
  13.1 0.0 collective-permute-done.col_a
  13.1 0.0 collective-permute-done.1.col_b
  13.1 1.2 %rows.1 = (f32[264,128]{1,0:T(8,128)S(1)}, f32[264,128]{1,0:T(8,128)S(1)}) custom-call(s32[2]{0:T(128)S(1)} %pad_add_fusion.place, f32[19,3,80,128]{3,2,1,0:T(8,128)S(1)} %get-tuple-element.21.own.start, f32[64,128]{1,0:T(8,128)S(1)} %collective-permute-done.col_a, f32[64,128]{1,0:T(8,128)S(1)} %collective-permute-done.1.col_b, f32[5,2,64,128]{3,2,1,0:T(8,128)} %deep_out.1), custom_call_target="tpu_custom_call" | custom-call | flops 99999997952 | bytes 1024 | tf_op jit(solution)/shard_map/rows/pallas_call | solution.py:674
  14.2 4.2 %collective-permute-start.3 = (f32[264,128]{1,0:T(8,128)S(1)}, f32[264,128]{1,0:T(8,128)S(1)}, u32[]{:S(2)}, u32[]{:S(2)}) collective-permute-start(f32[264,128]{1,0:T(8,128)S(1)} %get-tuple-element.25), channel_id=1, source_target_pairs={{16,32},{32,16},{48,64},{64,48},{80,96},{96,80},{112,128},{128,112... | collective-permute-start | bytes 405512 | tf_op jit(solution)/shard_map/ppermute | solution.py:735
  18.5 0.1 collective-permute-start.2
  18.6 0.1 layers_out.1
  18.7 0.0 copy-start
  18.7 0.0 copy-start.1
  18.7 0.0 copy-start.2
  18.7 0.0 copy-start.3
  18.7 0.0 copy-start.4
  18.7 3.1 %collective-permute-start.5 = (f32[4,2,64,128]{3,2,1,0:T(8,128)S(1)}, f32[4,2,64,128]{3,2,1,0:T(8,128)S(1)}, u32[]{:S(2)}, u32[]{:S(2)}) collective-permute-start(f32[4,2,64,128]{3,2,1,0:T(8,128)S(1)} %get-tuple-element.27), channel_id=1, source_target_pairs={{0,240},{16,224},{32,208},{48,192},{64,176},{80,160},{96,144},{112... | collective-permute-start | bytes 786440 | tf_op jit(solution)/shard_map/ppermute | solution.py:736
  21.9 3.7 %collective-permute-done.3.row_b = f32[264,128]{1,0:T(8,128)S(1)} collective-permute-done((f32[264,128]{1,0:T(8,128)S(1)}, f32[264,128]{1,0:T(8,128)S(1)}, u32[]{:S(2)}, u32[]{:S(2)}) %collective-permute-start.3) | collective-permute-done | bytes 135200 | tf_op jit(solution)/shard_map/ppermute | solution.py:735
  25.6 0.0 collective-permute-done.2.row_a
  25.6 0.0 collective-permute-done.4.deep_in
  25.6 1.7 %build.1 = (f32[19,3,80,128]{3,2,1,0:T(8,128)S(1)}, f32[304,128]{1,0:T(8,128)S(1)}) custom-call(s32[2]{0:T(128)S(1)} %pad_add_fusion.place, f32[19,3,80,128]{3,2,1,0:T(8,128)S(1)} %get-tuple-element.21.own.start, f32[64,128]{1,0:T(8,128)S(1)} %collective-permute-done.col_a, ...), custom_call_target="tpu_custom_call", output_to_operand_aliasing={{0}: (1, {})} | custom-call | flops 99999997952 | bytes 1024 | tf_op jit(solution)/shard_map/build/pallas_call | solution.py:674
  27.4 2.3 %collective-permute-start.6 = (f32[304,128]{1,0:T(8,128)S(1)}, f32[304,128]{1,0:T(8,128)S(1)}, u32[]{:S(2)}, u32[]{:S(2)}) collective-permute-start(f32[304,128]{1,0:T(8,128)S(1)} %get-tuple-element.28), channel_id=1, source_target_pairs={{0,240},{16,224},{32,208},{48,192},{64,176},{80,160},{96,144},{112... | collective-permute-start | bytes 466952 | tf_op jit(solution)/shard_map/ppermute | solution.py:747
  29.7 3.2 %collective-permute-start.7 = (f32[6,2,64,128]{3,2,1,0:T(8,128)S(1)}, f32[6,2,64,128]{3,2,1,0:T(8,128)S(1)}, u32[]{:S(2)}, u32[]{:S(2)}) collective-permute-start(f32[6,2,64,128]{3,2,1,0:T(8,128)S(1)} %get-tuple-element.31), channel_id=1, source_target_pairs={{0,240},{16,224},{32,208},{48,192},{64,176},{80,160},{96,144},{112... | collective-permute-start | bytes 1179656 | tf_op jit(solution)/shard_map/ppermute | solution.py:748
  32.8 0.0 collective-permute-done.5.sensor_in
  32.8 4.9 %collective-permute-done.6.message = f32[304,128]{1,0:T(8,128)S(1)} collective-permute-done((f32[304,128]{1,0:T(8,128)S(1)}, f32[304,128]{1,0:T(8,128)S(1)}, u32[]{:S(2)}, u32[]{:S(2)}) %collective-permute-start.6) | collective-permute-done | bytes 155680 | tf_op jit(solution)/shard_map/ppermute | solution.py:747
  37.7 0.0 copy-done
  37.7 0.0 copy-done.1
  37.7 0.0 copy-done.2
  37.7 0.0 copy-done.3
  37.7 0.0 copy-done.4
  37.7 9.6 %thermal_sensor.1 = (f32[2,4,64,256]{3,2,1,0:T(8,128)}, f32[2,4,64,256]{3,2,1,0:T(8,128)}, f32[2,3,3,80,128]{4,3,2,1,0:T(8,128)S(1)}, f32[2,4,3,80,128]{4,3,2,1,...) custom-call(s32[2]{0:T(128)S(1)} %pad_add_fusion.place, ...), custom_call_target="tpu_custom_call" | custom-call | flops 99999997952 | bytes 1024 | tf_op jit(solution)/shard_map/thermal_sensor/pallas_call | solution.py:674
  47.4 0.0 collective-permute-done.7.peak_in
  47.4 3.7 %peak.3 = (f32[2,4,64,256]{3,2,1,0:T(8,128)}, f32[2,2,4,3,96,128]{5,4,3,2,1,0:T(8,128)S(1)}) custom-call(s32[2]{0:T(128)S(1)} %pad_add_fusion.place, s32[2,4]{1,0:T(2,128)S(1)} %copy-done, f32[4]{0:T(128)S(1)} %copy-done.1, f32[4]{0:T(128)S(1)} %copy-done.2, f32[2]{0:T(128)S(1)} %copy-done.3, ...), custom_call_target="tpu_custom_call", output_to_operand_aliasing={{1}: (11, {})} | custom-call | bytes 1024 | tf_op jit(solution)/shard_map/peak/pallas_call | solution.py:674
Async XLA Ops:
  3.2 9.8 %collective-permute-start = (f32[64,128]{1,0:T(8,128)S(1)}, f32[64,128]{1,0:T(8,128)S(1)}, u32[]{:S(2)}, u32[]{:S(2)}) collective-permute-start(f32[64,128]{1,0:T(8,128)S(1)} %get-tuple-element.22), channel_id=1, source_target_pairs={{0,1},{1,0},{2,3},{3,2},{4,5},{5,4},{6,7},{7,6},{8,9},{9,8},{10,11... | collective-permute-start | bytes 98312 | tf_op jit(solution)/shard_map/ppermute | solution.py:721
  3.5 9.6 %collective-permute-start.1 = (f32[64,128]{1,0:T(8,128)S(1)}, f32[64,128]{1,0:T(8,128)S(1)}, u32[]{:S(2)}, u32[]{:S(2)}) collective-permute-start(f32[64,128]{1,0:T(8,128)S(1)} %get-tuple-element.23), channel_id=1, source_target_pairs={{1,2},{2,1},{3,4},{4,3},{5,6},{6,5},{7,8},{8,7},{9,10},{10,9},{11,... | collective-permute-start | bytes 98312 | tf_op jit(solution)/shard_map/ppermute | solution.py:722
  10.0 15.6 %collective-permute-start.4 = (f32[5,2,64,128]{3,2,1,0:T(8,128)}, f32[5,2,64,128]{3,2,1,0:T(8,128)}, u32[]{:S(2)}, u32[]{:S(2)}) collective-permute-start(f32[5,2,64,128]{3,2,1,0:T(8,128)} %deep_out.1), channel_id=1, source_target_pairs={{0,240},{16,224},{32,208},{48,192},{64,176},{80,160},{96,144},{112... | collective-permute-start | bytes 983048 | tf_op jit(solution)/shard_map/ppermute | solution.py:726
  14.2 11.4 %collective-permute-start.3 = (f32[264,128]{1,0:T(8,128)S(1)}, f32[264,128]{1,0:T(8,128)S(1)}, u32[]{:S(2)}, u32[]{:S(2)}) collective-permute-start(f32[264,128]{1,0:T(8,128)S(1)} %get-tuple-element.25), channel_id=1, source_target_pairs={{16,32},{32,16},{48,64},{64,48},{80,96},{96,80},{112,128},{128,112... | collective-permute-start | bytes 405512 | tf_op jit(solution)/shard_map/ppermute | solution.py:735
  18.5 7.1 %collective-permute-start.2 = (f32[264,128]{1,0:T(8,128)S(1)}, f32[264,128]{1,0:T(8,128)S(1)}, u32[]{:S(2)}, u32[]{:S(2)}) collective-permute-start(f32[264,128]{1,0:T(8,128)S(1)} %get-tuple-element.24.row_a), channel_id=1, source_target_pairs={{0,16},{16,0},{32,48},{48,32},{64,80},{80,64},{96,112},{112,96},{1... | collective-permute-start | bytes 405512 | tf_op jit(solution)/shard_map/ppermute | solution.py:734
  18.7 19.0 %copy-start = (s32[2,4]{1,0:T(2,128)S(1)}, s32[2,4]{1,0:T(2,128)}, u32[]{:S(2)}) copy-start(s32[2,4]{1,0:T(2,128)} %layer_class.3) | copy-start | bytes 100
  18.7 19.0 %copy-start.1 = (f32[4]{0:T(128)S(1)}, f32[4]{0:T(128)}, u32[]{:S(2)}) copy-start(f32[4]{0:T(128)} %lateral.3) | copy-start | bytes 52
  18.7 19.0 %copy-start.2 = (f32[4]{0:T(128)S(1)}, f32[4]{0:T(128)}, u32[]{:S(2)}) copy-start(f32[4]{0:T(128)} %vertical.3) | copy-start | bytes 52
  18.7 19.0 %copy-start.3 = (f32[2]{0:T(128)S(1)}, f32[2]{0:T(128)}, u32[]{:S(2)}) copy-start(f32[2]{0:T(128)} %sink.3) | copy-start | bytes 28
  18.7 19.0 %copy-start.4 = (f32[4]{0:T(128)S(1)}, f32[4]{0:T(128)}, u32[]{:S(2)}) copy-start(f32[4]{0:T(128)} %share.1) | copy-start | bytes 52
  18.7 14.1 %collective-permute-start.5 = (f32[4,2,64,128]{3,2,1,0:T(8,128)S(1)}, f32[4,2,64,128]{3,2,1,0:T(8,128)S(1)}, u32[]{:S(2)}, u32[]{:S(2)}) collective-permute-start(f32[4,2,64,128]{3,2,1,0:T(8,128)S(1)} %get-tuple-element.27), channel_id=1, source_target_pairs={{0,240},{16,224},{32,208},{48,192},{64,176},{80,160},{96,144},{112... | collective-permute-start | bytes 786440 | tf_op jit(solution)/shard_map/ppermute | solution.py:736
  27.4 10.3 %collective-permute-start.6 = (f32[304,128]{1,0:T(8,128)S(1)}, f32[304,128]{1,0:T(8,128)S(1)}, u32[]{:S(2)}, u32[]{:S(2)}) collective-permute-start(f32[304,128]{1,0:T(8,128)S(1)} %get-tuple-element.28), channel_id=1, source_target_pairs={{0,240},{16,224},{32,208},{48,192},{64,176},{80,160},{96,144},{112... | collective-permute-start | bytes 466952 | tf_op jit(solution)/shard_map/ppermute | solution.py:747
  29.7 17.7 %collective-permute-start.7 = (f32[6,2,64,128]{3,2,1,0:T(8,128)S(1)}, f32[6,2,64,128]{3,2,1,0:T(8,128)S(1)}, u32[]{:S(2)}, u32[]{:S(2)}) collective-permute-start(f32[6,2,64,128]{3,2,1,0:T(8,128)S(1)} %get-tuple-element.31), channel_id=1, source_target_pairs={{0,240},{16,224},{32,208},{48,192},{64,176},{80,160},{96,144},{112... | collective-permute-start | bytes 1179656 | tf_op jit(solution)/shard_map/ppermute | solution.py:748

commit v7 on v6

--- a/solution.py
+++ b/solution.py
@@ -212,18 +212,17 @@
             message[at : at + 8, :] = mirrored(own[n, t, 72:80, :])
             message[at + 8 : at + 16, :] = mirrored(own[n, t, 0:8, :])
     for field in range(2):
-        for d in range(2):
-            n = 3 + 8 * field + 4 * d
-            for t in range(2):
-                above = jnp.where(
-                    row >= 4, own[n + 3, t, 0:8, :], rolled(own[n + 2, t, 0:8, :], 4, 0)
-                )
-                below = jnp.where(
-                    row < 4, own[n + 3, t, 72:80, :], rolled(own[n + 2, t, 72:80, :], 4, 0)
-                )
-                at = 176 + 16 * (4 * field + 2 * d + t)
-                message[at : at + 8, :] = mirrored(below)
-                message[at + 8 : at + 16, :] = mirrored(above)
+        n = 3 + 8 * field
+        for t in range(2):
+            above = [own[m, t, 0:8, :] for m in (n + 3, n + 2, n + 7, n + 6)]
+            below = [own[m, t, 72:80, :] for m in (n + 3, n + 2, n + 7, n + 6)]
+            up, down = above[0], below[0]
+            for slot in (1, 2, 3):
+                up = jnp.where(row >= 8 - 2 * slot, up, rolled(above[slot], -2 * slot, 0))
+                down = jnp.where(row < 2 * slot, down, rolled(below[slot], 2 * slot, 0))
+            at = 176 + 16 * (2 * field + t)
+            message[at : at + 8, :] = mirrored(down)
+            message[at + 8 : at + 16, :] = mirrored(up)
 
 
 def partner_ring(message, slot, rows):
@@ -435,13 +434,12 @@
     for t in range(2):
         planes[d, 0, t, 0:8, :] = zero
         planes[d, 0, t, 72:80, :] = zero
-        at = 176 + 64 * field + 32 * other + 16 * t
+        at = 176 + 16 * (2 * field + t)
         above = message[at : at + 8, :]
         below = message[at + 8 : at + 16, :]
-        planes[d, 2, t, 0:8, :] = above
-        planes[d, 2, t, 72:80, :] = below
-        planes[d, 1, t, 0:8, :] = rolled(above, 4, 0)
-        planes[d, 1, t, 72:80, :] = rolled(below, -4, 0)
+        for l, slot in ((2, 2 * other), (1, 2 * other + 1)):
+            planes[d, l, t, 0:8, :] = rolled(above, 2 * slot, 0)
+            planes[d, l, t, 72:80, :] = rolled(below, -2 * slot, 0)
 
 
 def place_deep(planes, deep_in, message):
@@ -738,7 +736,7 @@
         build_kernel,
         (place,),
         (own, col_a, col_b, row_a, row_b, deep_in),
-        [PLANES, (304, 128)],
+        [PLANES, (240, 128)],
         aliases={0: 0},
         flops=10**11,
         name="build",

time: 51.4 us -> 50.7 us (0.986)
  waiting for transfers between devices: 8.64 us -> 7.94 us
    ppermute x1, waiting for transfers between devices: 4.89 us -> 4.19 us  [local(): message = lax.ppermute(message, 'gx', facing)]
  transfers between devices with their start and end apart: 8 -> 8, of which waited for: 2 -> 2; matrix products, arithmetic and copies ran while one was open for 0% -> 0% of each run, Pallas kernels for 26% -> 27%
where the time goes in v7:
time: 50.7 us; the launch traced here: 50.4 us
  starting transfers between devices  22 us (43%)
  Pallas kernels  19.6 us (39%)
  waiting for transfers between devices  7.94 us (16%)
  between operations  0.77 us (2%)
    pallas_call x7, Pallas kernels, call(): pl.pallas_call(kernel, out_shape=shapes, in_specs=[SMEM] * len(tables) +...  19.6 us
    ppermute x1, starting transfers between devices, local(): col_b = lax.ppermute(col_b, 'gy', pairs(ny, True))  5.76 us
    ppermute x1, starting transfers between devices, local(): row_b = lax.ppermute(row_b, 'gx', pairs(nx, True))  4.22 us
    ppermute x1, waiting for transfers between devices, local(): message = lax.ppermute(message, 'gx', facing)  4.19 us
    ppermute x1, waiting for transfers between devices, local(): row_b = lax.ppermute(row_b, 'gx', pairs(nx, True))  3.74 us
    ppermute x1, starting transfers between devices, local(): peak_in = lax.ppermute(peak_out, 'gx', facing)  3.16 us
    ppermute x1, starting transfers between devices, local(): sensor_in = lax.ppermute(sensor_out, 'gx', facing)  3.14 us
    ppermute x1, starting transfers between devices, local(): deep_in = lax.ppermute(deep_out, 'gx', facing)  3.05 us
  transfers between devices with their start and end apart: 8, of which 2 were waited for; matrix products, arithmetic and copies ran while one was open for 0% of the time, Pallas kernels for 27%

profile of v7, /device:TPU:111, one launch (start us, length us, event | category | flops | bytes accessed | tf_op | source)
XLA Modules:
  0.0 50.4 jit_solution(13865549247445415003)
XLA Ops:
  0.6 0.1 pad_add_fusion.place
  0.7 2.5 %gather.1 = (f32[19,3,80,128]{3,2,1,0:T(8,128)S(1)}, f32[64,128]{1,0:T(8,128)S(1)}, f32[64,128]{1,0:T(8,128)S(1)}) custom-call(s32[2]{0:T(128)S(1)} %pad_add_fusion.place, f32[32]{0:T(128)} %block_power.1, s32[2,64,256]{2,1,0:T(8,128)} %ids.1, f32[64,256]{1,0:T(8,128)} %bond.1, f32[2,4,64,256]{3,2,1,0:T(8,128)} %sensor.1, f32[2,4,64,256]{3,2,1,0:T(8,128)} %peak.2), custom_call_target="tpu_custom_call" | custom-call | bytes 1024 | tf_op jit(solution)/shard_map/gather/pallas_call | solution.py:672
  3.2 0.3 collective-permute-start
  3.5 5.8 %collective-permute-start.1 = (f32[64,128]{1,0:T(8,128)S(1)}, f32[64,128]{1,0:T(8,128)S(1)}, u32[]{:S(2)}, u32[]{:S(2)}) collective-permute-start(f32[64,128]{1,0:T(8,128)S(1)} %get-tuple-element.23), channel_id=1, source_target_pairs={{1,2},{2,1},{3,4},{4,3},{5,6},{6,5},{7,8},{8,7},{9,10},{10,9},{11,... | collective-permute-start | bytes 98312 | tf_op jit(solution)/shard_map/ppermute | solution.py:720
  9.3 0.8 %deep_out.1 = f32[5,2,64,128]{3,2,1,0:T(8,128)} custom-call(f32[19,3,80,128]{3,2,1,0:T(8,128)S(1)} %get-tuple-element.21.own.start), custom_call_target="tpu_custom_call" | custom-call | flops 99999997952 | bytes 1024 | tf_op jit(solution)/shard_map/deep_out/pallas_call | solution.py:672
  10.0 3.1 %collective-permute-start.4 = (f32[5,2,64,128]{3,2,1,0:T(8,128)}, f32[5,2,64,128]{3,2,1,0:T(8,128)}, u32[]{:S(2)}, u32[]{:S(2)}) collective-permute-start(f32[5,2,64,128]{3,2,1,0:T(8,128)} %deep_out.1), channel_id=1, source_target_pairs={{0,240},{16,224},{32,208},{48,192},{64,176},{80,160},{96,144},{112... | collective-permute-start | bytes 983048 | tf_op jit(solution)/shard_map/ppermute | solution.py:724
  13.1 0.0 collective-permute-done.col_a
  13.1 0.0 collective-permute-done.1.col_b
  13.1 1.2 %rows.1 = (f32[264,128]{1,0:T(8,128)S(1)}, f32[264,128]{1,0:T(8,128)S(1)}) custom-call(s32[2]{0:T(128)S(1)} %pad_add_fusion.place, f32[19,3,80,128]{3,2,1,0:T(8,128)S(1)} %get-tuple-element.21.own.start, f32[64,128]{1,0:T(8,128)S(1)} %collective-permute-done.col_a, f32[64,128]{1,0:T(8,128)S(1)} %collective-permute-done.1.col_b, f32[5,2,64,128]{3,2,1,0:T(8,128)} %deep_out.1), custom_call_target="tpu_custom_call" | custom-call | flops 99999997952 | bytes 1024 | tf_op jit(solution)/shard_map/rows/pallas_call | solution.py:672
  14.2 4.2 %collective-permute-start.3 = (f32[264,128]{1,0:T(8,128)S(1)}, f32[264,128]{1,0:T(8,128)S(1)}, u32[]{:S(2)}, u32[]{:S(2)}) collective-permute-start(f32[264,128]{1,0:T(8,128)S(1)} %get-tuple-element.25), channel_id=1, source_target_pairs={{16,32},{32,16},{48,64},{64,48},{80,96},{96,80},{112,128},{128,112... | collective-permute-start | bytes 405512 | tf_op jit(solution)/shard_map/ppermute | solution.py:733
  18.5 0.1 collective-permute-start.2
  18.6 0.1 layers_out.1
  18.7 0.0 copy-start
  18.7 0.0 copy-start.1
  18.7 0.0 copy-start.2
  18.7 0.0 copy-start.3
  18.7 0.0 copy-start.4
  18.7 3.1 %collective-permute-start.5 = (f32[4,2,64,128]{3,2,1,0:T(8,128)S(1)}, f32[4,2,64,128]{3,2,1,0:T(8,128)S(1)}, u32[]{:S(2)}, u32[]{:S(2)}) collective-permute-start(f32[4,2,64,128]{3,2,1,0:T(8,128)S(1)} %get-tuple-element.27), channel_id=1, source_target_pairs={{0,240},{16,224},{32,208},{48,192},{64,176},{80,160},{96,144},{112... | collective-permute-start | bytes 786440 | tf_op jit(solution)/shard_map/ppermute | solution.py:734
  21.9 3.7 %collective-permute-done.3.row_b = f32[264,128]{1,0:T(8,128)S(1)} collective-permute-done((f32[264,128]{1,0:T(8,128)S(1)}, f32[264,128]{1,0:T(8,128)S(1)}, u32[]{:S(2)}, u32[]{:S(2)}) %collective-permute-start.3) | collective-permute-done | bytes 135200 | tf_op jit(solution)/shard_map/ppermute | solution.py:733
  25.6 0.0 collective-permute-done.2.row_a
  25.6 0.0 collective-permute-done.4.deep_in
  25.6 1.7 %build.1 = (f32[19,3,80,128]{3,2,1,0:T(8,128)S(1)}, f32[240,128]{1,0:T(8,128)S(1)}) custom-call(s32[2]{0:T(128)S(1)} %pad_add_fusion.place, f32[19,3,80,128]{3,2,1,0:T(8,128)S(1)} %get-tuple-element.21.own.start, f32[64,128]{1,0:T(8,128)S(1)} %collective-permute-done.col_a, ...), custom_call_target="tpu_custom_call", output_to_operand_aliasing={{0}: (1, {})} | custom-call | flops 99999997952 | bytes 1024 | tf_op jit(solution)/shard_map/build/pallas_call | solution.py:672
  27.4 2.3 %collective-permute-start.6 = (f32[240,128]{1,0:T(8,128)S(1)}, f32[240,128]{1,0:T(8,128)S(1)}, u32[]{:S(2)}, u32[]{:S(2)}) collective-permute-start(f32[240,128]{1,0:T(8,128)S(1)} %get-tuple-element.28), channel_id=1, source_target_pairs={{0,240},{16,224},{32,208},{48,192},{64,176},{80,160},{96,144},{112... | collective-permute-start | bytes 368648 | tf_op jit(solution)/shard_map/ppermute | solution.py:745
  29.7 3.2 %collective-permute-start.7 = (f32[6,2,64,128]{3,2,1,0:T(8,128)S(1)}, f32[6,2,64,128]{3,2,1,0:T(8,128)S(1)}, u32[]{:S(2)}, u32[]{:S(2)}) collective-permute-start(f32[6,2,64,128]{3,2,1,0:T(8,128)S(1)} %get-tuple-element.31), channel_id=1, source_target_pairs={{0,240},{16,224},{32,208},{48,192},{64,176},{80,160},{96,144},{112... | collective-permute-start | bytes 1179656 | tf_op jit(solution)/shard_map/ppermute | solution.py:746
  32.8 0.0 collective-permute-done.5.sensor_in
  32.8 4.2 %collective-permute-done.6.message = f32[240,128]{1,0:T(8,128)S(1)} collective-permute-done((f32[240,128]{1,0:T(8,128)S(1)}, f32[240,128]{1,0:T(8,128)S(1)}, u32[]{:S(2)}, u32[]{:S(2)}) %collective-permute-start.6) | collective-permute-done | bytes 122912 | tf_op jit(solution)/shard_map/ppermute | solution.py:745
  37.0 0.0 copy-done
  37.0 0.0 copy-done.1
  37.0 0.0 copy-done.2
  37.0 0.0 copy-done.3
  37.0 0.0 copy-done.4
  37.0 9.6 %thermal_sensor.1 = (f32[2,4,64,256]{3,2,1,0:T(8,128)}, f32[2,4,64,256]{3,2,1,0:T(8,128)}, f32[2,3,3,80,128]{4,3,2,1,0:T(8,128)S(1)}, f32[2,4,3,80,128]{4,3,2,1,...) custom-call(s32[2]{0:T(128)S(1)} %pad_add_fusion.place, ...), custom_call_target="tpu_custom_call" | custom-call | flops 99999997952 | bytes 1024 | tf_op jit(solution)/shard_map/thermal_sensor/pallas_call | solution.py:672
  46.7 0.0 collective-permute-done.7.peak_in
  46.7 3.7 %peak.3 = (f32[2,4,64,256]{3,2,1,0:T(8,128)}, f32[2,2,4,3,96,128]{5,4,3,2,1,0:T(8,128)S(1)}) custom-call(s32[2]{0:T(128)S(1)} %pad_add_fusion.place, s32[2,4]{1,0:T(2,128)S(1)} %copy-done, f32[4]{0:T(128)S(1)} %copy-done.1, f32[4]{0:T(128)S(1)} %copy-done.2, f32[2]{0:T(128)S(1)} %copy-done.3, ...), custom_call_target="tpu_custom_call", output_to_operand_aliasing={{1}: (11, {})} | custom-call | bytes 1024 | tf_op jit(solution)/shard_map/peak/pallas_call | solution.py:672
Async XLA Ops:
  3.2 9.8 %collective-permute-start = (f32[64,128]{1,0:T(8,128)S(1)}, f32[64,128]{1,0:T(8,128)S(1)}, u32[]{:S(2)}, u32[]{:S(2)}) collective-permute-start(f32[64,128]{1,0:T(8,128)S(1)} %get-tuple-element.22), channel_id=1, source_target_pairs={{0,1},{1,0},{2,3},{3,2},{4,5},{5,4},{6,7},{7,6},{8,9},{9,8},{10,11... | collective-permute-start | bytes 98312 | tf_op jit(solution)/shard_map/ppermute | solution.py:719
  3.5 9.6 %collective-permute-start.1 = (f32[64,128]{1,0:T(8,128)S(1)}, f32[64,128]{1,0:T(8,128)S(1)}, u32[]{:S(2)}, u32[]{:S(2)}) collective-permute-start(f32[64,128]{1,0:T(8,128)S(1)} %get-tuple-element.23), channel_id=1, source_target_pairs={{1,2},{2,1},{3,4},{4,3},{5,6},{6,5},{7,8},{8,7},{9,10},{10,9},{11,... | collective-permute-start | bytes 98312 | tf_op jit(solution)/shard_map/ppermute | solution.py:720
  10.0 15.6 %collective-permute-start.4 = (f32[5,2,64,128]{3,2,1,0:T(8,128)}, f32[5,2,64,128]{3,2,1,0:T(8,128)}, u32[]{:S(2)}, u32[]{:S(2)}) collective-permute-start(f32[5,2,64,128]{3,2,1,0:T(8,128)} %deep_out.1), channel_id=1, source_target_pairs={{0,240},{16,224},{32,208},{48,192},{64,176},{80,160},{96,144},{112... | collective-permute-start | bytes 983048 | tf_op jit(solution)/shard_map/ppermute | solution.py:724
  14.2 11.4 %collective-permute-start.3 = (f32[264,128]{1,0:T(8,128)S(1)}, f32[264,128]{1,0:T(8,128)S(1)}, u32[]{:S(2)}, u32[]{:S(2)}) collective-permute-start(f32[264,128]{1,0:T(8,128)S(1)} %get-tuple-element.25), channel_id=1, source_target_pairs={{16,32},{32,16},{48,64},{64,48},{80,96},{96,80},{112,128},{128,112... | collective-permute-start | bytes 405512 | tf_op jit(solution)/shard_map/ppermute | solution.py:733
  18.5 7.1 %collective-permute-start.2 = (f32[264,128]{1,0:T(8,128)S(1)}, f32[264,128]{1,0:T(8,128)S(1)}, u32[]{:S(2)}, u32[]{:S(2)}) collective-permute-start(f32[264,128]{1,0:T(8,128)S(1)} %get-tuple-element.24.row_a), channel_id=1, source_target_pairs={{0,16},{16,0},{32,48},{48,32},{64,80},{80,64},{96,112},{112,96},{1... | collective-permute-start | bytes 405512 | tf_op jit(solution)/shard_map/ppermute | solution.py:732
  18.7 18.3 %copy-start = (s32[2,4]{1,0:T(2,128)S(1)}, s32[2,4]{1,0:T(2,128)}, u32[]{:S(2)}) copy-start(s32[2,4]{1,0:T(2,128)} %layer_class.3) | copy-start | bytes 100
  18.7 18.3 %copy-start.1 = (f32[4]{0:T(128)S(1)}, f32[4]{0:T(128)}, u32[]{:S(2)}) copy-start(f32[4]{0:T(128)} %lateral.3) | copy-start | bytes 52
  18.7 18.3 %copy-start.2 = (f32[4]{0:T(128)S(1)}, f32[4]{0:T(128)}, u32[]{:S(2)}) copy-start(f32[4]{0:T(128)} %vertical.3) | copy-start | bytes 52
  18.7 18.3 %copy-start.3 = (f32[2]{0:T(128)S(1)}, f32[2]{0:T(128)}, u32[]{:S(2)}) copy-start(f32[2]{0:T(128)} %sink.3) | copy-start | bytes 28
  18.7 18.3 %copy-start.4 = (f32[4]{0:T(128)S(1)}, f32[4]{0:T(128)}, u32[]{:S(2)}) copy-start(f32[4]{0:T(128)} %share.1) | copy-start | bytes 52
  18.7 14.1 %collective-permute-start.5 = (f32[4,2,64,128]{3,2,1,0:T(8,128)S(1)}, f32[4,2,64,128]{3,2,1,0:T(8,128)S(1)}, u32[]{:S(2)}, u32[]{:S(2)}) collective-permute-start(f32[4,2,64,128]{3,2,1,0:T(8,128)S(1)} %get-tuple-element.27), channel_id=1, source_target_pairs={{0,240},{16,224},{32,208},{48,192},{64,176},{80,160},{96,144},{112... | collective-permute-start | bytes 786440 | tf_op jit(solution)/shard_map/ppermute | solution.py:734
  27.4 9.6 %collective-permute-start.6 = (f32[240,128]{1,0:T(8,128)S(1)}, f32[240,128]{1,0:T(8,128)S(1)}, u32[]{:S(2)}, u32[]{:S(2)}) collective-permute-start(f32[240,128]{1,0:T(8,128)S(1)} %get-tuple-element.28), channel_id=1, source_target_pairs={{0,240},{16,224},{32,208},{48,192},{64,176},{80,160},{96,144},{112... | collective-permute-start | bytes 368648 | tf_op jit(solution)/shard_map/ppermute | solution.py:745
  29.7 17.0 %collective-permute-start.7 = (f32[6,2,64,128]{3,2,1,0:T(8,128)S(1)}, f32[6,2,64,128]{3,2,1,0:T(8,128)S(1)}, u32[]{:S(2)}, u32[]{:S(2)}) collective-permute-start(f32[6,2,64,128]{3,2,1,0:T(8,128)S(1)} %get-tuple-element.31), channel_id=1, source_target_pairs={{0,240},{16,224},{32,208},{48,192},{64,176},{80,160},{96,144},{112... | collective-permute-start | bytes 1179656 | tf_op jit(solution)/shard_map/ppermute | solution.py:746

commit v8 on v7

--- a/solution.py
+++ b/solution.py
@@ -131,11 +131,11 @@
 
 
 def deep_kernel(own, out):
-    mirror_into(out, own, (0, 1, 2, 4, 8))
+    mirror_into(out, own, (0, 1, 2, 4))
 
 
 def layers_kernel(own, row_a, sensor_out, peak_out):
-    mirror_into(sensor_out, own, (5, 6, 9, 10))
+    mirror_into(sensor_out, own, (5, 6, 8, 9, 10))
     mirror_into(peak_out, own, (12, 13, 14, 16, 17, 18))
 
 
@@ -501,10 +501,9 @@
     prepare(hot, lambda d, k, t: (own if d == 0 else deep)[2, t, tile_rows(k), :])
 
     def layers_in(n, t, rows):
-        die, l = divmod(n, 3)
-        if l == 0:
-            return deep_in[3 + die, t, rows, :]
-        return sensor_in[2 * die + l - 1, t, rows, :]
+        if n == 0:
+            return deep_in[3, t, rows, :]
+        return sensor_in[n - 1, t, rows, :]
 
     for d in both:
         place_other(planes, layers_in, message, 0, d)
@@ -719,7 +718,7 @@
     col_a = lax.ppermute(col_a, "gy", pairs(ny, False))
     col_b = lax.ppermute(col_b, "gy", pairs(ny, True))
     (deep_out,) = call(
-        deep_kernel, (), (own,), [(5, 2, 64, 128)], flops=10**11, name="deep_out"
+        deep_kernel, (), (own,), [(4, 2, 64, 128)], flops=10**11, name="deep_out"
     )
     deep_in = lax.ppermute(deep_out, "gx", facing)
     row_a, row_b = call(
@@ -727,7 +726,7 @@
     )
     layers = (6, 2, 64, 128)
     sensor_out, peak_out = call(
-        layers_kernel, (), (own, row_a), [(4, 2, 64, 128), layers], flops=10**11, name="layers_out"
+        layers_kernel, (), (own, row_a), [(5, 2, 64, 128), layers], flops=10**11, name="layers_out"
     )
     row_a = lax.ppermute(row_a, "gx", pairs(nx, False))
     row_b = lax.ppermute(row_b, "gx", pairs(nx, True))

time: 50.7 us -> 49.7 us (0.980)
  waiting for transfers between devices: 7.94 us -> 6.55 us
    ppermute x1, waiting for transfers between devices: 3.74 us -> 2.31 us  [local(): row_b = lax.ppermute(row_b, 'gx', pairs(nx, True))]
    ppermute x1, waiting for transfers between devices: 0.01 us -> 1.38 us  [local(): sensor_in = lax.ppermute(sensor_out, 'gx', facing)]
    ppermute x1, waiting for transfers between devices: 4.19 us -> 2.85 us  [local(): message = lax.ppermute(message, 'gx', facing)]
  transfers between devices with their start and end apart: 8 -> 8, of which waited for: 2 -> 3; matrix products, arithmetic and copies ran while one was open for 0% -> 0% of each run, Pallas kernels for 27% -> 27%
where the time goes in v8:
time: 49.7 us; the launch traced here: 49 us
  starting transfers between devices  22 us (44%)
  Pallas kernels  19.6 us (39%)
  waiting for transfers between devices  6.55 us (13%)
  between operations  0.77 us (2%)
    pallas_call x7, Pallas kernels, call(): pl.pallas_call(kernel, out_shape=shapes, in_specs=[SMEM] * len(tables) +...  19.6 us
    ppermute x1, starting transfers between devices, local(): col_b = lax.ppermute(col_b, 'gy', pairs(ny, True))  5.76 us
    ppermute x1, starting transfers between devices, local(): row_b = lax.ppermute(row_b, 'gx', pairs(nx, True))  4.22 us
    ppermute x1, starting transfers between devices, local(): sensor_in = lax.ppermute(sensor_out, 'gx', facing)  3.14 us
    ppermute x1, starting transfers between devices, local(): deep_in = lax.ppermute(deep_out, 'gx', facing)  3.05 us
    ppermute x1, starting transfers between devices, local(): peak_in = lax.ppermute(peak_out, 'gx', facing)  3.05 us
    ppermute x1, waiting for transfers between devices, local(): message = lax.ppermute(message, 'gx', facing)  2.85 us
    ppermute x1, starting transfers between devices, local(): message = lax.ppermute(message, 'gx', facing)  2.4 us
  transfers between devices with their start and end apart: 8, of which 3 were waited for; matrix products, arithmetic and copies ran while one was open for 0% of the time, Pallas kernels for 27%

profile of v8, /device:TPU:111, one launch (start us, length us, event | category | flops | bytes accessed | tf_op | source)
XLA Modules:
  0.0 49.0 jit_solution(12420694657385925046)
XLA Ops:
  0.6 0.1 pad_add_fusion.place
  0.7 2.5 %gather.1 = (f32[19,3,80,128]{3,2,1,0:T(8,128)S(1)}, f32[64,128]{1,0:T(8,128)S(1)}, f32[64,128]{1,0:T(8,128)S(1)}) custom-call(s32[2]{0:T(128)S(1)} %pad_add_fusion.place, f32[32]{0:T(128)} %block_power.1, s32[2,64,256]{2,1,0:T(8,128)} %ids.1, f32[64,256]{1,0:T(8,128)} %bond.1, f32[2,4,64,256]{3,2,1,0:T(8,128)} %sensor.1, f32[2,4,64,256]{3,2,1,0:T(8,128)} %peak.2), custom_call_target="tpu_custom_call" | custom-call | bytes 1024 | tf_op jit(solution)/shard_map/gather/pallas_call | solution.py:671
  3.2 0.3 collective-permute-start
  3.5 5.8 %collective-permute-start.1 = (f32[64,128]{1,0:T(8,128)S(1)}, f32[64,128]{1,0:T(8,128)S(1)}, u32[]{:S(2)}, u32[]{:S(2)}) collective-permute-start(f32[64,128]{1,0:T(8,128)S(1)} %get-tuple-element.23), channel_id=1, source_target_pairs={{1,2},{2,1},{3,4},{4,3},{5,6},{6,5},{7,8},{8,7},{9,10},{10,9},{11,... | collective-permute-start | bytes 98312 | tf_op jit(solution)/shard_map/ppermute | solution.py:719
  9.3 0.7 %deep_out.1 = f32[4,2,64,128]{3,2,1,0:T(8,128)} custom-call(f32[19,3,80,128]{3,2,1,0:T(8,128)S(1)} %get-tuple-element.21.own.start), custom_call_target="tpu_custom_call" | custom-call | flops 99999997952 | bytes 1024 | tf_op jit(solution)/shard_map/deep_out/pallas_call | solution.py:671
  10.0 3.1 %collective-permute-start.4 = (f32[4,2,64,128]{3,2,1,0:T(8,128)}, f32[4,2,64,128]{3,2,1,0:T(8,128)}, u32[]{:S(2)}, u32[]{:S(2)}) collective-permute-start(f32[4,2,64,128]{3,2,1,0:T(8,128)} %deep_out.1), channel_id=1, source_target_pairs={{0,240},{16,224},{32,208},{48,192},{64,176},{80,160},{96,144},{112... | collective-permute-start | bytes 786440 | tf_op jit(solution)/shard_map/ppermute | solution.py:723
  13.1 0.0 collective-permute-done.col_a
  13.1 0.0 collective-permute-done.1.col_b
  13.1 1.1 %rows.1 = (f32[264,128]{1,0:T(8,128)S(1)}, f32[264,128]{1,0:T(8,128)S(1)}) custom-call(s32[2]{0:T(128)S(1)} %pad_add_fusion.place, f32[19,3,80,128]{3,2,1,0:T(8,128)S(1)} %get-tuple-element.21.own.start, f32[64,128]{1,0:T(8,128)S(1)} %collective-permute-done.col_a, f32[64,128]{1,0:T(8,128)S(1)} %collective-permute-done.1.col_b, f32[4,2,64,128]{3,2,1,0:T(8,128)} %deep_out.1), custom_call_target="tpu_custom_call" | custom-call | flops 99999997952 | bytes 1024 | tf_op jit(solution)/shard_map/rows/pallas_call | solution.py:671
  14.2 4.2 %collective-permute-start.3 = (f32[264,128]{1,0:T(8,128)S(1)}, f32[264,128]{1,0:T(8,128)S(1)}, u32[]{:S(2)}, u32[]{:S(2)}) collective-permute-start(f32[264,128]{1,0:T(8,128)S(1)} %get-tuple-element.25), channel_id=1, source_target_pairs={{16,32},{32,16},{48,64},{64,48},{80,96},{96,80},{112,128},{128,112... | collective-permute-start | bytes 405512 | tf_op jit(solution)/shard_map/ppermute | solution.py:732
  18.4 0.1 collective-permute-start.2
  18.5 0.1 layers_out.1
  18.6 0.0 copy-start
  18.6 0.0 copy-start.1
  18.7 0.0 copy-start.2
  18.7 0.0 copy-start.3
  18.7 0.0 copy-start.4
  18.7 3.1 %collective-permute-start.5 = (f32[5,2,64,128]{3,2,1,0:T(8,128)S(1)}, f32[5,2,64,128]{3,2,1,0:T(8,128)S(1)}, u32[]{:S(2)}, u32[]{:S(2)}) collective-permute-start(f32[5,2,64,128]{3,2,1,0:T(8,128)S(1)} %get-tuple-element.27), channel_id=1, source_target_pairs={{0,240},{16,224},{32,208},{48,192},{64,176},{80,160},{96,144},{112... | collective-permute-start | bytes 983048 | tf_op jit(solution)/shard_map/ppermute | solution.py:733
  21.8 2.3 %collective-permute-done.3.row_b = f32[264,128]{1,0:T(8,128)S(1)} collective-permute-done((f32[264,128]{1,0:T(8,128)S(1)}, f32[264,128]{1,0:T(8,128)S(1)}, u32[]{:S(2)}, u32[]{:S(2)}) %collective-permute-start.3) | collective-permute-done | bytes 135200 | tf_op jit(solution)/shard_map/ppermute | solution.py:732
  24.1 0.0 collective-permute-done.2.row_a
  24.1 0.0 collective-permute-done.4.deep_in
  24.1 1.7 %build.1 = (f32[19,3,80,128]{3,2,1,0:T(8,128)S(1)}, f32[240,128]{1,0:T(8,128)S(1)}) custom-call(s32[2]{0:T(128)S(1)} %pad_add_fusion.place, f32[19,3,80,128]{3,2,1,0:T(8,128)S(1)} %get-tuple-element.21.own.start, f32[64,128]{1,0:T(8,128)S(1)} %collective-permute-done.col_a, ...), custom_call_target="tpu_custom_call", output_to_operand_aliasing={{0}: (1, {})} | custom-call | flops 99999997952 | bytes 1024 | tf_op jit(solution)/shard_map/build/pallas_call | solution.py:671
  25.9 2.4 %collective-permute-start.6 = (f32[240,128]{1,0:T(8,128)S(1)}, f32[240,128]{1,0:T(8,128)S(1)}, u32[]{:S(2)}, u32[]{:S(2)}) collective-permute-start(f32[240,128]{1,0:T(8,128)S(1)} %get-tuple-element.28), channel_id=1, source_target_pairs={{0,240},{16,224},{32,208},{48,192},{64,176},{80,160},{96,144},{112... | collective-permute-start | bytes 368648 | tf_op jit(solution)/shard_map/ppermute | solution.py:744
  28.3 3.1 %collective-permute-start.7 = (f32[6,2,64,128]{3,2,1,0:T(8,128)S(1)}, f32[6,2,64,128]{3,2,1,0:T(8,128)S(1)}, u32[]{:S(2)}, u32[]{:S(2)}) collective-permute-start(f32[6,2,64,128]{3,2,1,0:T(8,128)S(1)} %get-tuple-element.31), channel_id=1, source_target_pairs={{0,240},{16,224},{32,208},{48,192},{64,176},{80,160},{96,144},{112... | collective-permute-start | bytes 1179656 | tf_op jit(solution)/shard_map/ppermute | solution.py:745
  31.3 1.4 %collective-permute-done.5.sensor_in = f32[5,2,64,128]{3,2,1,0:T(8,128)S(1)} collective-permute-done((f32[5,2,64,128]{3,2,1,0:T(8,128)S(1)}, f32[5,2,64,128]{3,2,1,0:T(8,128)S(1)}, u32[]{:S(2)}, u32[]{:S(2)}) %collective-permute-start.5) | collective-permute-done | bytes 327712 | tf_op jit(solution)/shard_map/ppermute | solution.py:733
  32.7 2.8 %collective-permute-done.6.message = f32[240,128]{1,0:T(8,128)S(1)} collective-permute-done((f32[240,128]{1,0:T(8,128)S(1)}, f32[240,128]{1,0:T(8,128)S(1)}, u32[]{:S(2)}, u32[]{:S(2)}) %collective-permute-start.6) | collective-permute-done | bytes 122912 | tf_op jit(solution)/shard_map/ppermute | solution.py:744
  35.5 0.0 copy-done
  35.6 0.0 copy-done.1
  35.6 0.0 copy-done.2
  35.6 0.0 copy-done.3
  35.6 0.0 copy-done.4
  35.6 9.6 %thermal_sensor.1 = (f32[2,4,64,256]{3,2,1,0:T(8,128)}, f32[2,4,64,256]{3,2,1,0:T(8,128)}, f32[2,3,3,80,128]{4,3,2,1,0:T(8,128)S(1)}, f32[2,4,3,80,128]{4,3,2,1,...) custom-call(s32[2]{0:T(128)S(1)} %pad_add_fusion.place, ...), custom_call_target="tpu_custom_call" | custom-call | flops 99999997952 | bytes 1024 | tf_op jit(solution)/shard_map/thermal_sensor/pallas_call | solution.py:671
  45.2 0.0 collective-permute-done.7.peak_in
  45.2 3.7 %peak.3 = (f32[2,4,64,256]{3,2,1,0:T(8,128)}, f32[2,2,4,3,96,128]{5,4,3,2,1,0:T(8,128)S(1)}) custom-call(s32[2]{0:T(128)S(1)} %pad_add_fusion.place, s32[2,4]{1,0:T(2,128)S(1)} %copy-done, f32[4]{0:T(128)S(1)} %copy-done.1, f32[4]{0:T(128)S(1)} %copy-done.2, f32[2]{0:T(128)S(1)} %copy-done.3, ...), custom_call_target="tpu_custom_call", output_to_operand_aliasing={{1}: (11, {})} | custom-call | bytes 1024 | tf_op jit(solution)/shard_map/peak/pallas_call | solution.py:671
Async XLA Ops:
  3.2 9.8 %collective-permute-start = (f32[64,128]{1,0:T(8,128)S(1)}, f32[64,128]{1,0:T(8,128)S(1)}, u32[]{:S(2)}, u32[]{:S(2)}) collective-permute-start(f32[64,128]{1,0:T(8,128)S(1)} %get-tuple-element.22), channel_id=1, source_target_pairs={{0,1},{1,0},{2,3},{3,2},{4,5},{5,4},{6,7},{7,6},{8,9},{9,8},{10,11... | collective-permute-start | bytes 98312 | tf_op jit(solution)/shard_map/ppermute | solution.py:718
  3.5 9.6 %collective-permute-start.1 = (f32[64,128]{1,0:T(8,128)S(1)}, f32[64,128]{1,0:T(8,128)S(1)}, u32[]{:S(2)}, u32[]{:S(2)}) collective-permute-start(f32[64,128]{1,0:T(8,128)S(1)} %get-tuple-element.23), channel_id=1, source_target_pairs={{1,2},{2,1},{3,4},{4,3},{5,6},{6,5},{7,8},{8,7},{9,10},{10,9},{11,... | collective-permute-start | bytes 98312 | tf_op jit(solution)/shard_map/ppermute | solution.py:719
  10.0 14.1 %collective-permute-start.4 = (f32[4,2,64,128]{3,2,1,0:T(8,128)}, f32[4,2,64,128]{3,2,1,0:T(8,128)}, u32[]{:S(2)}, u32[]{:S(2)}) collective-permute-start(f32[4,2,64,128]{3,2,1,0:T(8,128)} %deep_out.1), channel_id=1, source_target_pairs={{0,240},{16,224},{32,208},{48,192},{64,176},{80,160},{96,144},{112... | collective-permute-start | bytes 786440 | tf_op jit(solution)/shard_map/ppermute | solution.py:723
  14.2 9.9 %collective-permute-start.3 = (f32[264,128]{1,0:T(8,128)S(1)}, f32[264,128]{1,0:T(8,128)S(1)}, u32[]{:S(2)}, u32[]{:S(2)}) collective-permute-start(f32[264,128]{1,0:T(8,128)S(1)} %get-tuple-element.25), channel_id=1, source_target_pairs={{16,32},{32,16},{48,64},{64,48},{80,96},{96,80},{112,128},{128,112... | collective-permute-start | bytes 405512 | tf_op jit(solution)/shard_map/ppermute | solution.py:732
  18.4 5.7 %collective-permute-start.2 = (f32[264,128]{1,0:T(8,128)S(1)}, f32[264,128]{1,0:T(8,128)S(1)}, u32[]{:S(2)}, u32[]{:S(2)}) collective-permute-start(f32[264,128]{1,0:T(8,128)S(1)} %get-tuple-element.24.row_a), channel_id=1, source_target_pairs={{0,16},{16,0},{32,48},{48,32},{64,80},{80,64},{96,112},{112,96},{1... | collective-permute-start | bytes 405512 | tf_op jit(solution)/shard_map/ppermute | solution.py:731
  18.6 16.9 %copy-start = (s32[2,4]{1,0:T(2,128)S(1)}, s32[2,4]{1,0:T(2,128)}, u32[]{:S(2)}) copy-start(s32[2,4]{1,0:T(2,128)} %layer_class.3) | copy-start | bytes 100
  18.6 16.9 %copy-start.1 = (f32[4]{0:T(128)S(1)}, f32[4]{0:T(128)}, u32[]{:S(2)}) copy-start(f32[4]{0:T(128)} %lateral.3) | copy-start | bytes 52
  18.7 16.9 %copy-start.2 = (f32[4]{0:T(128)S(1)}, f32[4]{0:T(128)}, u32[]{:S(2)}) copy-start(f32[4]{0:T(128)} %vertical.3) | copy-start | bytes 52
  18.7 16.9 %copy-start.3 = (f32[2]{0:T(128)S(1)}, f32[2]{0:T(128)}, u32[]{:S(2)}) copy-start(f32[2]{0:T(128)} %sink.3) | copy-start | bytes 28
  18.7 16.9 %copy-start.4 = (f32[4]{0:T(128)S(1)}, f32[4]{0:T(128)}, u32[]{:S(2)}) copy-start(f32[4]{0:T(128)} %share.1) | copy-start | bytes 52
  18.7 14.0 %collective-permute-start.5 = (f32[5,2,64,128]{3,2,1,0:T(8,128)S(1)}, f32[5,2,64,128]{3,2,1,0:T(8,128)S(1)}, u32[]{:S(2)}, u32[]{:S(2)}) collective-permute-start(f32[5,2,64,128]{3,2,1,0:T(8,128)S(1)} %get-tuple-element.27), channel_id=1, source_target_pairs={{0,240},{16,224},{32,208},{48,192},{64,176},{80,160},{96,144},{112... | collective-permute-start | bytes 983048 | tf_op jit(solution)/shard_map/ppermute | solution.py:733
  25.9 9.7 %collective-permute-start.6 = (f32[240,128]{1,0:T(8,128)S(1)}, f32[240,128]{1,0:T(8,128)S(1)}, u32[]{:S(2)}, u32[]{:S(2)}) collective-permute-start(f32[240,128]{1,0:T(8,128)S(1)} %get-tuple-element.28), channel_id=1, source_target_pairs={{0,240},{16,224},{32,208},{48,192},{64,176},{80,160},{96,144},{112... | collective-permute-start | bytes 368648 | tf_op jit(solution)/shard_map/ppermute | solution.py:744
  28.3 16.9 %collective-permute-start.7 = (f32[6,2,64,128]{3,2,1,0:T(8,128)S(1)}, f32[6,2,64,128]{3,2,1,0:T(8,128)S(1)}, u32[]{:S(2)}, u32[]{:S(2)}) collective-permute-start(f32[6,2,64,128]{3,2,1,0:T(8,128)S(1)} %get-tuple-element.31), channel_id=1, source_target_pairs={{0,240},{16,224},{32,208},{48,192},{64,176},{80,160},{96,144},{112... | collective-permute-start | bytes 1179656 | tf_op jit(solution)/shard_map/ppermute | solution.py:745
